TPU v7x, 128 devices: a whole 4x4x4 slice. The times are simulated.
128 devices in a mesh: tm: 16 (over y, z_hi, core), space: 8 (over x, z_lo).
Axes of the slice: x: 4, y: 4, z: 4 (z_hi: 2, z_lo: 2; z = z_hi * 2 + z_lo), core: 2. Of those that a mesh axis runs over, the one named last changes fastest.
Arguments:
- guess: float32 [64, 256, 4096], P('tm', 'space'), may hold values from -6 to 6
- forcing: float32 [64, 256, 4096], P('tm', 'space'), may hold values from -4 to 4
- initial: float32 [256, 4096], P('space'), may hold values from -6 to 6
- courant_rows: float32 [256, 4096], P('space'), may hold values from -0.12 to 0.12
- courant_cols: float32 [256, 4096], P('space'), may hold values from -0.12 to 0.12
- diffusion: float32 [256, 4096], P('space'), may hold values from 0.03 to 0.06
Outputs:
- states: float32 [64, 256, 4096], P('tm', 'space')
All inputs are finite; a program needn't handle non-finite values.
Results may differ from a plain program's by a relative error of at most 0.00002.
Values sent between devices are 32-bit elements; how exact they have to be, the bound alone decides.
No kernel may reach another device: no remote copies, remote signals or barrier semaphores. Data moves between devices by JAX's collectives and lax.ppermute only.
A program may use at most 64 MiB of HBM per device.

v0:
```python
import jax
import jax.numpy as jnp
from jax import lax
from jax.sharding import PartitionSpec as P


def padded(value, sides, width):
    for axis, dim in sides:
        count, length = (lax.axis_size(axis), value.shape[dim])
        up = [(i, (i + 1) % count) for i in range(count - 1)]
        down = [(j, i) for i, j in up]
        last = lax.slice_in_dim(value, length - width, length, axis=dim)
        leading = lax.slice_in_dim(value, 0, width, axis=dim)
        before = lax.ppermute(last, axis, up)
        after = lax.ppermute(leading, axis, down)
        value = jnp.concatenate([before, value, after], axis=dim)
    return value


def passed_along(value, axis, steps):
    count = lax.axis_size(axis)
    leading, last = (max(0, -steps), min(count, count - steps))
    return lax.ppermute(value, axis, [(source, source + steps) for source in range(leading, last)])


def local_step(extended, rate_rows, rate_cols, spread):
    field = extended[1:-1]
    upper = extended[:-2]
    lower = extended[2:]
    left = jnp.roll(field, 1, axis=1)
    right = jnp.roll(field, -1, axis=1)
    advect = jnp.maximum(rate_rows, 0.0) * (field - upper) + jnp.minimum(rate_rows, 0.0) * (
        lower - field
    )
    advect = (
        advect
        + jnp.maximum(rate_cols, 0.0) * (field - left)
        + jnp.minimum(rate_cols, 0.0) * (right - field)
    )
    laplace = upper + lower + left + right - 4.0 * field
    return field - advect + spread * laplace


def advance(field, rate_rows, rate_cols, spread):
    extended = padded(field, (("space", 0),), 1)
    return local_step(extended, rate_rows, rate_cols, spread)


def on_device(guess, forcing, initial, courant_rows, courant_cols, diffusion):
    steps_dev = guess.shape[0]
    owners = lax.axis_size("tm")
    is_first = lax.axis_index("tm") == 0
    previous = passed_along(guess[steps_dev - 1], "tm", 1)
    current = jnp.where(is_first, initial, previous)
    for inner in range(steps_dev):
        current = advance(current, courant_rows, courant_cols, diffusion) + forcing[inner]
    residual = current - guess[steps_dev - 1]
    twice_rows = 2.0 * courant_rows
    twice_cols = 2.0 * courant_cols
    twice_spread = 2.0 * diffusion

    def chain_turn(turn, correction):
        incoming = passed_along(correction, "tm", 1)
        for inner in range(steps_dev // 2):
            incoming = advance(incoming, twice_rows, twice_cols, twice_spread)
        return residual + incoming

    correction = lax.fori_loop(0, owners - 1, chain_turn, residual)
    corrected = guess[steps_dev - 1] + correction
    handed = passed_along(corrected, "tm", 1)
    current = jnp.where(is_first, initial, handed)
    outputs = []
    for inner in range(steps_dev - 1):
        current = advance(current, courant_rows, courant_cols, diffusion) + forcing[inner]
        outputs.append(current)
    outputs.append(corrected)
    return jnp.stack(outputs)


def solution(mesh):
    return jax.shard_map(
        on_device,
        mesh=mesh,
        in_specs=(
            P("tm", "space", None),
            P("tm", "space", None),
            P("space", None),
            P("space", None),
            P("space", None),
            P("space", None),
        ),
        out_specs=P("tm", "space", None),
        check_vma=False,
    )
```

profile of v0, /device:TPU:58, one launch (start us, length us, event | category | flops | bytes accessed | tf_op | source)
XLA Modules:
  0.0 596.7 jit_solution(14725180205031515515)
XLA Ops:
  3.2 11.1 %collective-permute-done.5 = f32[32,4096]{1,0:T(8,128)S(1)} collective-permute-done((f32[32,4096]{1,0:T(8,128)S(1)}, f32[32,4096]{1,0:T(8,128)S(1)}, u32[]{:S(2)}, u32[]{:S(2)}) %collective-permute-start.5) | collective-permute-done | bytes 524320 | tf_op jit(solution)/shard_map/ppermute | solution.py:23
  57.2 489.3 %while.10 = (s32[]{:T(128)}, f32[32,4096]{1,0:T(8,128)}, f32[32,4096]{1,0:T(8,128)S(1)}, f32[32,4096]{1,0:T(8,128)S(1)}, f32[32,4096]{1,0:T(8,128)S(1)}, /*index=5*/f32[32,4096]{1,0:T(8,128)S(1)}, s32[]{:T(128)}) while((s32[]{:T(128)}, f32[32,4096]{1,0:T(8,128)}, f32[32,4096]{1,0:T(8,128)S(1)}, f32[32,4096]{1,0:T(8,128)S(1)}, ...), condition=%wide.region_1.2_spmd, body=%wide.region_0.1_spmd.sunk | while | flops 7208962 | bytes 14614805 | solution.py:68
  59.1 11.3 %collective-permute-done = f32[32,4096]{1,0:T(8,128)S(1)} collective-permute-done((f32[32,4096]{1,0:T(8,128)}, f32[32,4096]{1,0:T(8,128)S(1)}, u32[]{:S(2)}, u32[]{:S(2)}) %collective-permute-start) | collective-permute-done | bytes 524320 | tf_op jit(solution)/shard_map/while/body/eval_jaxpr/ppermute | solution.py:23
  72.4 4.7 collective-permute-start.2
  79.4 4.5 collective-permute-start.3
  92.7 11.5 %collective-permute-done = f32[32,4096]{1,0:T(8,128)S(1)} collective-permute-done((f32[32,4096]{1,0:T(8,128)}, f32[32,4096]{1,0:T(8,128)S(1)}, u32[]{:S(2)}, u32[]{:S(2)}) %collective-permute-start) | collective-permute-done | bytes 524320 | tf_op jit(solution)/shard_map/while/body/eval_jaxpr/ppermute | solution.py:23
  125.2 11.4 %collective-permute-done = f32[32,4096]{1,0:T(8,128)S(1)} collective-permute-done((f32[32,4096]{1,0:T(8,128)}, f32[32,4096]{1,0:T(8,128)S(1)}, u32[]{:S(2)}, u32[]{:S(2)}) %collective-permute-start) | collective-permute-done | bytes 524320 | tf_op jit(solution)/shard_map/while/body/eval_jaxpr/ppermute | solution.py:23
  157.7 11.4 %collective-permute-done = f32[32,4096]{1,0:T(8,128)S(1)} collective-permute-done((f32[32,4096]{1,0:T(8,128)}, f32[32,4096]{1,0:T(8,128)S(1)}, u32[]{:S(2)}, u32[]{:S(2)}) %collective-permute-start) | collective-permute-done | bytes 524320 | tf_op jit(solution)/shard_map/while/body/eval_jaxpr/ppermute | solution.py:23
  190.1 11.4 %collective-permute-done = f32[32,4096]{1,0:T(8,128)S(1)} collective-permute-done((f32[32,4096]{1,0:T(8,128)}, f32[32,4096]{1,0:T(8,128)S(1)}, u32[]{:S(2)}, u32[]{:S(2)}) %collective-permute-start) | collective-permute-done | bytes 524320 | tf_op jit(solution)/shard_map/while/body/eval_jaxpr/ppermute | solution.py:23
  222.4 11.3 %collective-permute-done = f32[32,4096]{1,0:T(8,128)S(1)} collective-permute-done((f32[32,4096]{1,0:T(8,128)}, f32[32,4096]{1,0:T(8,128)S(1)}, u32[]{:S(2)}, u32[]{:S(2)}) %collective-permute-start) | collective-permute-done | bytes 524320 | tf_op jit(solution)/shard_map/while/body/eval_jaxpr/ppermute | solution.py:23
  254.6 11.3 %collective-permute-done = f32[32,4096]{1,0:T(8,128)S(1)} collective-permute-done((f32[32,4096]{1,0:T(8,128)}, f32[32,4096]{1,0:T(8,128)S(1)}, u32[]{:S(2)}, u32[]{:S(2)}) %collective-permute-start) | collective-permute-done | bytes 524320 | tf_op jit(solution)/shard_map/while/body/eval_jaxpr/ppermute | solution.py:23
  286.8 11.3 %collective-permute-done = f32[32,4096]{1,0:T(8,128)S(1)} collective-permute-done((f32[32,4096]{1,0:T(8,128)}, f32[32,4096]{1,0:T(8,128)S(1)}, u32[]{:S(2)}, u32[]{:S(2)}) %collective-permute-start) | collective-permute-done | bytes 524320 | tf_op jit(solution)/shard_map/while/body/eval_jaxpr/ppermute | solution.py:23
  319.4 11.6 %collective-permute-done = f32[32,4096]{1,0:T(8,128)S(1)} collective-permute-done((f32[32,4096]{1,0:T(8,128)}, f32[32,4096]{1,0:T(8,128)S(1)}, u32[]{:S(2)}, u32[]{:S(2)}) %collective-permute-start) | collective-permute-done | bytes 524320 | tf_op jit(solution)/shard_map/while/body/eval_jaxpr/ppermute | solution.py:23
  352.2 11.6 %collective-permute-done = f32[32,4096]{1,0:T(8,128)S(1)} collective-permute-done((f32[32,4096]{1,0:T(8,128)}, f32[32,4096]{1,0:T(8,128)S(1)}, u32[]{:S(2)}, u32[]{:S(2)}) %collective-permute-start) | collective-permute-done | bytes 524320 | tf_op jit(solution)/shard_map/while/body/eval_jaxpr/ppermute | solution.py:23
  366.6 4.1 collective-permute-start.2
  384.9 11.6 %collective-permute-done = f32[32,4096]{1,0:T(8,128)S(1)} collective-permute-done((f32[32,4096]{1,0:T(8,128)}, f32[32,4096]{1,0:T(8,128)S(1)}, u32[]{:S(2)}, u32[]{:S(2)}) %collective-permute-start) | collective-permute-done | bytes 524320 | tf_op jit(solution)/shard_map/while/body/eval_jaxpr/ppermute | solution.py:23
  399.3 4.1 collective-permute-start.2
  408.6 4.1 collective-permute-start.4
  417.7 11.6 %collective-permute-done = f32[32,4096]{1,0:T(8,128)S(1)} collective-permute-done((f32[32,4096]{1,0:T(8,128)}, f32[32,4096]{1,0:T(8,128)S(1)}, u32[]{:S(2)}, u32[]{:S(2)}) %collective-permute-start) | collective-permute-done | bytes 524320 | tf_op jit(solution)/shard_map/while/body/eval_jaxpr/ppermute | solution.py:23
  432.1 4.1 collective-permute-start.2
  441.3 4.1 collective-permute-start.4
  450.4 11.6 %collective-permute-done = f32[32,4096]{1,0:T(8,128)S(1)} collective-permute-done((f32[32,4096]{1,0:T(8,128)}, f32[32,4096]{1,0:T(8,128)S(1)}, u32[]{:S(2)}, u32[]{:S(2)}) %collective-permute-start) | collective-permute-done | bytes 524320 | tf_op jit(solution)/shard_map/while/body/eval_jaxpr/ppermute | solution.py:23
  474.0 4.1 collective-permute-start.4
  483.1 11.6 %collective-permute-done = f32[32,4096]{1,0:T(8,128)S(1)} collective-permute-done((f32[32,4096]{1,0:T(8,128)}, f32[32,4096]{1,0:T(8,128)S(1)}, u32[]{:S(2)}, u32[]{:S(2)}) %collective-permute-start) | collective-permute-done | bytes 524320 | tf_op jit(solution)/shard_map/while/body/eval_jaxpr/ppermute | solution.py:23
  506.8 4.1 collective-permute-start.4
  515.8 11.6 %collective-permute-done = f32[32,4096]{1,0:T(8,128)S(1)} collective-permute-done((f32[32,4096]{1,0:T(8,128)}, f32[32,4096]{1,0:T(8,128)S(1)}, u32[]{:S(2)}, u32[]{:S(2)}) %collective-permute-start) | collective-permute-done | bytes 524320 | tf_op jit(solution)/shard_map/while/body/eval_jaxpr/ppermute | solution.py:23
  530.3 4.1 collective-permute-start.2
  539.5 4.1 collective-permute-start.4
  550.0 11.3 %collective-permute-done.14 = f32[32,4096]{1,0:T(8,128)S(1)} collective-permute-done((f32[32,4096]{1,0:T(8,128)S(1)}, f32[32,4096]{1,0:T(8,128)S(1)}, u32[]{:S(2)}, u32[]{:S(2)}) %collective-permute-start.14) | collective-permute-done | bytes 524320 | tf_op jit(solution)/shard_map/ppermute | solution.py:23
  561.6 4.8 collective-permute-start.15
  568.5 4.5 collective-permute-done.16
  590.1 4.5 collective-permute-done.20
  (321 shorter events, 341.2 us)
Async XLA Ops:
  1.1 13.2 %collective-permute-start.5 = (f32[32,4096]{1,0:T(8,128)S(1)}, f32[32,4096]{1,0:T(8,128)S(1)}, u32[]{:S(2)}, u32[]{:S(2)}) collective-permute-start(f32[32,4096]{1,0:T(8,128)S(1)} %slice_bitcast_fusion), channel_id=1, source_target_pairs={{0,8},{8,16},{16,24},{24,32},{32,40},{40,48},{48,56},{56,64},{64,7... | collective-permute-start | bytes 1572872 | tf_op jit(solution)/shard_map/ppermute | solution.py:23
  57.2 13.2 %collective-permute-start = (f32[32,4096]{1,0:T(8,128)}, f32[32,4096]{1,0:T(8,128)S(1)}, u32[]{:S(2)}, u32[]{:S(2)}) collective-permute-start(f32[32,4096]{1,0:T(8,128)} %get-tuple-element.177), channel_id=1, source_target_pairs={{0,8},{8,16},{16,24},{24,32},{32,40},{40,48},{48,56},{56,64},{64,7... | collective-permute-start | bytes 1572872 | tf_op jit(solution)/shard_map/while/body/eval_jaxpr/ppermute | solution.py:23
  70.4 7.0 %collective-permute-start.1 = (f32[1,4096]{1,0:T(1,128)S(1)}, f32[1,4096]{1,0:T(1,128)S(1)}, u32[]{:S(2)}, u32[]{:S(2)}) collective-permute-start(f32[1,4096]{1,0:T(1,128)S(1)} %get-tuple-element.157), channel_id=1, source_target_pairs={{1,0},{2,1},{3,2},{4,3},{5,4},{6,5},{7,6},{9,8},{10,9},{11,10},{12... | collective-permute-start | bytes 49160 | tf_op jit(solution)/shard_map/while/body/eval_jaxpr/ppermute | solution.py:15
  79.4 7.1 %collective-permute-start.3 = (f32[1,4096]{1,0:T(1,128)S(1)}, f32[1,4096]{1,0:T(1,128)S(1)}, u32[]{:S(2)}, u32[]{:S(2)}) collective-permute-start(f32[1,4096]{1,0:T(1,128)S(1)} %get-tuple-element.163), channel_id=1, source_target_pairs={{1,0},{2,1},{3,2},{4,3},{5,4},{6,5},{7,6},{9,8},{10,9},{11,10},{12... | collective-permute-start | bytes 49160 | tf_op jit(solution)/shard_map/while/body/eval_jaxpr/ppermute | solution.py:15
  90.8 13.4 %collective-permute-start = (f32[32,4096]{1,0:T(8,128)}, f32[32,4096]{1,0:T(8,128)S(1)}, u32[]{:S(2)}, u32[]{:S(2)}) collective-permute-start(f32[32,4096]{1,0:T(8,128)} %get-tuple-element.177), channel_id=1, source_target_pairs={{0,8},{8,16},{16,24},{24,32},{32,40},{40,48},{48,56},{56,64},{64,7... | collective-permute-start | bytes 1572872 | tf_op jit(solution)/shard_map/while/body/eval_jaxpr/ppermute | solution.py:23
  104.2 7.0 %collective-permute-start.1 = (f32[1,4096]{1,0:T(1,128)S(1)}, f32[1,4096]{1,0:T(1,128)S(1)}, u32[]{:S(2)}, u32[]{:S(2)}) collective-permute-start(f32[1,4096]{1,0:T(1,128)S(1)} %get-tuple-element.157), channel_id=1, source_target_pairs={{1,0},{2,1},{3,2},{4,3},{5,4},{6,5},{7,6},{9,8},{10,9},{11,10},{12... | collective-permute-start | bytes 49160 | tf_op jit(solution)/shard_map/while/body/eval_jaxpr/ppermute | solution.py:15
  123.3 13.3 %collective-permute-start = (f32[32,4096]{1,0:T(8,128)}, f32[32,4096]{1,0:T(8,128)S(1)}, u32[]{:S(2)}, u32[]{:S(2)}) collective-permute-start(f32[32,4096]{1,0:T(8,128)} %get-tuple-element.177), channel_id=1, source_target_pairs={{0,8},{8,16},{16,24},{24,32},{32,40},{40,48},{48,56},{56,64},{64,7... | collective-permute-start | bytes 1572872 | tf_op jit(solution)/shard_map/while/body/eval_jaxpr/ppermute | solution.py:23
  136.6 7.2 %collective-permute-start.1 = (f32[1,4096]{1,0:T(1,128)S(1)}, f32[1,4096]{1,0:T(1,128)S(1)}, u32[]{:S(2)}, u32[]{:S(2)}) collective-permute-start(f32[1,4096]{1,0:T(1,128)S(1)} %get-tuple-element.157), channel_id=1, source_target_pairs={{1,0},{2,1},{3,2},{4,3},{5,4},{6,5},{7,6},{9,8},{10,9},{11,10},{12... | collective-permute-start | bytes 49160 | tf_op jit(solution)/shard_map/while/body/eval_jaxpr/ppermute | solution.py:15
  155.7 13.3 %collective-permute-start = (f32[32,4096]{1,0:T(8,128)}, f32[32,4096]{1,0:T(8,128)S(1)}, u32[]{:S(2)}, u32[]{:S(2)}) collective-permute-start(f32[32,4096]{1,0:T(8,128)} %get-tuple-element.177), channel_id=1, source_target_pairs={{0,8},{8,16},{16,24},{24,32},{32,40},{40,48},{48,56},{56,64},{64,7... | collective-permute-start | bytes 1572872 | tf_op jit(solution)/shard_map/while/body/eval_jaxpr/ppermute | solution.py:23
  169.0 7.2 %collective-permute-start.1 = (f32[1,4096]{1,0:T(1,128)S(1)}, f32[1,4096]{1,0:T(1,128)S(1)}, u32[]{:S(2)}, u32[]{:S(2)}) collective-permute-start(f32[1,4096]{1,0:T(1,128)S(1)} %get-tuple-element.157), channel_id=1, source_target_pairs={{1,0},{2,1},{3,2},{4,3},{5,4},{6,5},{7,6},{9,8},{10,9},{11,10},{12... | collective-permute-start | bytes 49160 | tf_op jit(solution)/shard_map/while/body/eval_jaxpr/ppermute | solution.py:15
  188.2 13.3 %collective-permute-start = (f32[32,4096]{1,0:T(8,128)}, f32[32,4096]{1,0:T(8,128)S(1)}, u32[]{:S(2)}, u32[]{:S(2)}) collective-permute-start(f32[32,4096]{1,0:T(8,128)} %get-tuple-element.177), channel_id=1, source_target_pairs={{0,8},{8,16},{16,24},{24,32},{32,40},{40,48},{48,56},{56,64},{64,7... | collective-permute-start | bytes 1572872 | tf_op jit(solution)/shard_map/while/body/eval_jaxpr/ppermute | solution.py:23
  201.5 7.1 %collective-permute-start.1 = (f32[1,4096]{1,0:T(1,128)S(1)}, f32[1,4096]{1,0:T(1,128)S(1)}, u32[]{:S(2)}, u32[]{:S(2)}) collective-permute-start(f32[1,4096]{1,0:T(1,128)S(1)} %get-tuple-element.157), channel_id=1, source_target_pairs={{1,0},{2,1},{3,2},{4,3},{5,4},{6,5},{7,6},{9,8},{10,9},{11,10},{12... | collective-permute-start | bytes 49160 | tf_op jit(solution)/shard_map/while/body/eval_jaxpr/ppermute | solution.py:15
  220.5 13.2 %collective-permute-start = (f32[32,4096]{1,0:T(8,128)}, f32[32,4096]{1,0:T(8,128)S(1)}, u32[]{:S(2)}, u32[]{:S(2)}) collective-permute-start(f32[32,4096]{1,0:T(8,128)} %get-tuple-element.177), channel_id=1, source_target_pairs={{0,8},{8,16},{16,24},{24,32},{32,40},{40,48},{48,56},{56,64},{64,7... | collective-permute-start | bytes 1572872 | tf_op jit(solution)/shard_map/while/body/eval_jaxpr/ppermute | solution.py:23
  233.7 7.1 %collective-permute-start.1 = (f32[1,4096]{1,0:T(1,128)S(1)}, f32[1,4096]{1,0:T(1,128)S(1)}, u32[]{:S(2)}, u32[]{:S(2)}) collective-permute-start(f32[1,4096]{1,0:T(1,128)S(1)} %get-tuple-element.157), channel_id=1, source_target_pairs={{1,0},{2,1},{3,2},{4,3},{5,4},{6,5},{7,6},{9,8},{10,9},{11,10},{12... | collective-permute-start | bytes 49160 | tf_op jit(solution)/shard_map/while/body/eval_jaxpr/ppermute | solution.py:15
  252.7 13.2 %collective-permute-start = (f32[32,4096]{1,0:T(8,128)}, f32[32,4096]{1,0:T(8,128)S(1)}, u32[]{:S(2)}, u32[]{:S(2)}) collective-permute-start(f32[32,4096]{1,0:T(8,128)} %get-tuple-element.177), channel_id=1, source_target_pairs={{0,8},{8,16},{16,24},{24,32},{32,40},{40,48},{48,56},{56,64},{64,7... | collective-permute-start | bytes 1572872 | tf_op jit(solution)/shard_map/while/body/eval_jaxpr/ppermute | solution.py:23
  284.9 13.2 %collective-permute-start = (f32[32,4096]{1,0:T(8,128)}, f32[32,4096]{1,0:T(8,128)S(1)}, u32[]{:S(2)}, u32[]{:S(2)}) collective-permute-start(f32[32,4096]{1,0:T(8,128)} %get-tuple-element.177), channel_id=1, source_target_pairs={{0,8},{8,16},{16,24},{24,32},{32,40},{40,48},{48,56},{56,64},{64,7... | collective-permute-start | bytes 1572872 | tf_op jit(solution)/shard_map/while/body/eval_jaxpr/ppermute | solution.py:23
  298.1 7.4 %collective-permute-start.1 = (f32[1,4096]{1,0:T(1,128)S(1)}, f32[1,4096]{1,0:T(1,128)S(1)}, u32[]{:S(2)}, u32[]{:S(2)}) collective-permute-start(f32[1,4096]{1,0:T(1,128)S(1)} %get-tuple-element.157), channel_id=1, source_target_pairs={{1,0},{2,1},{3,2},{4,3},{5,4},{6,5},{7,6},{9,8},{10,9},{11,10},{12... | collective-permute-start | bytes 49160 | tf_op jit(solution)/shard_map/while/body/eval_jaxpr/ppermute | solution.py:15
  317.5 13.6 %collective-permute-start = (f32[32,4096]{1,0:T(8,128)}, f32[32,4096]{1,0:T(8,128)S(1)}, u32[]{:S(2)}, u32[]{:S(2)}) collective-permute-start(f32[32,4096]{1,0:T(8,128)} %get-tuple-element.177), channel_id=1, source_target_pairs={{0,8},{8,16},{16,24},{24,32},{32,40},{40,48},{48,56},{56,64},{64,7... | collective-permute-start | bytes 1572872 | tf_op jit(solution)/shard_map/while/body/eval_jaxpr/ppermute | solution.py:23
  331.0 7.2 %collective-permute-start.1 = (f32[1,4096]{1,0:T(1,128)S(1)}, f32[1,4096]{1,0:T(1,128)S(1)}, u32[]{:S(2)}, u32[]{:S(2)}) collective-permute-start(f32[1,4096]{1,0:T(1,128)S(1)} %get-tuple-element.157), channel_id=1, source_target_pairs={{1,0},{2,1},{3,2},{4,3},{5,4},{6,5},{7,6},{9,8},{10,9},{11,10},{12... | collective-permute-start | bytes 49160 | tf_op jit(solution)/shard_map/while/body/eval_jaxpr/ppermute | solution.py:15
  350.3 13.6 %collective-permute-start = (f32[32,4096]{1,0:T(8,128)}, f32[32,4096]{1,0:T(8,128)S(1)}, u32[]{:S(2)}, u32[]{:S(2)}) collective-permute-start(f32[32,4096]{1,0:T(8,128)} %get-tuple-element.177), channel_id=1, source_target_pairs={{0,8},{8,16},{16,24},{24,32},{32,40},{40,48},{48,56},{56,64},{64,7... | collective-permute-start | bytes 1572872 | tf_op jit(solution)/shard_map/while/body/eval_jaxpr/ppermute | solution.py:23
  363.9 7.1 %collective-permute-start.1 = (f32[1,4096]{1,0:T(1,128)S(1)}, f32[1,4096]{1,0:T(1,128)S(1)}, u32[]{:S(2)}, u32[]{:S(2)}) collective-permute-start(f32[1,4096]{1,0:T(1,128)S(1)} %get-tuple-element.157), channel_id=1, source_target_pairs={{1,0},{2,1},{3,2},{4,3},{5,4},{6,5},{7,6},{9,8},{10,9},{11,10},{12... | collective-permute-start | bytes 49160 | tf_op jit(solution)/shard_map/while/body/eval_jaxpr/ppermute | solution.py:15
  383.0 13.6 %collective-permute-start = (f32[32,4096]{1,0:T(8,128)}, f32[32,4096]{1,0:T(8,128)S(1)}, u32[]{:S(2)}, u32[]{:S(2)}) collective-permute-start(f32[32,4096]{1,0:T(8,128)} %get-tuple-element.177), channel_id=1, source_target_pairs={{0,8},{8,16},{16,24},{24,32},{32,40},{40,48},{48,56},{56,64},{64,7... | collective-permute-start | bytes 1572872 | tf_op jit(solution)/shard_map/while/body/eval_jaxpr/ppermute | solution.py:23
  396.6 7.1 %collective-permute-start.1 = (f32[1,4096]{1,0:T(1,128)S(1)}, f32[1,4096]{1,0:T(1,128)S(1)}, u32[]{:S(2)}, u32[]{:S(2)}) collective-permute-start(f32[1,4096]{1,0:T(1,128)S(1)} %get-tuple-element.157), channel_id=1, source_target_pairs={{1,0},{2,1},{3,2},{4,3},{5,4},{6,5},{7,6},{9,8},{10,9},{11,10},{12... | collective-permute-start | bytes 49160 | tf_op jit(solution)/shard_map/while/body/eval_jaxpr/ppermute | solution.py:15
  415.7 13.6 %collective-permute-start = (f32[32,4096]{1,0:T(8,128)}, f32[32,4096]{1,0:T(8,128)S(1)}, u32[]{:S(2)}, u32[]{:S(2)}) collective-permute-start(f32[32,4096]{1,0:T(8,128)} %get-tuple-element.177), channel_id=1, source_target_pairs={{0,8},{8,16},{16,24},{24,32},{32,40},{40,48},{48,56},{56,64},{64,7... | collective-permute-start | bytes 1572872 | tf_op jit(solution)/shard_map/while/body/eval_jaxpr/ppermute | solution.py:23
  429.3 7.1 %collective-permute-start.1 = (f32[1,4096]{1,0:T(1,128)S(1)}, f32[1,4096]{1,0:T(1,128)S(1)}, u32[]{:S(2)}, u32[]{:S(2)}) collective-permute-start(f32[1,4096]{1,0:T(1,128)S(1)} %get-tuple-element.157), channel_id=1, source_target_pairs={{1,0},{2,1},{3,2},{4,3},{5,4},{6,5},{7,6},{9,8},{10,9},{11,10},{12... | collective-permute-start | bytes 49160 | tf_op jit(solution)/shard_map/while/body/eval_jaxpr/ppermute | solution.py:15
  448.5 13.6 %collective-permute-start = (f32[32,4096]{1,0:T(8,128)}, f32[32,4096]{1,0:T(8,128)S(1)}, u32[]{:S(2)}, u32[]{:S(2)}) collective-permute-start(f32[32,4096]{1,0:T(8,128)} %get-tuple-element.177), channel_id=1, source_target_pairs={{0,8},{8,16},{16,24},{24,32},{32,40},{40,48},{48,56},{56,64},{64,7... | collective-permute-start | bytes 1572872 | tf_op jit(solution)/shard_map/while/body/eval_jaxpr/ppermute | solution.py:23
  462.0 7.1 %collective-permute-start.1 = (f32[1,4096]{1,0:T(1,128)S(1)}, f32[1,4096]{1,0:T(1,128)S(1)}, u32[]{:S(2)}, u32[]{:S(2)}) collective-permute-start(f32[1,4096]{1,0:T(1,128)S(1)} %get-tuple-element.157), channel_id=1, source_target_pairs={{1,0},{2,1},{3,2},{4,3},{5,4},{6,5},{7,6},{9,8},{10,9},{11,10},{12... | collective-permute-start | bytes 49160 | tf_op jit(solution)/shard_map/while/body/eval_jaxpr/ppermute | solution.py:15
  481.2 13.6 %collective-permute-start = (f32[32,4096]{1,0:T(8,128)}, f32[32,4096]{1,0:T(8,128)S(1)}, u32[]{:S(2)}, u32[]{:S(2)}) collective-permute-start(f32[32,4096]{1,0:T(8,128)} %get-tuple-element.177), channel_id=1, source_target_pairs={{0,8},{8,16},{16,24},{24,32},{32,40},{40,48},{48,56},{56,64},{64,7... | collective-permute-start | bytes 1572872 | tf_op jit(solution)/shard_map/while/body/eval_jaxpr/ppermute | solution.py:23
  494.8 7.1 %collective-permute-start.1 = (f32[1,4096]{1,0:T(1,128)S(1)}, f32[1,4096]{1,0:T(1,128)S(1)}, u32[]{:S(2)}, u32[]{:S(2)}) collective-permute-start(f32[1,4096]{1,0:T(1,128)S(1)} %get-tuple-element.157), channel_id=1, source_target_pairs={{1,0},{2,1},{3,2},{4,3},{5,4},{6,5},{7,6},{9,8},{10,9},{11,10},{12... | collective-permute-start | bytes 49160 | tf_op jit(solution)/shard_map/while/body/eval_jaxpr/ppermute | solution.py:15
  513.9 13.6 %collective-permute-start = (f32[32,4096]{1,0:T(8,128)}, f32[32,4096]{1,0:T(8,128)S(1)}, u32[]{:S(2)}, u32[]{:S(2)}) collective-permute-start(f32[32,4096]{1,0:T(8,128)} %get-tuple-element.177), channel_id=1, source_target_pairs={{0,8},{8,16},{16,24},{24,32},{32,40},{40,48},{48,56},{56,64},{64,7... | collective-permute-start | bytes 1572872 | tf_op jit(solution)/shard_map/while/body/eval_jaxpr/ppermute | solution.py:23
  527.5 7.1 %collective-permute-start.1 = (f32[1,4096]{1,0:T(1,128)S(1)}, f32[1,4096]{1,0:T(1,128)S(1)}, u32[]{:S(2)}, u32[]{:S(2)}) collective-permute-start(f32[1,4096]{1,0:T(1,128)S(1)} %get-tuple-element.157), channel_id=1, source_target_pairs={{1,0},{2,1},{3,2},{4,3},{5,4},{6,5},{7,6},{9,8},{10,9},{11,10},{12... | collective-permute-start | bytes 49160 | tf_op jit(solution)/shard_map/while/body/eval_jaxpr/ppermute | solution.py:15
  547.8 13.5 %collective-permute-start.14 = (f32[32,4096]{1,0:T(8,128)S(1)}, f32[32,4096]{1,0:T(8,128)S(1)}, u32[]{:S(2)}, u32[]{:S(2)}) collective-permute-start(f32[32,4096]{1,0:T(8,128)S(1)} %fusion.136), channel_id=1, source_target_pairs={{0,8},{8,16},{16,24},{24,32},{32,40},{40,48},{48,56},{56,64},{64,7... | collective-permute-start | bytes 1572872 | tf_op jit(solution)/shard_map/ppermute | solution.py:23
  (67 other events, 538.4 us)
where the time goes:
time: 599 us; the launch traced here: 597 us
  starting transfers between devices  280 us (47%)
  waiting for transfers between devices  266 us (44%)
  other arithmetic  36.3 us (6%)
  local copies, waits for them, and re-layouts  13 us (2%)
    ppermute x17, waiting for transfers between devices, passed_along(): lax.ppermute(value, axis, [(source, source + steps) for source in range(l...  195 us
    ppermute x37, starting transfers between devices, padded(): before = lax.ppermute(last, axis, up)  144 us
    ppermute x37, starting transfers between devices, padded(): after = lax.ppermute(leading, axis, down)  104 us
    ppermute x37, waiting for transfers between devices, padded(): before = lax.ppermute(last, axis, up)  44.6 us
    ppermute x17, starting transfers between devices, passed_along(): lax.ppermute(value, axis, [(source, source + steps) for source in range(l...  32.9 us
    ppermute x37, waiting for transfers between devices, padded(): after = lax.ppermute(leading, axis, down)  26.7 us
    add x15, other arithmetic, chain_turn(): return residual + incoming  20.3 us
  transfers between devices with their start and end apart: 91, of which 54 were waited for; matrix products, arithmetic and copies ran while one was open for 1% of the time, Pallas kernels for 0%

commit v1 on v0

v1 whole, which is shorter than its diff:
```python
import jax
import jax.numpy as jnp
from jax import lax
from jax.experimental import pallas as pl
from jax.experimental.pallas import tpu as pltpu
from jax.sharding import Mesh, PartitionSpec as P

ROWS = 32
LANES = 128
HALO = 32
VMEM = pl.BlockSpec(memory_space=pltpu.VMEM)
SMEM = pl.BlockSpec(memory_space=pltpu.SMEM)
F32 = jnp.float32
RIM = ((0, 3), (3, 3), (6, 3), (9, 3), (12, 2), (14, 1))


def params(mib):
    return pltpu.CompilerParams(vmem_limit_bytes=mib * 1024 * 1024)


def iota(dim):
    return lax.broadcasted_iota(jnp.int32, (8, LANES), dim)


def cols(j):
    return slice(LANES * j, LANES * (j + 1))


def tile(r, first=0):
    return slice(first + 8 * r, first + 8 * r + 8)


def rates(a, b, d):
    a_pos, a_neg = jnp.maximum(a, 0.0), jnp.minimum(a, 0.0)
    b_pos, b_neg = jnp.maximum(b, 0.0), jnp.minimum(b, 0.0)
    own = 1.0 - (a_pos - a_neg) - (b_pos - b_neg) - 4.0 * d
    return own, d + a_pos, d - a_neg, d + b_pos, d - b_neg


def put(ref, j, r, value):
    ref[j, tile(r, 8), :] = value
    if r == 4:
        ref[j, 0:8, :] = value


def sweep(ref, coef, rows, use):
    tiles = ref.shape[0]
    lane = iota(1)
    for r in rows:
        at = 8 + 8 * r
        mids, rights, lefts = {}, {}, {}

        def load(j):
            j %= tiles
            if j not in mids:
                mids[j] = ref[j, at : at + 8, :]
                rights[j] = pltpu.roll(mids[j], 1, 1)
                lefts[j] = pltpu.roll(mids[j], LANES - 1, 1)

        for j in range(tiles):
            for i in (j - 1, j, j + 1):
                load(i)
            mid = mids[j]
            up = ref[j, at - 1 : at + 7, :]
            low = ref[j, at + 1 : at + 9, :] if r < 4 else ref[j, 1:9, :]
            left = jnp.where(lane == 0, rights[(j - 1) % tiles], rights[j])
            right = jnp.where(lane == LANES - 1, lefts[(j + 1) % tiles], lefts[j])
            total = coef[0, j, tile(r), :] * mid + coef[1, j, tile(r), :] * up
            total += coef[2, j, tile(r), :] * low + coef[3, j, tile(r), :] * left
            use(j, r, total + coef[4, j, tile(r), :] * right, mid)


def rim_kernel(flag, guess, initial, a, b, d, forcing, last, start_low, start_up, low, up):
    tiles = a.shape[1] // LANES
    at_end = flag[2] == 1
    last[...] = guess[0]
    rows = last.shape[0]
    start_low[...] = jnp.where(at_end, initial[0:4, :], guess[0, 0:4, :])
    start_up[...] = jnp.where(at_end, initial[rows - 4 : rows, :], guess[0, rows - 4 : rows, :])
    sources = [lambda at, j, x=x: x[at, cols(j)] for x in (a, b, d)]
    sources += [lambda at, j, i=i: forcing[i, at, cols(j)] for i in range(3)]
    for j in range(tiles):
        for source, (to, count) in zip(sources, RIM, strict=True):
            low[j, to : to + count, :] = source(slice(0, count), j)
            up[j, to : to + count, :] = source(slice(rows - count, rows), j)
        low[j, 15:16, :] = jnp.zeros((1, LANES), F32)
        up[j, 15:16, :] = jnp.zeros((1, LANES), F32)


def rim_tile(low, up, j, item, sub):
    at, count = RIM[item]
    under = low[j, at : at + 8, :] if at <= 8 else pltpu.roll(low[j, 8:16, :], 16 - at, 0)
    begin = at + count - 8
    over = up[j, begin : begin + 8, :] if begin >= 0 else pltpu.roll(up[j, 0:8, :], -begin, 0)
    return jnp.where(sub < 4, under, over)


def residual_kernel(flag, before, initial, start_low, start_up, low, up, guess, forcing, a, b, d,
                    messages, ends, coef, rims, one, two, three, res):
    tiles = a.shape[1] // LANES
    lane, sub = iota(1), iota(0)
    first = flag[0] == 1
    turn = flag[3]
    for j in range(tiles):
        for r in range(5):
            if r < 4:
                values = a[tile(r), cols(j)], b[tile(r), cols(j)], d[tile(r), cols(j)]
                put(one, j, r, jnp.where(first, initial[tile(r), cols(j)], before[tile(r), cols(j)]))
            else:
                values = [rim_tile(low, up, j, item, sub) for item in range(3)]
                for at in (0, 40):
                    one[j, at : at + 4, :] = start_low[:, cols(j)]
                    one[j, at + 4 : at + 8, :] = start_up[:, cols(j)]
            for i, value in enumerate(rates(*values)):
                coef[i, j, tile(r), :] = value
        for inner in range(3):
            rims[inner, j, :, :] = rim_tile(low, up, j, 3 + inner, sub)

    for inner, (source, target) in enumerate([(one, two), (two, three), (three, two)]):

        def fine(j, r, value, _, inner=inner, target=target):
            put(target, j, r, value + (forcing[inner, tile(r), cols(j)] if r < 4 else rims[inner, j, :, :]))

        sweep(source, coef, range(5), fine)

    def last(j, r, value, _):
        value = value + forcing[3, tile(r), cols(j)]
        ends[j, tile(r), :] = value
        res[j, tile(r), :] = value - guess[tile(r), cols(j)]

    sweep(two, coef, range(4), last)

    for r in range(4):
        for j in range(tiles):
            x, y, z = (res[i % tiles, tile(r), :] for i in (j - 1, j, j + 1))
            messages[2 * j, tile(r), :] = pltpu.roll(jnp.where(lane >= LANES - HALO, x, y), HALO, 1)
            messages[2 * j + 1, tile(r), :] = pltpu.roll(jnp.where(lane < HALO, z, y), LANES - HALO, 1)

    which, row = lax.div(turn, 4), pl.ds(pl.multiple_of(8 * lax.rem(turn, 4), 8), 8)
    for j in range(tiles):
        x, y, z = (
            jnp.where(which == 0, a[row, cols(i % tiles)], jnp.where(which == 1, b[row, cols(i % tiles)], d[row, cols(i % tiles)]))
            for i in (j - 1, j, j + 1)
        )
        messages[2 * j, tile(4), :] = pltpu.roll(jnp.where(lane >= LANES - HALO, x, y), HALO, 1)
        messages[2 * j + 1, tile(4), :] = pltpu.roll(jnp.where(lane < HALO, z, y), LANES - HALO, 1)


def chain_kernel(flag, mine, other, messages, coef, one, two):
    pairs = spaces = 8
    rows = spaces * ROWS
    blocks = rows // 8
    lane, sub = iota(1), iota(0)
    even = flag[1] == 0
    zero = jnp.zeros((8, LANES), F32)

    def arrived(pair, odd, s, r):
        same, across = mine[pair * spaces + s, tile(r), :], other[pair * spaces + s, tile(r), :]
        return jnp.where(even, across, same) if odd else jnp.where(even, same, across)

    for s in range(spaces):
        for r in range(4):
            a, b, d = (arrived((4 * i + r) // 2, r % 2 == 1, s, 4) for i in range(3))
            own, up, low, left, right = rates(a, b, d)
            at = tile(r, s * ROWS)
            coef[0, at, :] = 2.0 * own - 1.0
            for i, value in enumerate((up, low, left, right)):
                coef[i + 1, at, :] = 2.0 * value
    for ref in (one, two):
        ref[0:8, :] = zero
        ref[rows + 8 : rows + 16, :] = zero
    for t in range(blocks):
        one[tile(t, 8), :] = zero

    def step(source, t):
        at = 8 * t + 8
        mid = source[at : at + 8, :]
        total = coef[0, tile(t), :] * mid + coef[1, tile(t), :] * source[at - 1 : at + 7, :]
        total += coef[2, tile(t), :] * source[at + 1 : at + 9, :]
        total += coef[3, tile(t), :] * pltpu.roll(mid, 1, 1)
        return total + coef[4, tile(t), :] * pltpu.roll(mid, LANES - 1, 1)

    def emit(pair):
        for s in range(spaces):
            at = 8 + ROWS * s
            tiles = [one[tile(r, at), :] for r in range(4)]
            rim = jnp.where(sub < 4, one[at + ROWS : at + ROWS + 8, :], one[at - 8 : at, :])
            low = [pltpu.roll(x, LANES - HALO, 1) for x in tiles[:3]]
            high = [pltpu.roll(x, HALO, 1) for x in (tiles[3], rim)]
            where = pair * spaces + s
            messages[where, 0:8, :] = jnp.where(lane < 64, low[0], high[0])
            messages[where, 8:16, :] = jnp.where(lane < 64, low[1], high[1])
            messages[where, 16:24, :] = low[2]

    def advance(pair, odd):
        for t in range(blocks):
            two[tile(t, 8), :] = step(one, t)
        for t in range(blocks):
            one[tile(t, 8), :] = step(two, t) + arrived(pair, odd, t // 4, t % 4)

    def turn(pair, _):
        pl.when(even)(lambda: emit(pair))
        advance(pair, False)
        pl.when(jnp.logical_not(even))(lambda: emit(pair))
        pl.when(pair < pairs - 1)(lambda: advance(pair, True))
        return 0

    lax.fori_loop(0, pairs, turn, 0)


def final_kernel(start, coef, rims, forcing, ends, returned, states, one, two, err, half):
    tiles = start.shape[0]
    lane = iota(1)
    for j in range(tiles):
        for r in range(5):
            x, y = returned[2 * j, tile(r % 3), :], returned[2 * j + 1, tile(r % 3), :]
            if r < 3:
                error = jnp.where(lane < 64, x, pltpu.roll(y, 64, 1))
            else:
                error = jnp.where(lane < 64, pltpu.roll(x, 64, 1), y)
            put(err, j, r, error)
            put(one, j, r, start[j, tile(r, 8), :] + error)

    def coarse(j, r, value, own):
        put(half, j, r, 2.0 * value - own)

    def corrected(j, r, value, own):
        states[3, tile(r), cols(j)] = ends[j, tile(r), :] + (2.0 * value - own)

    def fine(inner, target):
        def use(j, r, value, _):
            value = value + (forcing[inner, tile(r), cols(j)] if r < 4 else rims[inner, j, :, :])
            if r < 4:
                states[inner, tile(r), cols(j)] = value
            if target is not None:
                put(target, j, r, value)

        return use

    sweep(one, coef, range(5), fine(0, two))
    sweep(err, coef, range(5), coarse)
    sweep(two, coef, range(5), fine(1, one))
    sweep(half, coef, range(4), corrected)
    sweep(one, coef, range(4), fine(2, None))


def on_device(guess, forcing, initial, courant_rows, courant_cols, diffusion):
    chips, cores, spaces = (lax.axis_size(n) for n in ("chip", "core", "space"))
    owners = chips * cores
    columns = initial.shape[1]
    tiles = columns // LANES
    everything = ("chip", "core", "space")
    chip, core = lax.axis_index("chip"), lax.axis_index("core")
    turn = chip * cores + core
    flag = jnp.stack([turn == 0, core, turn == owners - 1, turn]).astype(jnp.int32)

    def shaped(*shape):
        return jax.ShapeDtypeStruct(shape, F32)

    def whole(*shape):
        return pl.BlockSpec(shape, lambda i: (0,) * len(shape))

    block = whole(ROWS, columns)
    last, start_low, start_up, low, up = pl.pallas_call(
        rim_kernel,
        grid=(1,),
        in_specs=[SMEM, pl.BlockSpec((1, ROWS, columns), lambda i: (3, 0, 0)), block, block, block, block,
                  whole(3, ROWS, columns)],
        out_specs=[block, whole(4, columns), whole(4, columns), whole(tiles, 16, LANES), whole(tiles, 16, LANES)],
        out_shape=[shaped(ROWS, columns), shaped(4, columns), shaped(4, columns), shaped(tiles, 16, LANES),
                   shaped(tiles, 16, LANES)],
        compiler_params=params(20),
        name="rim",
    )(flag, guess, initial, courant_rows, courant_cols, diffusion, forcing)

    before = lax.ppermute(last, ("chip", "core"), [(i, i + 1) for i in range(owners - 1)])

    def shifted(value, by_turn, by_space):
        pairs = []
        for k in range(owners):
            for s in range(spaces):
                if 0 <= s + by_space < spaces:
                    pairs.append((k * spaces + s, (k + by_turn) % owners * spaces + s + by_space))
        return lax.ppermute(value, everything, pairs)

    start_up, start_low = shifted(start_up, 1, 1), shifted(start_low, 1, -1)
    up, low = shifted(up, 0, 1), shifted(low, 0, -1)

    field = pltpu.VMEM((tiles, 48, LANES), F32)
    messages, ends, coef, rims, start = pl.pallas_call(
        residual_kernel,
        in_specs=[SMEM] + [VMEM] * 11,
        out_specs=[VMEM] * 5,
        out_shape=[shaped(2 * tiles, 40, LANES), shaped(tiles, ROWS, LANES), shaped(5, tiles, 40, LANES),
                   shaped(3, tiles, 8, LANES), shaped(tiles, 48, LANES)],
        scratch_shapes=[field, field, pltpu.VMEM((tiles, ROWS, LANES), F32)],
        compiler_params=params(20),
        name="residual",
    )(flag, before, initial, start_low, start_up, low, up, last, forcing, courant_rows, courant_cols, diffusion)

    mine = lax.all_to_all(messages, ("chip", "space"), 0, 0, tiled=True)
    other = lax.ppermute(mine, "core", [(0, 1), (1, 0)])
    rows = spaces * ROWS
    answer = pl.pallas_call(
        chain_kernel,
        in_specs=[SMEM, VMEM, VMEM],
        out_specs=VMEM,
        out_shape=shaped(chips * spaces, 24, LANES),
        scratch_shapes=[
            pltpu.VMEM((5, rows, LANES), F32),
            pltpu.VMEM((rows + 16, LANES), F32),
            pltpu.VMEM((rows + 16, LANES), F32),
        ],
        compiler_params=params(20),
        name="chain",
    )(flag, mine, other)
    returned = lax.all_to_all(answer, ("chip", "space"), 0, 0, tiled=True)
    return pl.pallas_call(
        final_kernel,
        in_specs=[VMEM] * 6,
        out_specs=VMEM,
        out_shape=shaped(4, ROWS, columns),
        scratch_shapes=[field, field, field, field],
        compiler_params=params(20),
        name="final",
    )(start, coef, rims, forcing, ends, returned)


def solution(mesh):
    cores = 2
    devices = mesh.devices
    grid = Mesh(
        devices.reshape(devices.shape[0] // cores, cores, devices.shape[1]), ("chip", "core", "space")
    )
    time_rows = P(("chip", "core"), "space", None)
    rows = P("space", None)
    return jax.shard_map(
        on_device,
        mesh=grid,
        in_specs=(time_rows, time_rows, rows, rows, rows, rows),
        out_specs=time_rows,
        check_vma=False,
    )
```

time: 599 us -> 102 us (0.17)
  the two profiles are of different devices: /device:TPU:58 before, /device:TPU:0 now
where the time goes in v1:
time: 102 us; the launch traced here: 101 us
  blocking collectives  56.6 us (55%)
  starting transfers between devices  16.6 us (16%)
  Pallas kernels  12.8 us (13%)
  waiting for transfers between devices  7.54 us (7%)
  local copies, waits for them, and re-layouts  7.35 us (7%)
    all_to_all x1, blocking collectives, on_device(): mine = lax.all_to_all(messages, ('chip', 'space'), 0, 0, tiled=True)  35.9 us
    all_to_all x1, blocking collectives, on_device(): returned = lax.all_to_all(answer, ('chip', 'space'), 0, 0, tiled=True)  20.8 us
    ppermute x4, starting transfers between devices, shifted(): return lax.ppermute(value, everything, pairs)  15.3 us
    unnamed x14, local copies, waits for them, and re-layouts  7.35 us
    pallas_call x1, Pallas kernels, on_device(): pl.pallas_call(chain_kernel, in_specs=[SMEM, VMEM, VMEM], out_specs=VMEM,...  5.03 us
    ppermute x4, waiting for transfers between devices, shifted(): return lax.ppermute(value, everything, pairs)  4.51 us
    pallas_call x1, Pallas kernels, on_device(): pl.pallas_call(final_kernel, in_specs=[VMEM] * 6, out_specs=VMEM, out_sha...  3.83 us
    pallas_call x1, Pallas kernels, on_device(): pl.pallas_call(residual_kernel, in_specs=[SMEM] + [VMEM] * 11, out_specs=...  3.17 us
  transfers between devices with their start and end apart: 6, of which 3 were waited for; matrix products, arithmetic and copies ran while one was open for 0% of the time, Pallas kernels for 0%

profile of v1, /device:TPU:0, one launch (start us, length us, event | category | flops | bytes accessed | tf_op | source)
XLA Modules:
  0.0 101.1 jit_solution(2801263561082258404)
XLA Ops:
  0.0 0.1 pad_add_fusion.flag
  0.1 0.0 copy-start
  0.1 1.6 %copy-done = f32[4,32,4096]{2,1,0:T(8,128)S(1)} copy-done((f32[4,32,4096]{2,1,0:T(8,128)S(1)}, f32[4,32,4096]{2,1,0:T(8,128)}, u32[]{:S(2)}) %copy-start) | copy-done | bytes 2097176
  1.7 0.0 copy-start.2
  1.7 1.6 %copy-done.2 = f32[4,32,4096]{2,1,0:T(8,128)S(1)} copy-done((f32[4,32,4096]{2,1,0:T(8,128)S(1)}, f32[4,32,4096]{2,1,0:T(8,128)}, u32[]{:S(2)}) %copy-start.2) | copy-done | bytes 2097176
  3.3 0.0 copy-start.3
  3.3 1.0 %copy-done.3 = f32[32,4096]{1,0:T(8,128)S(1)} copy-done((f32[32,4096]{1,0:T(8,128)S(1)}, f32[32,4096]{1,0:T(8,128)}, u32[]{:S(2)}) %copy-start.3) | copy-done | bytes 524312
  4.3 0.0 copy-start.4
  4.3 1.0 %copy-done.4 = f32[32,4096]{1,0:T(8,128)S(1)} copy-done((f32[32,4096]{1,0:T(8,128)S(1)}, f32[32,4096]{1,0:T(8,128)}, u32[]{:S(2)}) %copy-start.4) | copy-done | bytes 524312
  5.3 0.0 copy-start.5
  5.3 1.0 %copy-done.5 = f32[32,4096]{1,0:T(8,128)S(1)} copy-done((f32[32,4096]{1,0:T(8,128)S(1)}, f32[32,4096]{1,0:T(8,128)}, u32[]{:S(2)}) %copy-start.5) | copy-done | bytes 524312
  6.4 0.0 copy-start.6
  6.4 1.0 %copy-done.6 = f32[32,4096]{1,0:T(8,128)S(1)} copy-done((f32[32,4096]{1,0:T(8,128)S(1)}, f32[32,4096]{1,0:T(8,128)}, u32[]{:S(2)}) %copy-start.6) | copy-done | bytes 524312
  7.4 0.7 rim.1
  8.2 1.3 %collective-permute-start = (f32[32,4096]{1,0:T(8,128)S(1)}, f32[32,4096]{1,0:T(8,128)S(1)}, u32[]{:S(2)}, u32[]{:S(2)}) collective-permute-start(f32[32,4096]{1,0:T(8,128)S(1)} %get-tuple-element.15.guess), channel_id=1, source_target_pairs={{0,8},{8,16},{16,24},{24,32},{32,40},{40,48},{48,56},{56,64},{64,7... | collective-permute-start | bytes 1572872 | tf_op jit(solution)/shard_map/ppermute | solution.py:276
  9.5 1.3 %collective-permute-start.3 = (f32[32,16,128]{2,1,0:T(8,128)S(1)}, f32[32,16,128]{2,1,0:T(8,128)S(1)}, u32[]{:S(2)}, u32[]{:S(2)}) collective-permute-start(f32[32,16,128]{2,1,0:T(8,128)S(1)} %get-tuple-element.18), channel_id=1, source_target_pairs={{1,0},{2,1},{3,2},{4,3},{5,4},{6,5},{7,6},{9,8},{10,9},{11,10},{12... | collective-permute-start | bytes 786440 | tf_op jit(solution)/shard_map/ppermute | solution.py:284
  10.8 5.0 %collective-permute-start.4 = (f32[32,16,128]{2,1,0:T(8,128)S(1)}, f32[32,16,128]{2,1,0:T(8,128)S(1)}, u32[]{:S(2)}, u32[]{:S(2)}) collective-permute-start(f32[32,16,128]{2,1,0:T(8,128)S(1)} %get-tuple-element.19), channel_id=1, source_target_pairs={{0,1},{1,2},{2,3},{3,4},{4,5},{5,6},{6,7},{8,9},{9,10},{10,11},{11... | collective-permute-start | bytes 786440 | tf_op jit(solution)/shard_map/ppermute | solution.py:284
  15.8 1.3 %collective-permute-start.1 = (f32[4,4096]{1,0:T(4,128)S(1)}, f32[4,4096]{1,0:T(4,128)S(1)}, u32[]{:S(2)}, u32[]{:S(2)}) collective-permute-start(f32[4,4096]{1,0:T(4,128)S(1)} %get-tuple-element.16), channel_id=1, source_target_pairs={{1,8},{2,9},{3,10},{4,11},{5,12},{6,13},{7,14},{9,16},{10,17},{11,... | collective-permute-start | bytes 196616 | tf_op jit(solution)/shard_map/ppermute | solution.py:284
  17.1 7.7 %collective-permute-start.2 = (f32[4,4096]{1,0:T(4,128)S(1)}, f32[4,4096]{1,0:T(4,128)S(1)}, u32[]{:S(2)}, u32[]{:S(2)}) collective-permute-start(f32[4,4096]{1,0:T(4,128)S(1)} %get-tuple-element.17), channel_id=1, source_target_pairs={{0,9},{1,10},{2,11},{3,12},{4,13},{5,14},{6,15},{8,17},{9,18},{10,... | collective-permute-start | bytes 196616 | tf_op jit(solution)/shard_map/ppermute | solution.py:284
  24.8 0.7 collective-permute-done.1.start_low
  25.5 3.8 %collective-permute-done.2.start_up = f32[4,4096]{1,0:T(4,128)S(1)} collective-permute-done((f32[4,4096]{1,0:T(4,128)S(1)}, f32[4,4096]{1,0:T(4,128)S(1)}, u32[]{:S(2)}, u32[]{:S(2)}) %collective-permute-start.2) | collective-permute-done | bytes 65568 | tf_op jit(solution)/shard_map/ppermute | solution.py:284
  29.3 0.0 collective-permute-done.3.low
  29.3 0.0 collective-permute-done.4.up
  29.3 0.0 collective-permute-done.before
  29.4 0.0 copy-done.1
  29.4 3.2 %residual.1 = (f32[64,40,128]{2,1,0:T(8,128)S(1)}, f32[32,32,128]{2,1,0:T(8,128)S(1)}, f32[5,32,40,128]{3,2,1,0:T(8,128)S(1)}, f32[3,32,8,128]{3,2,1,0:T(8,128)S(1)}, f32[32,48,128]{2,1,0:T(8,128)S(1)}) custom-call(s32[4]{0:T(128)S(1)} %pad_add_fusion.flag, f32[32,4096]{1,0:T(8,128)S(1)} %collective-permute-done.before, f32[32,4096]{1,0:T(8,128)S(1)} %copy-done.3, ...), custom_call_target="tpu_custom_call" | custom-call | tf_op jit(solution)/shard_map/residual/pallas_call | solution.py:290
  32.5 35.9 %all_to_all.10.mine = f32[64,40,128]{2,1,0:T(8,128)S(1)} all-to-all(f32[64,40,128]{2,1,0:T(8,128)S(1)} %get-tuple-element.24), channel_id=1, replica_groups=mesh['chip'=8,'core'=2,'space'=8] {'chip','space'}, dimensions={0} | all-to-all | bytes 2621440 | tf_op jit(solution)/shard_map/all_to_all | solution.py:301
  68.4 0.0 collective-permute-start.5
  68.4 3.0 %collective-permute-done.5.other = f32[64,40,128]{2,1,0:T(8,128)S(1)} collective-permute-done((f32[64,40,128]{2,1,0:T(8,128)S(1)}, f32[64,40,128]{2,1,0:T(8,128)S(1)}, u32[]{:S(2)}, u32[]{:S(2)}) %collective-permute-start.5) | collective-permute-done | bytes 1310752 | tf_op jit(solution)/shard_map/ppermute | solution.py:302
  71.5 5.0 %chain.1 = f32[64,24,128]{2,1,0:T(8,128)S(1)} custom-call(s32[4]{0:T(128)S(1)} %pad_add_fusion.flag, f32[64,40,128]{2,1,0:T(8,128)S(1)} %all_to_all.10.mine, f32[64,40,128]{2,1,0:T(8,128)S(1)} %collective-permute-done.5.other), custom_call_target="tpu_custom_call" | custom-call | tf_op jit(solution)/shard_map/chain/pallas_call | solution.py:304
  76.5 20.8 %all_to_all.11.returned = f32[64,24,128]{2,1,0:T(8,128)S(1)} all-to-all(f32[64,24,128]{2,1,0:T(8,128)S(1)} %chain.1), channel_id=1, replica_groups=mesh['chip'=8,'core'=2,'space'=8] {'chip','space'}, dimensions={0} | all-to-all | bytes 1572864 | tf_op jit(solution)/shard_map/all_to_all | solution.py:317
  97.3 3.8 %final.1 = f32[4,32,4096]{2,1,0:T(8,128)} custom-call(f32[32,48,128]{2,1,0:T(8,128)S(1)} %get-tuple-element.20.start, f32[5,32,40,128]{3,2,1,0:T(8,128)S(1)} %get-tuple-element.21.coef, f32[3,32,8,128]{3,2,1,0:T(8,128)S(1)} %get-tuple-element.22.rims, f32[4,32,4096]{2,1,0:T(8,128)S(1)} %copy-done.1, f32[32,32,128]{2,1,0:T(8,128)S(1)} %get-tuple-element.23.ends, ...), custom_call_target="tpu_custom_call" | custom-call | tf_op jit(solution)/shard_map/final/pallas_call | solution.py:318
  (1 shorter events, 0.0 us)
Async XLA Ops:
  0.1 1.6 %copy-start = (f32[4,32,4096]{2,1,0:T(8,128)S(1)}, f32[4,32,4096]{2,1,0:T(8,128)}, u32[]{:S(2)}) copy-start(f32[4,32,4096]{2,1,0:T(8,128)} %forcing.5) | copy-start | bytes 6291460
  1.7 1.6 %copy-start.2 = (f32[4,32,4096]{2,1,0:T(8,128)S(1)}, f32[4,32,4096]{2,1,0:T(8,128)}, u32[]{:S(2)}) copy-start(f32[4,32,4096]{2,1,0:T(8,128)} %guess.1) | copy-start | bytes 6291460
  3.3 1.0 %copy-start.3 = (f32[32,4096]{1,0:T(8,128)S(1)}, f32[32,4096]{1,0:T(8,128)}, u32[]{:S(2)}) copy-start(f32[32,4096]{1,0:T(8,128)} %initial.3) | copy-start | bytes 1572868
  4.3 1.0 %copy-start.4 = (f32[32,4096]{1,0:T(8,128)S(1)}, f32[32,4096]{1,0:T(8,128)}, u32[]{:S(2)}) copy-start(f32[32,4096]{1,0:T(8,128)} %a.3) | copy-start | bytes 1572868
  5.3 1.0 %copy-start.5 = (f32[32,4096]{1,0:T(8,128)S(1)}, f32[32,4096]{1,0:T(8,128)}, u32[]{:S(2)}) copy-start(f32[32,4096]{1,0:T(8,128)} %b.3) | copy-start | bytes 1572868
  6.4 1.0 %copy-start.6 = (f32[32,4096]{1,0:T(8,128)S(1)}, f32[32,4096]{1,0:T(8,128)}, u32[]{:S(2)}) copy-start(f32[32,4096]{1,0:T(8,128)} %d.3) | copy-start | bytes 1572868
  7.4 21.9 %copy-start.1 = (f32[4,32,4096]{2,1,0:T(8,128)S(1)}, f32[4,32,4096]{2,1,0:T(8,128)}, u32[]{:S(2)}) copy-start(f32[4,32,4096]{2,1,0:T(8,128)} %forcing.5) | copy-start | bytes 6291460
  8.2 21.2 %collective-permute-start = (f32[32,4096]{1,0:T(8,128)S(1)}, f32[32,4096]{1,0:T(8,128)S(1)}, u32[]{:S(2)}, u32[]{:S(2)}) collective-permute-start(f32[32,4096]{1,0:T(8,128)S(1)} %get-tuple-element.15.guess), channel_id=1, source_target_pairs={{0,8},{8,16},{16,24},{24,32},{32,40},{40,48},{48,56},{56,64},{64,7... | collective-permute-start | bytes 1572872 | tf_op jit(solution)/shard_map/ppermute | solution.py:276
  9.5 19.8 %collective-permute-start.3 = (f32[32,16,128]{2,1,0:T(8,128)S(1)}, f32[32,16,128]{2,1,0:T(8,128)S(1)}, u32[]{:S(2)}, u32[]{:S(2)}) collective-permute-start(f32[32,16,128]{2,1,0:T(8,128)S(1)} %get-tuple-element.18), channel_id=1, source_target_pairs={{1,0},{2,1},{3,2},{4,3},{5,4},{6,5},{7,6},{9,8},{10,9},{11,10},{12... | collective-permute-start | bytes 786440 | tf_op jit(solution)/shard_map/ppermute | solution.py:284
  10.8 18.5 %collective-permute-start.4 = (f32[32,16,128]{2,1,0:T(8,128)S(1)}, f32[32,16,128]{2,1,0:T(8,128)S(1)}, u32[]{:S(2)}, u32[]{:S(2)}) collective-permute-start(f32[32,16,128]{2,1,0:T(8,128)S(1)} %get-tuple-element.19), channel_id=1, source_target_pairs={{0,1},{1,2},{2,3},{3,4},{4,5},{5,6},{6,7},{8,9},{9,10},{10,11},{11... | collective-permute-start | bytes 786440 | tf_op jit(solution)/shard_map/ppermute | solution.py:284
  15.8 9.7 %collective-permute-start.1 = (f32[4,4096]{1,0:T(4,128)S(1)}, f32[4,4096]{1,0:T(4,128)S(1)}, u32[]{:S(2)}, u32[]{:S(2)}) collective-permute-start(f32[4,4096]{1,0:T(4,128)S(1)} %get-tuple-element.16), channel_id=1, source_target_pairs={{1,8},{2,9},{3,10},{4,11},{5,12},{6,13},{7,14},{9,16},{10,17},{11,... | collective-permute-start | bytes 196616 | tf_op jit(solution)/shard_map/ppermute | solution.py:284
  17.1 12.2 %collective-permute-start.2 = (f32[4,4096]{1,0:T(4,128)S(1)}, f32[4,4096]{1,0:T(4,128)S(1)}, u32[]{:S(2)}, u32[]{:S(2)}) collective-permute-start(f32[4,4096]{1,0:T(4,128)S(1)} %get-tuple-element.17), channel_id=1, source_target_pairs={{0,9},{1,10},{2,11},{3,12},{4,13},{5,14},{6,15},{8,17},{9,18},{10,... | collective-permute-start | bytes 196616 | tf_op jit(solution)/shard_map/ppermute | solution.py:284
  68.4 3.0 %collective-permute-start.5 = (f32[64,40,128]{2,1,0:T(8,128)S(1)}, f32[64,40,128]{2,1,0:T(8,128)S(1)}, u32[]{:S(2)}, u32[]{:S(2)}) collective-permute-start(f32[64,40,128]{2,1,0:T(8,128)S(1)} %all_to_all.10.mine), channel_id=1, source_target_pairs={{0,8},{8,0},{1,9},{9,1},{2,10},{10,2},{3,11},{11,3},{4,12},{12,4},... | collective-permute-start | bytes 3932168 | tf_op jit(solution)/shard_map/ppermute | solution.py:302

commit v2 on v1

--- a/solution.py
+++ b/solution.py
@@ -11,7 +11,9 @@
 VMEM = pl.BlockSpec(memory_space=pltpu.VMEM)
 SMEM = pl.BlockSpec(memory_space=pltpu.SMEM)
 F32 = jnp.float32
-RIM = ((0, 3), (3, 3), (6, 3), (9, 3), (12, 2), (14, 1))
+ANY = pl.BlockSpec(memory_space=pl.ANY)
+G1, G2, G3, PART, A1, B1, D1, INWARD = range(8)
+START1, START2, STEP1, STEP2 = range(4)
 
 
 def params(mib):
@@ -70,56 +72,134 @@
             use(j, r, total + coef[4, j, tile(r), :] * right, mid)
 
 
-def rim_kernel(flag, guess, initial, a, b, d, forcing, last, start_low, start_up, low, up):
-    tiles = a.shape[1] // LANES
-    at_end = flag[2] == 1
-    last[...] = guess[0]
-    rows = last.shape[0]
-    start_low[...] = jnp.where(at_end, initial[0:4, :], guess[0, 0:4, :])
-    start_up[...] = jnp.where(at_end, initial[rows - 4 : rows, :], guess[0, rows - 4 : rows, :])
-    sources = [lambda at, j, x=x: x[at, cols(j)] for x in (a, b, d)]
-    sources += [lambda at, j, i=i: forcing[i, at, cols(j)] for i in range(3)]
+def last_kernel(guess, last, sem):
+    copy = pltpu.make_async_copy(guess.at[3], last, sem)
+    copy.start()
+    copy.wait()
+
+
+def rim_kernel(flag, guess, initial, a, b, d, forcing, rim_one, rim_two, start_one, start_two,
+               va, vi, vg, vc, coef, field, after, sems):
+    rows, columns = a.shape
+    tiles = columns // LANES
+    sub, lane = iota(0), iota(1)
+    copies = []
+    for side in range(2):
+        at = pl.ds(0 if side == 0 else rows - 8, 8)
+        moves = [(x.at[at, :], vc.at[i, side]) for i, x in enumerate((a, b, d))]
+        moves += [(forcing.at[i, at, :], vg.at[i, side]) for i in range(3)]
+        moves += [(guess.at[3, at, :], va.at[side]), (initial.at[at, :], vi.at[side])]
+        for source, target in moves:
+            copies.append(pltpu.make_async_copy(source, target, sems.at[len(copies)]))
+    for copy in copies:
+        copy.start()
+    for copy in copies:
+        copy.wait()
+    at_end, even = flag[2] == 1, flag[4] == 0
+
+    def outward(x, side):
+        return pltpu.roll(x, 7 if side == 0 else 1, 0)
+
+    def inward(x, side):
+        return pltpu.roll(x, 1 if side == 0 else 7, 0)
+
+    def row(x, side, place, to):
+        at = place - 1 if side == 0 else 8 - place
+        return pltpu.roll(x, (to - at) % 8, 0)
+
+    def open_step(values, j, side):
+        x, y, z = (values[i % tiles] for i in (j - 1, j, j + 1))
+        left = pltpu.roll(jnp.where(lane == LANES - 1, x, y), 1, 1)
+        right = pltpu.roll(jnp.where(lane == 0, z, y), LANES - 1, 1)
+        out = coef[side, 2 - side, j]
+        return coef[side, 0, j] * y + out * outward(y, side) + coef[side, 3, j] * left + coef[side, 4, j] * right
+
+    class Tiles:
+        def __init__(self, get):
+            self.get, self.seen = get, {}
+
+        def __getitem__(self, j):
+            if j not in self.seen:
+                self.seen[j] = self.get(j)
+            return self.seen[j]
+
+    for side in range(2):
+        for j in range(tiles):
+            for i, value in enumerate(rates(*(vc[n, side, :, cols(j)] for n in range(3)))):
+                coef[side, i, j] = value
+            field[side, j] = jnp.where(at_end, vi[side, :, cols(j)], va[side, :, cols(j)])
+    for side in range(2):
+        values = Tiles(lambda j, side=side: field[side, j])
+        for j in range(tiles):
+            part = open_step(values, j, side)
+            after[side, 0, j] = part
+            after[side, 1, j] = part + coef[side, 1 + side, j] * inward(values[j], side)
     for j in range(tiles):
-        for source, (to, count) in zip(sources, RIM, strict=True):
-            low[j, to : to + count, :] = source(slice(0, count), j)
-            up[j, to : to + count, :] = source(slice(rows - count, rows), j)
-        low[j, 15:16, :] = jnp.zeros((1, LANES), F32)
-        up[j, 15:16, :] = jnp.zeros((1, LANES), F32)
-
-
-def rim_tile(low, up, j, item, sub):
-    at, count = RIM[item]
-    under = low[j, at : at + 8, :] if at <= 8 else pltpu.roll(low[j, 8:16, :], 16 - at, 0)
-    begin = at + count - 8
-    over = up[j, begin : begin + 8, :] if begin >= 0 else pltpu.roll(up[j, 0:8, :], -begin, 0)
-    return jnp.where(sub < 4, under, over)
-
-
-def residual_kernel(flag, before, initial, start_low, start_up, low, up, guess, forcing, a, b, d,
-                    messages, ends, coef, rims, one, two, three, res):
+        rims, starts = [], []
+        for side in range(2):
+            forced = Tiles(lambda j, side=side: vg[0, side, :, cols(j)])
+            stepped = Tiles(lambda j, side=side: after[side, 1, j])
+            g1, g2, g3 = (vg[i, side, :, cols(j)] for i in range(3))
+            second = g2 + coef[side, 2 - side, j] * outward(g1, side)
+            part = open_step(forced, j, side) + g2
+            items = [(G1, g1, 1), (G2, second, 1), (G3, g3, 1), (PART, part, 2)]
+            items += [(A1 + i, vc[i, side, :, cols(j)], 1) for i in range(3)]
+            items += [(INWARD, coef[side, 1 + side, j], 2)]
+            total = row(g1, side, 1, 0)
+            for to, value, place in items[1:]:
+                total = jnp.where(sub == to, row(value, side, place, to), total)
+            rims.append(total)
+            values = field[side, j]
+            total = row(values, side, 1, START1)
+            for to, value in ((START2, values), (STEP1, after[side, 0, j]), (STEP2, open_step(stepped, j, side))):
+                total = jnp.where(sub == to, row(value, side, 2, to), total)
+            starts.append(total[0:4])
+        rim_one[j] = jnp.where(even, rims[1], rims[0])
+        rim_two[j] = jnp.where(even, rims[0], rims[1])
+        start_one[j] = jnp.where(even, starts[1], starts[0])
+        start_two[j] = jnp.where(even, starts[0], starts[1])
+
+
+def residual_kernel(flag, before, initial, start_one, start_two, rim_one, rim_two, guess, forcing, a, b, d,
+                    messages, ends, coef, rims, one, two, three, res, edge):
     tiles = a.shape[1] // LANES
     lane, sub = iota(1), iota(0)
-    first = flag[0] == 1
+    first, even = flag[0] == 1, flag[4] == 0
     turn = flag[3]
+    zero = jnp.zeros((8, LANES), F32)
     for j in range(tiles):
-        for r in range(5):
-            if r < 4:
-                values = a[tile(r), cols(j)], b[tile(r), cols(j)], d[tile(r), cols(j)]
-                put(one, j, r, jnp.where(first, initial[tile(r), cols(j)], before[tile(r), cols(j)]))
-            else:
-                values = [rim_tile(low, up, j, item, sub) for item in range(3)]
-                for at in (0, 40):
-                    one[j, at : at + 4, :] = start_low[:, cols(j)]
-                    one[j, at + 4 : at + 8, :] = start_up[:, cols(j)]
+        edge[0, j, 0:4, :] = jnp.where(even, start_one[j], start_two[j])
+        edge[1, j, 0:4, :] = jnp.where(even, start_two[j], start_one[j])
+    for j in range(tiles):
+        low, up = jnp.where(even, rim_one[j], rim_two[j]), jnp.where(even, rim_two[j], rim_one[j])
+        start_low, start_up = edge[0, j], edge[1, j]
+
+        def border(under, over, item, place=1, rest=zero):
+            under = pltpu.roll(under, (place - 1 - item) % 8, 0)
+            over = pltpu.roll(over, (8 - place - item) % 8, 0)
+            return jnp.where(sub == place - 1, under, jnp.where(sub == 8 - place, over, rest))
+
+        for r in range(4):
+            values = a[tile(r), cols(j)], b[tile(r), cols(j)], d[tile(r), cols(j)]
+            put(one, j, r, jnp.where(first, initial[tile(r), cols(j)], before[tile(r), cols(j)]))
             for i, value in enumerate(rates(*values)):
                 coef[i, j, tile(r), :] = value
-        for inner in range(3):
-            rims[inner, j, :, :] = rim_tile(low, up, j, 3 + inner, sub)
+        start = border(start_low, start_up, START1)
+        put(one, j, 4, border(start_low, start_up, START2, 2, start))
+        own, upper, lower, left, right = rates(*(border(low, up, item) for item in (A1, B1, D1)))
+        own = jnp.where((sub == 0) | (sub == 7), own, 0.0)
+        upper = jnp.where(sub == 1, pltpu.roll(low, (1 - INWARD) % 8, 0), upper)
+        lower = jnp.where(sub == 6, pltpu.roll(up, (6 - INWARD) % 8, 0), lower)
+        for i, value in enumerate((own, upper, lower, left, right)):
+            coef[i, j, tile(4), :] = value
+        rims[0, j] = border(start_low, start_up, STEP1, 2, border(low, up, G1))
+        rims[1, j] = border(low, up, G2) + border(start_low, start_up, STEP2, 2) + border(low, up, PART, 2)
+        rims[2, j] = border(low, up, G3)
 
     for inner, (source, target) in enumerate([(one, two), (two, three), (three, two)]):
 
         def fine(j, r, value, _, inner=inner, target=target):
-            put(target, j, r, value + (forcing[inner, tile(r), cols(j)] if r < 4 else rims[inner, j, :, :]))
+            put(target, j, r, value + (forcing[inner, tile(r), cols(j)] if r < 4 else rims[inner, j]))
 
         sweep(source, coef, range(5), fine)
 
@@ -136,10 +216,10 @@
             messages[2 * j, tile(r), :] = pltpu.roll(jnp.where(lane >= LANES - HALO, x, y), HALO, 1)
             messages[2 * j + 1, tile(r), :] = pltpu.roll(jnp.where(lane < HALO, z, y), LANES - HALO, 1)
 
-    which, row = lax.div(turn, 4), pl.ds(pl.multiple_of(8 * lax.rem(turn, 4), 8), 8)
+    which, at = lax.div(turn, 4), pl.ds(pl.multiple_of(8 * lax.rem(turn, 4), 8), 8)
     for j in range(tiles):
         x, y, z = (
-            jnp.where(which == 0, a[row, cols(i % tiles)], jnp.where(which == 1, b[row, cols(i % tiles)], d[row, cols(i % tiles)]))
+            jnp.where(which == 0, a[at, cols(i % tiles)], jnp.where(which == 1, b[at, cols(i % tiles)], d[at, cols(i % tiles)]))
             for i in (j - 1, j, j + 1)
         )
         messages[2 * j, tile(4), :] = pltpu.roll(jnp.where(lane >= LANES - HALO, x, y), HALO, 1)
@@ -184,7 +264,11 @@
         for s in range(spaces):
             at = 8 + ROWS * s
             tiles = [one[tile(r, at), :] for r in range(4)]
-            rim = jnp.where(sub < 4, one[at + ROWS : at + ROWS + 8, :], one[at - 8 : at, :])
+            under, over = slice(at + ROWS, at + ROWS + 8), slice(at - 8, at)
+            low_step = pltpu.roll(0.5 * (two[under, :] + one[under, :]), 1, 0)
+            up_step = pltpu.roll(0.5 * (two[over, :] + one[over, :]), 7, 0)
+            rim = jnp.where(sub < 2, one[under, :], one[over, :])
+            rim = jnp.where(sub == 2, low_step, jnp.where(sub == 5, up_step, rim))
             low = [pltpu.roll(x, LANES - HALO, 1) for x in tiles[:3]]
             high = [pltpu.roll(x, HALO, 1) for x in (tiles[3], rim)]
             where = pair * spaces + s
@@ -192,25 +276,29 @@
             messages[where, 8:16, :] = jnp.where(lane < 64, low[1], high[1])
             messages[where, 16:24, :] = low[2]
 
-    def advance(pair, odd):
+    def half():
         for t in range(blocks):
             two[tile(t, 8), :] = step(one, t)
+
+    def rest(pair, odd):
         for t in range(blocks):
             one[tile(t, 8), :] = step(two, t) + arrived(pair, odd, t // 4, t % 4)
 
     def turn(pair, _):
+        half()
         pl.when(even)(lambda: emit(pair))
-        advance(pair, False)
+        rest(pair, False)
+        half()
         pl.when(jnp.logical_not(even))(lambda: emit(pair))
-        pl.when(pair < pairs - 1)(lambda: advance(pair, True))
+        pl.when(pair < pairs - 1)(lambda: rest(pair, True))
         return 0
 
     lax.fori_loop(0, pairs, turn, 0)
 
 
-def final_kernel(start, coef, rims, forcing, ends, returned, states, one, two, err, half):
+def final_kernel(start, coef, rims, forcing, ends, returned, states, one, two, err, half, extra):
     tiles = start.shape[0]
-    lane = iota(1)
+    lane, sub = iota(1), iota(0)
     for j in range(tiles):
         for r in range(5):
             x, y = returned[2 * j, tile(r % 3), :], returned[2 * j + 1, tile(r % 3), :]
@@ -220,6 +308,10 @@
                 error = jnp.where(lane < 64, pltpu.roll(x, 64, 1), y)
             put(err, j, r, error)
             put(one, j, r, start[j, tile(r, 8), :] + error)
+        after, behind = pltpu.roll(error, 7, 0), pltpu.roll(error, 1, 0)
+        under = after - coef[1, j, tile(4), :] * behind
+        over = behind - coef[2, j, tile(4), :] * after
+        extra[j] = rims[0, j] + jnp.where(sub == 1, under, jnp.where(sub == 6, over, 0.0))
 
     def coarse(j, r, value, own):
         put(half, j, r, 2.0 * value - own)
@@ -229,7 +321,8 @@
 
     def fine(inner, target):
         def use(j, r, value, _):
-            value = value + (forcing[inner, tile(r), cols(j)] if r < 4 else rims[inner, j, :, :])
+            beyond = extra if inner == 0 else rims.at[1]
+            value = value + (forcing[inner, tile(r), cols(j)] if r < 4 else beyond[j])
             if r < 4:
                 states[inner, tile(r), cols(j)] = value
             if target is not None:
@@ -252,39 +345,53 @@
     everything = ("chip", "core", "space")
     chip, core = lax.axis_index("chip"), lax.axis_index("core")
     turn = chip * cores + core
-    flag = jnp.stack([turn == 0, core, turn == owners - 1, turn]).astype(jnp.int32)
+    flag = jnp.stack([turn == 0, core, turn == owners - 1, turn, lax.axis_index("space") % 2]).astype(jnp.int32)
 
     def shaped(*shape):
         return jax.ShapeDtypeStruct(shape, F32)
 
-    def whole(*shape):
-        return pl.BlockSpec(shape, lambda i: (0,) * len(shape))
-
-    block = whole(ROWS, columns)
-    last, start_low, start_up, low, up = pl.pallas_call(
+    last = pl.pallas_call(
+        last_kernel,
+        in_specs=[ANY],
+        out_specs=VMEM,
+        out_shape=shaped(ROWS, columns),
+        scratch_shapes=[pltpu.SemaphoreType.DMA],
+        compiler_params=params(52),
+        name="last",
+    )(guess)
+    before = lax.ppermute(last, ("chip", "core"), [(i, i + 1) for i in range(owners - 1)])
+    small = pltpu.VMEM((2, tiles, 8, LANES), F32)
+    edge_rows = pltpu.VMEM((2, 8, columns), F32)
+    rim_one, rim_two, start_one, start_two = pl.pallas_call(
         rim_kernel,
-        grid=(1,),
-        in_specs=[SMEM, pl.BlockSpec((1, ROWS, columns), lambda i: (3, 0, 0)), block, block, block, block,
-                  whole(3, ROWS, columns)],
-        out_specs=[block, whole(4, columns), whole(4, columns), whole(tiles, 16, LANES), whole(tiles, 16, LANES)],
-        out_shape=[shaped(ROWS, columns), shaped(4, columns), shaped(4, columns), shaped(tiles, 16, LANES),
-                   shaped(tiles, 16, LANES)],
-        compiler_params=params(20),
+        in_specs=[SMEM] + [ANY] * 6,
+        out_specs=[VMEM] * 4,
+        out_shape=[shaped(tiles, 8, LANES), shaped(tiles, 8, LANES), shaped(tiles, 4, LANES), shaped(tiles, 4, LANES)],
+        scratch_shapes=[
+            edge_rows,
+            edge_rows,
+            pltpu.VMEM((3, 2, 8, columns), F32),
+            pltpu.VMEM((3, 2, 8, columns), F32),
+            pltpu.VMEM((2, 5, tiles, 8, LANES), F32),
+            small,
+            pltpu.VMEM((2, 2, tiles, 8, LANES), F32),
+            pltpu.SemaphoreType.DMA((16,)),
+        ],
+        compiler_params=params(52),
         name="rim",
     )(flag, guess, initial, courant_rows, courant_cols, diffusion, forcing)
 
-    before = lax.ppermute(last, ("chip", "core"), [(i, i + 1) for i in range(owners - 1)])
-
-    def shifted(value, by_turn, by_space):
+    def exchanged(value, by_turn, first):
         pairs = []
         for k in range(owners):
             for s in range(spaces):
-                if 0 <= s + by_space < spaces:
-                    pairs.append((k * spaces + s, (k + by_turn) % owners * spaces + s + by_space))
+                partner = s + 1 if (s % 2 == 0) == first else s - 1
+                if 0 <= partner < spaces:
+                    pairs.append((k * spaces + s, (k + by_turn) % owners * spaces + partner))
         return lax.ppermute(value, everything, pairs)
 
-    start_up, start_low = shifted(start_up, 1, 1), shifted(start_low, 1, -1)
-    up, low = shifted(up, 0, 1), shifted(low, 0, -1)
+    rim_one, rim_two = exchanged(rim_one, 0, True), exchanged(rim_two, 0, False)
+    start_one, start_two = exchanged(start_one, 1, True), exchanged(start_two, 1, False)
 
     field = pltpu.VMEM((tiles, 48, LANES), F32)
     messages, ends, coef, rims, start = pl.pallas_call(
@@ -293,10 +400,10 @@
         out_specs=[VMEM] * 5,
         out_shape=[shaped(2 * tiles, 40, LANES), shaped(tiles, ROWS, LANES), shaped(5, tiles, 40, LANES),
                    shaped(3, tiles, 8, LANES), shaped(tiles, 48, LANES)],
-        scratch_shapes=[field, field, pltpu.VMEM((tiles, ROWS, LANES), F32)],
+        scratch_shapes=[field, field, pltpu.VMEM((tiles, ROWS, LANES), F32), small],
         compiler_params=params(20),
         name="residual",
-    )(flag, before, initial, start_low, start_up, low, up, last, forcing, courant_rows, courant_cols, diffusion)
+    )(flag, before, initial, start_one, start_two, rim_one, rim_two, last, forcing, courant_rows, courant_cols, diffusion)
 
     mine = lax.all_to_all(messages, ("chip", "space"), 0, 0, tiled=True)
     other = lax.ppermute(mine, "core", [(0, 1), (1, 0)])
@@ -320,7 +427,7 @@
         in_specs=[VMEM] * 6,
         out_specs=VMEM,
         out_shape=shaped(4, ROWS, columns),
-        scratch_shapes=[field, field, field, field],
+        scratch_shapes=[field, field, field, field, pltpu.VMEM((tiles, 8, LANES), F32)],
         compiler_params=params(20),
         name="final",
     )(start, coef, rims, forcing, ends, returned)

time: 102 us -> 89.7 us (0.88)
  local copies, waits for them, and re-layouts: 7.35 us -> 0.11 us
  starting transfers between devices: 16.6 us -> 11.7 us
  Pallas kernels: 12.8 us -> 17.2 us
  waiting for transfers between devices: 7.54 us -> 5.03 us
  blocking collectives: 56.6 us -> 55.2 us
    unnamed x14 -> x10, local copies, waits for them, and re-layouts: 7.35 us -> 0.02 us
    ppermute x4, starting transfers between devices: 15.3 us -> 10.4 us  [exchanged(): return lax.ppermute(value, everything, pairs)]
    pallas_call x1 -> x2, Pallas kernels: 0.74 us -> 4.54 us  [the longest x1 3.37 us: on_device(): pl.pallas_call(rim_kernel, in_specs=[SMEM] + [ANY] * 6, out_specs=[VMEM]...]
    ppermute x4, waiting for transfers between devices: 4.51 us -> 1.99 us  [exchanged(): return lax.ppermute(value, everything, pairs)]
    all_to_all x1, blocking collectives: 35.9 us -> 34.4 us  [on_device(): mine = lax.all_to_all(messages, ('chip', 'space'), 0, 0, tiled=True)]
  transfers between devices with their start and end apart: 6 -> 6, of which waited for: 3 -> 2; matrix products, arithmetic and copies ran while one was open for 0% -> 0% of each run, Pallas kernels for 0% -> 4%
where the time goes in v2:
time: 89.7 us; the launch traced here: 89.4 us
  blocking collectives  55.2 us (62%)
  Pallas kernels  17.2 us (19%)
  starting transfers between devices  11.7 us (13%)
  waiting for transfers between devices  5.03 us (6%)
    all_to_all x1, blocking collectives, on_device(): mine = lax.all_to_all(messages, ('chip', 'space'), 0, 0, tiled=True)  34.4 us
    all_to_all x1, blocking collectives, on_device(): returned = lax.all_to_all(answer, ('chip', 'space'), 0, 0, tiled=True)  20.8 us
    ppermute x4, starting transfers between devices, exchanged(): return lax.ppermute(value, everything, pairs)  10.4 us
    pallas_call x1, Pallas kernels, on_device(): pl.pallas_call(chain_kernel, in_specs=[SMEM, VMEM, VMEM], out_specs=VMEM,...  5.55 us
    pallas_call x1, Pallas kernels, on_device(): pl.pallas_call(final_kernel, in_specs=[VMEM] * 6, out_specs=VMEM, out_sha...  3.81 us
    pallas_call x1, Pallas kernels, on_device(): pl.pallas_call(rim_kernel, in_specs=[SMEM] + [ANY] * 6, out_specs=[VMEM]...  3.37 us
    pallas_call x1, Pallas kernels, on_device(): pl.pallas_call(residual_kernel, in_specs=[SMEM] + [VMEM] * 11, out_specs=...  3.33 us
    ppermute x1, waiting for transfers between devices, on_device(): other = lax.ppermute(mine, 'core', [(0, 1), (1, 0)])  3.03 us
  transfers between devices with their start and end apart: 6, of which 2 were waited for; matrix products, arithmetic and copies ran while one was open for 0% of the time, Pallas kernels for 4%

profile of v2, /device:TPU:0, one launch (start us, length us, event | category | flops | bytes accessed | tf_op | source)
XLA Modules:
  0.0 89.4 jit_solution(15019447843614154151)
XLA Ops:
  0.0 0.0 copy-start.3
  0.0 0.0 copy-start.2
  0.0 0.0 copy-start.1
  0.0 1.2 %last.1.guess = f32[32,4096]{1,0:T(8,128)S(1)} custom-call(f32[4,32,4096]{2,1,0:T(8,128)} %guess.3), custom_call_target="tpu_custom_call" | custom-call | tf_op jit(solution)/shard_map/last/pallas_call | solution.py:353
  1.2 1.3 %collective-permute-start = (f32[32,4096]{1,0:T(8,128)S(1)}, f32[32,4096]{1,0:T(8,128)S(1)}, u32[]{:S(2)}, u32[]{:S(2)}) collective-permute-start(f32[32,4096]{1,0:T(8,128)S(1)} %last.1.guess), channel_id=1, source_target_pairs={{0,8},{8,16},{16,24},{24,32},{32,40},{40,48},{48,56},{56,64},{64,7... | collective-permute-start | bytes 1572872 | tf_op jit(solution)/shard_map/ppermute | solution.py:362
  2.5 0.1 stack.31.flag
  2.6 0.0 copy-done.3
  2.6 0.0 copy-done.2
  2.6 0.0 copy-done.1
  2.6 0.0 copy-start
  2.6 0.0 copy-start.4
  2.6 3.4 %rim.1 = (f32[32,8,128]{2,1,0:T(8,128)S(1)}, f32[32,8,128]{2,1,0:T(8,128)S(1)}, f32[32,4,128]{2,1,0:T(4,128)S(1)}, f32[32,4,128]{2,1,0:T(4,128)S(1)}) custom-call(s32[5]{0:T(128)S(1)} %stack.31.flag, f32[4,32,4096]{2,1,0:T(8,128)} %guess.3, f32[32,4096]{1,0:T(8,128)S(1)} %copy-done.1, f32[32,4096]{1,0:T(8,128)S(1)} %copy-done.2, f32[32,4096]{1,0:T(8,128)S(1)} %copy-done.3, ...), custom_call_target="tpu_custom_call" | custom-call | tf_op jit(solution)/shard_map/rim/pallas_call | solution.py:365
  6.0 2.5 %collective-permute-start.3 = (f32[32,8,128]{2,1,0:T(8,128)S(1)}, f32[32,8,128]{2,1,0:T(8,128)S(1)}, u32[]{:S(2)}, u32[]{:S(2)}) collective-permute-start(f32[32,8,128]{2,1,0:T(8,128)S(1)} %get-tuple-element.16), channel_id=1, source_target_pairs={{0,1},{1,0},{2,3},{3,2},{4,5},{5,4},{6,7},{7,6},{8,9},{9,8},{10,11... | collective-permute-start | bytes 393224 | tf_op jit(solution)/shard_map/ppermute | solution.py:391
  8.6 0.7 collective-permute-start.4
  9.2 6.5 %collective-permute-start.1 = (f32[32,4,128]{2,1,0:T(4,128)S(1)}, f32[32,4,128]{2,1,0:T(4,128)S(1)}, u32[]{:S(2)}, u32[]{:S(2)}) collective-permute-start(f32[32,4,128]{2,1,0:T(4,128)S(1)} %get-tuple-element.14), channel_id=1, source_target_pairs={{0,9},{1,8},{2,11},{3,10},{4,13},{5,12},{6,15},{7,14},{8,17},{9,16... | collective-permute-start | bytes 196616 | tf_op jit(solution)/shard_map/ppermute | solution.py:391
  15.8 0.7 collective-permute-start.2
  16.4 2.0 %collective-permute-done.1.start_one = f32[32,4,128]{2,1,0:T(4,128)S(1)} collective-permute-done((f32[32,4,128]{2,1,0:T(4,128)S(1)}, f32[32,4,128]{2,1,0:T(4,128)S(1)}, u32[]{:S(2)}, u32[]{:S(2)}) %collective-permute-start.1) | collective-permute-done | bytes 65568 | tf_op jit(solution)/shard_map/ppermute | solution.py:391
  18.4 0.0 collective-permute-done.2.start_two
  18.4 0.0 collective-permute-done.3.rim_one
  18.4 0.0 collective-permute-done.4.rim_two
  18.4 0.0 collective-permute-done.before
  18.4 0.0 copy-done
  18.4 0.0 copy-done.4
  18.4 3.3 %residual.1 = (f32[64,40,128]{2,1,0:T(8,128)S(1)}, f32[32,32,128]{2,1,0:T(8,128)S(1)}, f32[5,32,40,128]{3,2,1,0:T(8,128)S(1)}, f32[3,32,8,128]{3,2,1,0:T(8,128)S(1)}, f32[32,48,128]{2,1,0:T(8,128)S(1)}) custom-call(s32[5]{0:T(128)S(1)} %stack.31.flag, f32[32,4096]{1,0:T(8,128)S(1)} %collective-permute-done.before, f32[32,4096]{1,0:T(8,128)S(1)} %copy-done.1, ...), custom_call_target="tpu_custom_call" | custom-call | tf_op jit(solution)/shard_map/residual/pallas_call | solution.py:397
  21.8 34.4 %all_to_all.10.mine = f32[64,40,128]{2,1,0:T(8,128)S(1)} all-to-all(f32[64,40,128]{2,1,0:T(8,128)S(1)} %get-tuple-element.22), channel_id=1, replica_groups=mesh['chip'=8,'core'=2,'space'=8] {'chip','space'}, dimensions={0} | all-to-all | bytes 2621440 | tf_op jit(solution)/shard_map/all_to_all | solution.py:408
  56.2 0.0 collective-permute-start.5
  56.2 3.0 %collective-permute-done.5.other = f32[64,40,128]{2,1,0:T(8,128)S(1)} collective-permute-done((f32[64,40,128]{2,1,0:T(8,128)S(1)}, f32[64,40,128]{2,1,0:T(8,128)S(1)}, u32[]{:S(2)}, u32[]{:S(2)}) %collective-permute-start.5) | collective-permute-done | bytes 1310752 | tf_op jit(solution)/shard_map/ppermute | solution.py:409
  59.2 5.5 %chain.1 = f32[64,24,128]{2,1,0:T(8,128)S(1)} custom-call(s32[5]{0:T(128)S(1)} %stack.31.flag, f32[64,40,128]{2,1,0:T(8,128)S(1)} %all_to_all.10.mine, f32[64,40,128]{2,1,0:T(8,128)S(1)} %collective-permute-done.5.other), custom_call_target="tpu_custom_call" | custom-call | tf_op jit(solution)/shard_map/chain/pallas_call | solution.py:411
  64.8 20.8 %all_to_all.11.returned = f32[64,24,128]{2,1,0:T(8,128)S(1)} all-to-all(f32[64,24,128]{2,1,0:T(8,128)S(1)} %chain.1), channel_id=1, replica_groups=mesh['chip'=8,'core'=2,'space'=8] {'chip','space'}, dimensions={0} | all-to-all | bytes 1572864 | tf_op jit(solution)/shard_map/all_to_all | solution.py:424
  85.6 3.8 %final.1 = f32[4,32,4096]{2,1,0:T(8,128)} custom-call(f32[32,48,128]{2,1,0:T(8,128)S(1)} %get-tuple-element.18.start, f32[5,32,40,128]{3,2,1,0:T(8,128)S(1)} %get-tuple-element.19.coef, f32[3,32,8,128]{3,2,1,0:T(8,128)S(1)} %get-tuple-element.20.rims, f32[4,32,4096]{2,1,0:T(8,128)S(1)} %copy-done, f32[32,32,128]{2,1,0:T(8,128)S(1)} %get-tuple-element.21.ends, ...), custom_call_target="tpu_custom_call" | custom-call | tf_op jit(solution)/shard_map/final/pallas_call | solution.py:425
Async XLA Ops:
  0.0 2.6 %copy-start.3 = (f32[32,4096]{1,0:T(8,128)S(1)}, f32[32,4096]{1,0:T(8,128)}, u32[]{:S(2)}) copy-start(f32[32,4096]{1,0:T(8,128)} %b.3) | copy-start | bytes 1572868
  0.0 2.6 %copy-start.2 = (f32[32,4096]{1,0:T(8,128)S(1)}, f32[32,4096]{1,0:T(8,128)}, u32[]{:S(2)}) copy-start(f32[32,4096]{1,0:T(8,128)} %a.3) | copy-start | bytes 1572868
  0.0 2.6 %copy-start.1 = (f32[32,4096]{1,0:T(8,128)S(1)}, f32[32,4096]{1,0:T(8,128)}, u32[]{:S(2)}) copy-start(f32[32,4096]{1,0:T(8,128)} %initial.3) | copy-start | bytes 1572868
  1.2 17.2 %collective-permute-start = (f32[32,4096]{1,0:T(8,128)S(1)}, f32[32,4096]{1,0:T(8,128)S(1)}, u32[]{:S(2)}, u32[]{:S(2)}) collective-permute-start(f32[32,4096]{1,0:T(8,128)S(1)} %last.1.guess), channel_id=1, source_target_pairs={{0,8},{8,16},{16,24},{24,32},{32,40},{40,48},{48,56},{56,64},{64,7... | collective-permute-start | bytes 1572872 | tf_op jit(solution)/shard_map/ppermute | solution.py:362
  2.6 15.8 %copy-start = (f32[4,32,4096]{2,1,0:T(8,128)S(1)}, f32[4,32,4096]{2,1,0:T(8,128)}, u32[]{:S(2)}) copy-start(f32[4,32,4096]{2,1,0:T(8,128)} %forcing.5) | copy-start | bytes 6291460
  2.6 15.8 %copy-start.4 = (f32[32,4096]{1,0:T(8,128)S(1)}, f32[32,4096]{1,0:T(8,128)}, u32[]{:S(2)}) copy-start(f32[32,4096]{1,0:T(8,128)} %d.3) | copy-start | bytes 1572868
  6.0 12.4 %collective-permute-start.3 = (f32[32,8,128]{2,1,0:T(8,128)S(1)}, f32[32,8,128]{2,1,0:T(8,128)S(1)}, u32[]{:S(2)}, u32[]{:S(2)}) collective-permute-start(f32[32,8,128]{2,1,0:T(8,128)S(1)} %get-tuple-element.16), channel_id=1, source_target_pairs={{0,1},{1,0},{2,3},{3,2},{4,5},{5,4},{6,7},{7,6},{8,9},{9,8},{10,11... | collective-permute-start | bytes 393224 | tf_op jit(solution)/shard_map/ppermute | solution.py:391
  8.6 9.9 %collective-permute-start.4 = (f32[32,8,128]{2,1,0:T(8,128)S(1)}, f32[32,8,128]{2,1,0:T(8,128)S(1)}, u32[]{:S(2)}, u32[]{:S(2)}) collective-permute-start(f32[32,8,128]{2,1,0:T(8,128)S(1)} %get-tuple-element.17), channel_id=1, source_target_pairs={{1,2},{2,1},{3,4},{4,3},{5,6},{6,5},{9,10},{10,9},{11,12},{12,11},... | collective-permute-start | bytes 393224 | tf_op jit(solution)/shard_map/ppermute | solution.py:391
  9.2 9.2 %collective-permute-start.1 = (f32[32,4,128]{2,1,0:T(4,128)S(1)}, f32[32,4,128]{2,1,0:T(4,128)S(1)}, u32[]{:S(2)}, u32[]{:S(2)}) collective-permute-start(f32[32,4,128]{2,1,0:T(4,128)S(1)} %get-tuple-element.14), channel_id=1, source_target_pairs={{0,9},{1,8},{2,11},{3,10},{4,13},{5,12},{6,15},{7,14},{8,17},{9,16... | collective-permute-start | bytes 196616 | tf_op jit(solution)/shard_map/ppermute | solution.py:391
  15.8 2.6 %collective-permute-start.2 = (f32[32,4,128]{2,1,0:T(4,128)S(1)}, f32[32,4,128]{2,1,0:T(4,128)S(1)}, u32[]{:S(2)}, u32[]{:S(2)}) collective-permute-start(f32[32,4,128]{2,1,0:T(4,128)S(1)} %get-tuple-element.15), channel_id=1, source_target_pairs={{1,10},{2,9},{3,12},{4,11},{5,14},{6,13},{9,18},{10,17},{11,20},{1... | collective-permute-start | bytes 196616 | tf_op jit(solution)/shard_map/ppermute | solution.py:391
  56.2 3.0 %collective-permute-start.5 = (f32[64,40,128]{2,1,0:T(8,128)S(1)}, f32[64,40,128]{2,1,0:T(8,128)S(1)}, u32[]{:S(2)}, u32[]{:S(2)}) collective-permute-start(f32[64,40,128]{2,1,0:T(8,128)S(1)} %all_to_all.10.mine), channel_id=1, source_target_pairs={{0,8},{8,0},{1,9},{9,1},{2,10},{10,2},{3,11},{11,3},{4,12},{12,4},... | collective-permute-start | bytes 3932168 | tf_op jit(solution)/shard_map/ppermute | solution.py:409

commit v3 on v2

--- a/solution.py
+++ b/solution.py
@@ -78,8 +78,18 @@
     copy.wait()
 
 
+class Tiles:
+    def __init__(self, get):
+        self.get, self.seen = get, {}
+
+    def __getitem__(self, j):
+        if j not in self.seen:
+            self.seen[j] = self.get(j)
+        return self.seen[j]
+
+
 def rim_kernel(flag, guess, initial, a, b, d, forcing, rim_one, rim_two, start_one, start_two,
-               va, vi, vg, vc, coef, field, after, sems):
+               va, vi, vg, vc, coef, field, part, after, sems):
     rows, columns = a.shape
     tiles = columns // LANES
     sub, lane = iota(0), iota(1)
@@ -96,72 +106,63 @@
     for copy in copies:
         copy.wait()
     at_end, even = flag[2] == 1, flag[4] == 0
-
-    def outward(x, side):
-        return pltpu.roll(x, 7 if side == 0 else 1, 0)
-
-    def inward(x, side):
-        return pltpu.roll(x, 1 if side == 0 else 7, 0)
+    top = sub < 4
+
+    def both(ref, j):
+        return jnp.where(top, ref[0, :, cols(j)], ref[1, :, cols(j)])
+
+    def outward(x):
+        return jnp.where(top, pltpu.roll(x, 7, 0), pltpu.roll(x, 1, 0))
+
+    def inward(x):
+        return jnp.where(top, pltpu.roll(x, 1, 0), pltpu.roll(x, 7, 0))
 
     def row(x, side, place, to):
         at = place - 1 if side == 0 else 8 - place
         return pltpu.roll(x, (to - at) % 8, 0)
 
-    def open_step(values, j, side):
+    OWN, OUT, IN, LEFT, RIGHT = range(5)
+
+    def open_step(values, j):
         x, y, z = (values[i % tiles] for i in (j - 1, j, j + 1))
         left = pltpu.roll(jnp.where(lane == LANES - 1, x, y), 1, 1)
         right = pltpu.roll(jnp.where(lane == 0, z, y), LANES - 1, 1)
-        out = coef[side, 2 - side, j]
-        return coef[side, 0, j] * y + out * outward(y, side) + coef[side, 3, j] * left + coef[side, 4, j] * right
-
-    class Tiles:
-        def __init__(self, get):
-            self.get, self.seen = get, {}
-
-        def __getitem__(self, j):
-            if j not in self.seen:
-                self.seen[j] = self.get(j)
-            return self.seen[j]
-
-    for side in range(2):
-        for j in range(tiles):
-            for i, value in enumerate(rates(*(vc[n, side, :, cols(j)] for n in range(3)))):
-                coef[side, i, j] = value
-            field[side, j] = jnp.where(at_end, vi[side, :, cols(j)], va[side, :, cols(j)])
-    for side in range(2):
-        values = Tiles(lambda j, side=side: field[side, j])
-        for j in range(tiles):
-            part = open_step(values, j, side)
-            after[side, 0, j] = part
-            after[side, 1, j] = part + coef[side, 1 + side, j] * inward(values[j], side)
-    for j in range(tiles):
+        total = coef[OWN, j] * y + coef[OUT, j] * outward(y)
+        return total + (coef[LEFT, j] * left + coef[RIGHT, j] * right)
+
+    for j in range(tiles):
+        own, upper, lower, left, right = rates(*(both(vc.at[n], j) for n in range(3)))
+        coef[OWN, j], coef[LEFT, j], coef[RIGHT, j] = own, left, right
+        coef[OUT, j], coef[IN, j] = jnp.where(top, lower, upper), jnp.where(top, upper, lower)
+        field[j] = jnp.where(at_end, both(vi, j), both(va, j))
+    values = Tiles(lambda j: field[j])
+    for j in range(tiles):
+        part[j] = open_step(values, j)
+        after[j] = part[j] + coef[IN, j] * inward(values[j])
+    forced, stepped = Tiles(lambda j: both(vg.at[0], j)), Tiles(lambda j: after[j])
+    for j in range(tiles):
+        g1, g2, g3 = forced[j], both(vg.at[1], j), both(vg.at[2], j)
+        items = [(G1, g1, 1), (G2, g2 + coef[OUT, j] * outward(g1), 1), (G3, g3, 1), (PART, open_step(forced, j) + g2, 2)]
+        items += [(A1 + i, both(vc.at[i], j), 1) for i in range(3)]
+        items += [(INWARD, coef[IN, j], 2)]
+        values, second = field[j], open_step(stepped, j)
+        begins = [(START1, values, 1), (START2, values, 2), (STEP1, part[j], 2), (STEP2, second, 2)]
         rims, starts = [], []
         for side in range(2):
-            forced = Tiles(lambda j, side=side: vg[0, side, :, cols(j)])
-            stepped = Tiles(lambda j, side=side: after[side, 1, j])
-            g1, g2, g3 = (vg[i, side, :, cols(j)] for i in range(3))
-            second = g2 + coef[side, 2 - side, j] * outward(g1, side)
-            part = open_step(forced, j, side) + g2
-            items = [(G1, g1, 1), (G2, second, 1), (G3, g3, 1), (PART, part, 2)]
-            items += [(A1 + i, vc[i, side, :, cols(j)], 1) for i in range(3)]
-            items += [(INWARD, coef[side, 1 + side, j], 2)]
-            total = row(g1, side, 1, 0)
-            for to, value, place in items[1:]:
-                total = jnp.where(sub == to, row(value, side, place, to), total)
-            rims.append(total)
-            values = field[side, j]
-            total = row(values, side, 1, START1)
-            for to, value in ((START2, values), (STEP1, after[side, 0, j]), (STEP2, open_step(stepped, j, side))):
-                total = jnp.where(sub == to, row(value, side, 2, to), total)
-            starts.append(total[0:4])
+            for found, made in ((items, rims), (begins, starts)):
+                total = None
+                for to, value, place in found:
+                    value = row(value, side, place, to)
+                    total = value if total is None else jnp.where(sub == to, value, total)
+                made.append(total)
         rim_one[j] = jnp.where(even, rims[1], rims[0])
         rim_two[j] = jnp.where(even, rims[0], rims[1])
-        start_one[j] = jnp.where(even, starts[1], starts[0])
-        start_two[j] = jnp.where(even, starts[0], starts[1])
+        start_one[j] = jnp.where(even, starts[1], starts[0])[0:4]
+        start_two[j] = jnp.where(even, starts[0], starts[1])[0:4]
 
 
 def residual_kernel(flag, before, initial, start_one, start_two, rim_one, rim_two, guess, forcing, a, b, d,
-                    messages, ends, coef, rims, one, two, three, res, edge):
+                    messages, ends, coef, two, three, four, rims, one, res, edge):
     tiles = a.shape[1] // LANES
     lane, sub = iota(1), iota(0)
     first, even = flag[0] == 1, flag[4] == 0
@@ -196,7 +197,7 @@
         rims[1, j] = border(low, up, G2) + border(start_low, start_up, STEP2, 2) + border(low, up, PART, 2)
         rims[2, j] = border(low, up, G3)
 
-    for inner, (source, target) in enumerate([(one, two), (two, three), (three, two)]):
+    for inner, (source, target) in enumerate([(one, two), (two, three), (three, four)]):
 
         def fine(j, r, value, _, inner=inner, target=target):
             put(target, j, r, value + (forcing[inner, tile(r), cols(j)] if r < 4 else rims[inner, j]))
@@ -208,7 +209,7 @@
         ends[j, tile(r), :] = value
         res[j, tile(r), :] = value - guess[tile(r), cols(j)]
 
-    sweep(two, coef, range(4), last)
+    sweep(four, coef, range(4), last)
 
     for r in range(4):
         for j in range(tiles):
@@ -231,26 +232,10 @@
     rows = spaces * ROWS
     blocks = rows // 8
     lane, sub = iota(1), iota(0)
-    even = flag[1] == 0
     zero = jnp.zeros((8, LANES), F32)
-
-    def arrived(pair, odd, s, r):
-        same, across = mine[pair * spaces + s, tile(r), :], other[pair * spaces + s, tile(r), :]
-        return jnp.where(even, across, same) if odd else jnp.where(even, same, across)
-
-    for s in range(spaces):
-        for r in range(4):
-            a, b, d = (arrived((4 * i + r) // 2, r % 2 == 1, s, 4) for i in range(3))
-            own, up, low, left, right = rates(a, b, d)
-            at = tile(r, s * ROWS)
-            coef[0, at, :] = 2.0 * own - 1.0
-            for i, value in enumerate((up, low, left, right)):
-                coef[i + 1, at, :] = 2.0 * value
     for ref in (one, two):
         ref[0:8, :] = zero
         ref[rows + 8 : rows + 16, :] = zero
-    for t in range(blocks):
-        one[tile(t, 8), :] = zero
 
     def step(source, t):
         at = 8 * t + 8
@@ -280,25 +265,54 @@
         for t in range(blocks):
             two[tile(t, 8), :] = step(one, t)
 
-    def rest(pair, odd):
+    def run(even):
+        sources = (mine, other) if even else (other, mine)
+
+        def arrived(pair, odd, t):
+            return sources[int(odd)][pair * spaces + t // 4, tile(t % 4), :]
+
+        def rest(pair, odd):
+            for t in range(blocks):
+                one[tile(t, 8), :] = step(two, t) + arrived(pair, odd, t)
+
+        for s in range(spaces):
+            for r in range(4):
+                a, b, d = (sources[r % 2][(4 * i + r) // 2 * spaces + s, tile(4), :] for i in range(3))
+                own, up, low, left, right = rates(a, b, d)
+                at = tile(r, s * ROWS)
+                coef[0, at, :] = 2.0 * own - 1.0
+                for i, value in enumerate((up, low, left, right)):
+                    coef[i + 1, at, :] = 2.0 * value
         for t in range(blocks):
-            one[tile(t, 8), :] = step(two, t) + arrived(pair, odd, t // 4, t % 4)
-
-    def turn(pair, _):
-        half()
-        pl.when(even)(lambda: emit(pair))
-        rest(pair, False)
-        half()
-        pl.when(jnp.logical_not(even))(lambda: emit(pair))
-        pl.when(pair < pairs - 1)(lambda: rest(pair, True))
-        return 0
-
-    lax.fori_loop(0, pairs, turn, 0)
-
-
-def final_kernel(start, coef, rims, forcing, ends, returned, states, one, two, err, half, extra):
-    tiles = start.shape[0]
+            one[tile(t, 8), :] = arrived(0, False, t)
+        if even:
+            for s in range(spaces):
+                messages[s] = jnp.zeros((24, LANES), F32)
+
+        def turn(pair, _):
+            half()
+            if not even:
+                emit(pair)
+            rest(pair, True)
+            half()
+            if even:
+                emit(pair + 1)
+            rest(pair + 1, False)
+            return 0
+
+        lax.fori_loop(0, pairs - 1, turn, 0)
+        if not even:
+            half()
+            emit(pairs - 1)
+
+    pl.when(flag[1] == 0)(lambda: run(True))
+    pl.when(flag[1] != 0)(lambda: run(False))
+
+
+def final_kernel(coef, first, second, third, ends, returned, states, err, one, two, extra, out, sems):
+    tiles = first.shape[0]
     lane, sub = iota(1), iota(0)
+    copies = [pltpu.make_async_copy(out.at[i], states.at[i], sems.at[i]) for i in range(4)]
     for j in range(tiles):
         for r in range(5):
             x, y = returned[2 * j, tile(r % 3), :], returned[2 * j + 1, tile(r % 3), :]
@@ -307,34 +321,34 @@
             else:
                 error = jnp.where(lane < 64, pltpu.roll(x, 64, 1), y)
             put(err, j, r, error)
-            put(one, j, r, start[j, tile(r, 8), :] + error)
         after, behind = pltpu.roll(error, 7, 0), pltpu.roll(error, 1, 0)
         under = after - coef[1, j, tile(4), :] * behind
         over = behind - coef[2, j, tile(4), :] * after
-        extra[j] = rims[0, j] + jnp.where(sub == 1, under, jnp.where(sub == 6, over, 0.0))
-
-    def coarse(j, r, value, own):
-        put(half, j, r, 2.0 * value - own)
-
-    def corrected(j, r, value, own):
-        states[3, tile(r), cols(j)] = ends[j, tile(r), :] + (2.0 * value - own)
-
-    def fine(inner, target):
-        def use(j, r, value, _):
-            beyond = extra if inner == 0 else rims.at[1]
-            value = value + (forcing[inner, tile(r), cols(j)] if r < 4 else beyond[j])
-            if r < 4:
-                states[inner, tile(r), cols(j)] = value
-            if target is not None:
-                put(target, j, r, value)
-
-        return use
-
-    sweep(one, coef, range(5), fine(0, two))
-    sweep(err, coef, range(5), coarse)
-    sweep(two, coef, range(5), fine(1, one))
-    sweep(half, coef, range(4), corrected)
-    sweep(one, coef, range(4), fine(2, None))
+        extra[j] = jnp.where(sub == 1, under, jnp.where(sub == 6, over, 0.0))
+
+    def step_one(j, r, value, _):
+        if r < 4:
+            out[0, tile(r), cols(j)] = first[j, tile(r, 8), :] + value
+        put(one, j, r, value if r < 4 else value + extra[j])
+
+    def step_two(j, r, value, before):
+        if r < 4:
+            out[1, tile(r), cols(j)] = second[j, tile(r, 8), :] + value
+            out[3, tile(r), cols(j)] = ends[j, tile(r), :] + (4.0 * (value - before) + err[j, tile(r, 8), :])
+        put(two, j, r, value)
+
+    def step_three(j, r, value, _):
+        out[2, tile(r), cols(j)] = third[j, tile(r, 8), :] + value
+
+    sweep(err, coef, range(5), step_one)
+    copies[0].start()
+    sweep(one, coef, range(5), step_two)
+    copies[1].start()
+    copies[3].start()
+    sweep(two, coef, range(4), step_three)
+    copies[2].start()
+    for copy in copies:
+        copy.wait()
 
 
 def on_device(guess, forcing, initial, courant_rows, courant_cols, diffusion):
@@ -360,7 +374,7 @@
         name="last",
     )(guess)
     before = lax.ppermute(last, ("chip", "core"), [(i, i + 1) for i in range(owners - 1)])
-    small = pltpu.VMEM((2, tiles, 8, LANES), F32)
+    small = pltpu.VMEM((tiles, 8, LANES), F32)
     edge_rows = pltpu.VMEM((2, 8, columns), F32)
     rim_one, rim_two, start_one, start_two = pl.pallas_call(
         rim_kernel,
@@ -372,9 +386,10 @@
             edge_rows,
             pltpu.VMEM((3, 2, 8, columns), F32),
             pltpu.VMEM((3, 2, 8, columns), F32),
-            pltpu.VMEM((2, 5, tiles, 8, LANES), F32),
+            pltpu.VMEM((5, tiles, 8, LANES), F32),
             small,
-            pltpu.VMEM((2, 2, tiles, 8, LANES), F32),
+            small,
+            small,
             pltpu.SemaphoreType.DMA((16,)),
         ],
         compiler_params=params(52),
@@ -394,13 +409,18 @@
     start_one, start_two = exchanged(start_one, 1, True), exchanged(start_two, 1, False)
 
     field = pltpu.VMEM((tiles, 48, LANES), F32)
-    messages, ends, coef, rims, start = pl.pallas_call(
+    tall = shaped(tiles, 48, LANES)
+    messages, ends, coef, *fields = pl.pallas_call(
         residual_kernel,
         in_specs=[SMEM] + [VMEM] * 11,
-        out_specs=[VMEM] * 5,
-        out_shape=[shaped(2 * tiles, 40, LANES), shaped(tiles, ROWS, LANES), shaped(5, tiles, 40, LANES),
-                   shaped(3, tiles, 8, LANES), shaped(tiles, 48, LANES)],
-        scratch_shapes=[field, field, pltpu.VMEM((tiles, ROWS, LANES), F32), small],
+        out_specs=[VMEM] * 6,
+        out_shape=[shaped(2 * tiles, 40, LANES), shaped(tiles, ROWS, LANES), shaped(5, tiles, 40, LANES), tall, tall, tall],
+        scratch_shapes=[
+            pltpu.VMEM((3, tiles, 8, LANES), F32),
+            field,
+            pltpu.VMEM((tiles, ROWS, LANES), F32),
+            pltpu.VMEM((2, tiles, 8, LANES), F32),
+        ],
         compiler_params=params(20),
         name="residual",
     )(flag, before, initial, start_one, start_two, rim_one, rim_two, last, forcing, courant_rows, courant_cols, diffusion)
@@ -425,12 +445,12 @@
     return pl.pallas_call(
         final_kernel,
         in_specs=[VMEM] * 6,
-        out_specs=VMEM,
+        out_specs=ANY,
         out_shape=shaped(4, ROWS, columns),
-        scratch_shapes=[field, field, field, field, pltpu.VMEM((tiles, 8, LANES), F32)],
+        scratch_shapes=[field, field, field, small, pltpu.VMEM((4, ROWS, columns), F32), pltpu.SemaphoreType.DMA((4,))],
         compiler_params=params(20),
         name="final",
-    )(start, coef, rims, forcing, ends, returned)
+    )(coef, *fields, ends, returned)
 
 
 def solution(mesh):

time: 89.7 us -> 86.6 us (0.965)
  Pallas kernels: 17.2 us -> 13.6 us
    pallas_call x1, Pallas kernels: 5.55 us -> 3.72 us  [on_device(): pl.pallas_call(chain_kernel, in_specs=[SMEM, VMEM, VMEM], out_specs=VMEM,...]
    pallas_call x1, Pallas kernels: 3.81 us -> 2.54 us  [on_device(): pl.pallas_call(final_kernel, in_specs=[VMEM] * 6, out_specs=ANY, out_shap...]
where the time goes in v3:
time: 86.6 us; the launch traced here: 86.3 us
  blocking collectives  55.7 us (64%)
  Pallas kernels  13.6 us (16%)
  starting transfers between devices  11.7 us (14%)
  waiting for transfers between devices  5.03 us (6%)
    all_to_all x1, blocking collectives, on_device(): mine = lax.all_to_all(messages, ('chip', 'space'), 0, 0, tiled=True)  34.6 us
    all_to_all x1, blocking collectives, on_device(): returned = lax.all_to_all(answer, ('chip', 'space'), 0, 0, tiled=True)  21.1 us
    ppermute x4, starting transfers between devices, exchanged(): return lax.ppermute(value, everything, pairs)  10.4 us
    pallas_call x1, Pallas kernels, on_device(): pl.pallas_call(chain_kernel, in_specs=[SMEM, VMEM, VMEM], out_specs=VMEM,...  3.72 us
    pallas_call x1, Pallas kernels, on_device(): pl.pallas_call(rim_kernel, in_specs=[SMEM] + [ANY] * 6, out_specs=[VMEM]...  3.18 us
    ppermute x1, waiting for transfers between devices, on_device(): other = lax.ppermute(mine, 'core', [(0, 1), (1, 0)])  3.03 us
    pallas_call x1, Pallas kernels, on_device(): pl.pallas_call(residual_kernel, in_specs=[SMEM] + [VMEM] * 11, out_specs=...  2.99 us
    pallas_call x1, Pallas kernels, on_device(): pl.pallas_call(final_kernel, in_specs=[VMEM] * 6, out_specs=ANY, out_shap...  2.54 us
  transfers between devices with their start and end apart: 6, of which 2 were waited for; matrix products, arithmetic and copies ran while one was open for 0% of the time, Pallas kernels for 4%

profile of v3, /device:TPU:0, one launch (start us, length us, event | category | flops | bytes accessed | tf_op | source)
XLA Modules:
  0.0 86.3 jit_solution(2954626290377149199)
XLA Ops:
  0.0 0.0 copy-start.3
  0.0 0.0 copy-start.2
  0.0 0.0 copy-start.1
  0.0 1.2 %last.1.guess = f32[32,4096]{1,0:T(8,128)S(1)} custom-call(f32[4,32,4096]{2,1,0:T(8,128)} %guess.3), custom_call_target="tpu_custom_call" | custom-call | tf_op jit(solution)/shard_map/last/pallas_call | solution.py:367
  1.2 1.3 %collective-permute-start = (f32[32,4096]{1,0:T(8,128)S(1)}, f32[32,4096]{1,0:T(8,128)S(1)}, u32[]{:S(2)}, u32[]{:S(2)}) collective-permute-start(f32[32,4096]{1,0:T(8,128)S(1)} %last.1.guess), channel_id=1, source_target_pairs={{0,8},{8,16},{16,24},{24,32},{32,40},{40,48},{48,56},{56,64},{64,7... | collective-permute-start | bytes 1572872 | tf_op jit(solution)/shard_map/ppermute | solution.py:376
  2.5 0.1 stack.31.flag
  2.6 0.0 copy-done.3
  2.6 0.0 copy-done.2
  2.6 0.0 copy-done.1
  2.6 0.0 copy-start
  2.6 0.0 copy-start.4
  2.6 3.2 %rim.1 = (f32[32,8,128]{2,1,0:T(8,128)S(1)}, f32[32,8,128]{2,1,0:T(8,128)S(1)}, f32[32,4,128]{2,1,0:T(4,128)S(1)}, f32[32,4,128]{2,1,0:T(4,128)S(1)}) custom-call(s32[5]{0:T(128)S(1)} %stack.31.flag, f32[4,32,4096]{2,1,0:T(8,128)} %guess.3, f32[32,4096]{1,0:T(8,128)S(1)} %copy-done.1, f32[32,4096]{1,0:T(8,128)S(1)} %copy-done.2, f32[32,4096]{1,0:T(8,128)S(1)} %copy-done.3, ...), custom_call_target="tpu_custom_call" | custom-call | tf_op jit(solution)/shard_map/rim/pallas_call | solution.py:379
  5.8 2.5 %collective-permute-start.3 = (f32[32,8,128]{2,1,0:T(8,128)S(1)}, f32[32,8,128]{2,1,0:T(8,128)S(1)}, u32[]{:S(2)}, u32[]{:S(2)}) collective-permute-start(f32[32,8,128]{2,1,0:T(8,128)S(1)} %get-tuple-element.17), channel_id=1, source_target_pairs={{0,1},{1,0},{2,3},{3,2},{4,5},{5,4},{6,7},{7,6},{8,9},{9,8},{10,11... | collective-permute-start | bytes 393224 | tf_op jit(solution)/shard_map/ppermute | solution.py:406
  8.4 0.7 collective-permute-start.4
  9.0 6.5 %collective-permute-start.1 = (f32[32,4,128]{2,1,0:T(4,128)S(1)}, f32[32,4,128]{2,1,0:T(4,128)S(1)}, u32[]{:S(2)}, u32[]{:S(2)}) collective-permute-start(f32[32,4,128]{2,1,0:T(4,128)S(1)} %get-tuple-element.15), channel_id=1, source_target_pairs={{0,9},{1,8},{2,11},{3,10},{4,13},{5,12},{6,15},{7,14},{8,17},{9,16... | collective-permute-start | bytes 196616 | tf_op jit(solution)/shard_map/ppermute | solution.py:406
  15.6 0.7 collective-permute-start.2
  16.2 2.0 %collective-permute-done.1.start_one = f32[32,4,128]{2,1,0:T(4,128)S(1)} collective-permute-done((f32[32,4,128]{2,1,0:T(4,128)S(1)}, f32[32,4,128]{2,1,0:T(4,128)S(1)}, u32[]{:S(2)}, u32[]{:S(2)}) %collective-permute-start.1) | collective-permute-done | bytes 65568 | tf_op jit(solution)/shard_map/ppermute | solution.py:406
  18.2 0.0 collective-permute-done.2.start_two
  18.2 0.0 collective-permute-done.3.rim_one
  18.2 0.0 collective-permute-done.4.rim_two
  18.2 0.0 collective-permute-done.before
  18.2 0.0 copy-done
  18.3 0.0 copy-done.4
  18.3 3.0 %residual.1 = (f32[64,40,128]{2,1,0:T(8,128)S(1)}, f32[32,32,128]{2,1,0:T(8,128)S(1)}, f32[5,32,40,128]{3,2,1,0:T(8,128)S(1)}, f32[32,48,128]{2,1,0:T(8,128)S(1)...) custom-call(s32[5]{0:T(128)S(1)} %stack.31.flag, f32[32,4096]{1,0:T(8,128)S(1)} %collective-permute-done.before, ...), custom_call_target="tpu_custom_call" | custom-call | tf_op jit(solution)/shard_map/residual/pallas_call | solution.py:413
  21.3 34.6 %all_to_all.10.mine = f32[64,40,128]{2,1,0:T(8,128)S(1)} all-to-all(f32[64,40,128]{2,1,0:T(8,128)S(1)} %get-tuple-element.24), channel_id=1, replica_groups=mesh['chip'=8,'core'=2,'space'=8] {'chip','space'}, dimensions={0} | all-to-all | bytes 2621440 | tf_op jit(solution)/shard_map/all_to_all | solution.py:428
  55.9 0.0 collective-permute-start.5
  55.9 3.0 %collective-permute-done.5.other = f32[64,40,128]{2,1,0:T(8,128)S(1)} collective-permute-done((f32[64,40,128]{2,1,0:T(8,128)S(1)}, f32[64,40,128]{2,1,0:T(8,128)S(1)}, u32[]{:S(2)}, u32[]{:S(2)}) %collective-permute-start.5) | collective-permute-done | bytes 1310752 | tf_op jit(solution)/shard_map/ppermute | solution.py:429
  58.9 3.7 %chain.1 = f32[64,24,128]{2,1,0:T(8,128)S(1)} custom-call(s32[5]{0:T(128)S(1)} %stack.31.flag, f32[64,40,128]{2,1,0:T(8,128)S(1)} %all_to_all.10.mine, f32[64,40,128]{2,1,0:T(8,128)S(1)} %collective-permute-done.5.other), custom_call_target="tpu_custom_call" | custom-call | tf_op jit(solution)/shard_map/chain/pallas_call | solution.py:431
  62.6 21.1 %all_to_all.11.returned = f32[64,24,128]{2,1,0:T(8,128)S(1)} all-to-all(f32[64,24,128]{2,1,0:T(8,128)S(1)} %chain.1), channel_id=1, replica_groups=mesh['chip'=8,'core'=2,'space'=8] {'chip','space'}, dimensions={0} | all-to-all | bytes 1572864 | tf_op jit(solution)/shard_map/all_to_all | solution.py:444
  83.8 2.5 %final.1 = f32[4,32,4096]{2,1,0:T(8,128)} custom-call(f32[5,32,40,128]{3,2,1,0:T(8,128)S(1)} %get-tuple-element.19.coef, f32[32,48,128]{2,1,0:T(8,128)S(1)} %get-tuple-element.20.first, f32[32,48,128]{2,1,0:T(8,128)S(1)} %get-tuple-element.21.second, f32[32,48,128]{2,1,0:T(8,128)S(1)} %get-tuple-element.22.third, f32[32,32,128]{2,1,0:T(8,128)S(1)} %get-tuple-element.23.ends, ...), custom_call_target="tpu_custom_call" | custom-call | tf_op jit(solution)/shard_map/final/pallas_call | solution.py:445
Async XLA Ops:
  0.0 2.6 %copy-start.3 = (f32[32,4096]{1,0:T(8,128)S(1)}, f32[32,4096]{1,0:T(8,128)}, u32[]{:S(2)}) copy-start(f32[32,4096]{1,0:T(8,128)} %b.3) | copy-start | bytes 1572868
  0.0 2.6 %copy-start.2 = (f32[32,4096]{1,0:T(8,128)S(1)}, f32[32,4096]{1,0:T(8,128)}, u32[]{:S(2)}) copy-start(f32[32,4096]{1,0:T(8,128)} %a.3) | copy-start | bytes 1572868
  0.0 2.6 %copy-start.1 = (f32[32,4096]{1,0:T(8,128)S(1)}, f32[32,4096]{1,0:T(8,128)}, u32[]{:S(2)}) copy-start(f32[32,4096]{1,0:T(8,128)} %initial.3) | copy-start | bytes 1572868
  1.2 17.1 %collective-permute-start = (f32[32,4096]{1,0:T(8,128)S(1)}, f32[32,4096]{1,0:T(8,128)S(1)}, u32[]{:S(2)}, u32[]{:S(2)}) collective-permute-start(f32[32,4096]{1,0:T(8,128)S(1)} %last.1.guess), channel_id=1, source_target_pairs={{0,8},{8,16},{16,24},{24,32},{32,40},{40,48},{48,56},{56,64},{64,7... | collective-permute-start | bytes 1572872 | tf_op jit(solution)/shard_map/ppermute | solution.py:376
  2.6 15.6 %copy-start = (f32[4,32,4096]{2,1,0:T(8,128)S(1)}, f32[4,32,4096]{2,1,0:T(8,128)}, u32[]{:S(2)}) copy-start(f32[4,32,4096]{2,1,0:T(8,128)} %forcing.3) | copy-start | bytes 6291460
  2.6 15.6 %copy-start.4 = (f32[32,4096]{1,0:T(8,128)S(1)}, f32[32,4096]{1,0:T(8,128)}, u32[]{:S(2)}) copy-start(f32[32,4096]{1,0:T(8,128)} %d.3) | copy-start | bytes 1572868
  5.8 12.4 %collective-permute-start.3 = (f32[32,8,128]{2,1,0:T(8,128)S(1)}, f32[32,8,128]{2,1,0:T(8,128)S(1)}, u32[]{:S(2)}, u32[]{:S(2)}) collective-permute-start(f32[32,8,128]{2,1,0:T(8,128)S(1)} %get-tuple-element.17), channel_id=1, source_target_pairs={{0,1},{1,0},{2,3},{3,2},{4,5},{5,4},{6,7},{7,6},{8,9},{9,8},{10,11... | collective-permute-start | bytes 393224 | tf_op jit(solution)/shard_map/ppermute | solution.py:406
  8.4 9.9 %collective-permute-start.4 = (f32[32,8,128]{2,1,0:T(8,128)S(1)}, f32[32,8,128]{2,1,0:T(8,128)S(1)}, u32[]{:S(2)}, u32[]{:S(2)}) collective-permute-start(f32[32,8,128]{2,1,0:T(8,128)S(1)} %get-tuple-element.18), channel_id=1, source_target_pairs={{1,2},{2,1},{3,4},{4,3},{5,6},{6,5},{9,10},{10,9},{11,12},{12,11},... | collective-permute-start | bytes 393224 | tf_op jit(solution)/shard_map/ppermute | solution.py:406
  9.0 9.2 %collective-permute-start.1 = (f32[32,4,128]{2,1,0:T(4,128)S(1)}, f32[32,4,128]{2,1,0:T(4,128)S(1)}, u32[]{:S(2)}, u32[]{:S(2)}) collective-permute-start(f32[32,4,128]{2,1,0:T(4,128)S(1)} %get-tuple-element.15), channel_id=1, source_target_pairs={{0,9},{1,8},{2,11},{3,10},{4,13},{5,12},{6,15},{7,14},{8,17},{9,16... | collective-permute-start | bytes 196616 | tf_op jit(solution)/shard_map/ppermute | solution.py:406
  15.6 2.6 %collective-permute-start.2 = (f32[32,4,128]{2,1,0:T(4,128)S(1)}, f32[32,4,128]{2,1,0:T(4,128)S(1)}, u32[]{:S(2)}, u32[]{:S(2)}) collective-permute-start(f32[32,4,128]{2,1,0:T(4,128)S(1)} %get-tuple-element.16), channel_id=1, source_target_pairs={{1,10},{2,9},{3,12},{4,11},{5,14},{6,13},{9,18},{10,17},{11,20},{1... | collective-permute-start | bytes 196616 | tf_op jit(solution)/shard_map/ppermute | solution.py:406
  55.9 3.0 %collective-permute-start.5 = (f32[64,40,128]{2,1,0:T(8,128)S(1)}, f32[64,40,128]{2,1,0:T(8,128)S(1)}, u32[]{:S(2)}, u32[]{:S(2)}) collective-permute-start(f32[64,40,128]{2,1,0:T(8,128)S(1)} %all_to_all.10.mine), channel_id=1, source_target_pairs={{0,8},{8,0},{1,9},{9,1},{2,10},{10,2},{3,11},{11,3},{4,12},{12,4},... | collective-permute-start | bytes 3932168 | tf_op jit(solution)/shard_map/ppermute | solution.py:429

commit v4 on v3

--- a/solution.py
+++ b/solution.py
@@ -161,46 +161,62 @@
         start_two[j] = jnp.where(even, starts[0], starts[1])[0:4]
 
 
-def residual_kernel(flag, before, initial, start_one, start_two, rim_one, rim_two, guess, forcing, a, b, d,
-                    messages, ends, coef, two, three, four, rims, one, res, edge):
+def border(sub, under, over, item, place=1, rest=0.0):
+    under = pltpu.roll(under, (place - 1 - item) % 8, 0)
+    over = pltpu.roll(over, (8 - place - item) % 8, 0)
+    return jnp.where(sub == place - 1, under, jnp.where(sub == 8 - place, over, rest))
+
+
+def prepare_kernel(flag, rim_one, rim_two, a, b, d, coef, rims, packed):
     tiles = a.shape[1] // LANES
     lane, sub = iota(1), iota(0)
-    first, even = flag[0] == 1, flag[4] == 0
-    turn = flag[3]
-    zero = jnp.zeros((8, LANES), F32)
-    for j in range(tiles):
-        edge[0, j, 0:4, :] = jnp.where(even, start_one[j], start_two[j])
-        edge[1, j, 0:4, :] = jnp.where(even, start_two[j], start_one[j])
+    even, turn = flag[4] == 0, flag[3]
     for j in range(tiles):
         low, up = jnp.where(even, rim_one[j], rim_two[j]), jnp.where(even, rim_two[j], rim_one[j])
-        start_low, start_up = edge[0, j], edge[1, j]
-
-        def border(under, over, item, place=1, rest=zero):
-            under = pltpu.roll(under, (place - 1 - item) % 8, 0)
-            over = pltpu.roll(over, (8 - place - item) % 8, 0)
-            return jnp.where(sub == place - 1, under, jnp.where(sub == 8 - place, over, rest))
-
         for r in range(4):
             values = a[tile(r), cols(j)], b[tile(r), cols(j)], d[tile(r), cols(j)]
-            put(one, j, r, jnp.where(first, initial[tile(r), cols(j)], before[tile(r), cols(j)]))
             for i, value in enumerate(rates(*values)):
                 coef[i, j, tile(r), :] = value
-        start = border(start_low, start_up, START1)
-        put(one, j, 4, border(start_low, start_up, START2, 2, start))
-        own, upper, lower, left, right = rates(*(border(low, up, item) for item in (A1, B1, D1)))
+        own, upper, lower, left, right = rates(*(border(sub, low, up, item) for item in (A1, B1, D1)))
         own = jnp.where((sub == 0) | (sub == 7), own, 0.0)
         upper = jnp.where(sub == 1, pltpu.roll(low, (1 - INWARD) % 8, 0), upper)
         lower = jnp.where(sub == 6, pltpu.roll(up, (6 - INWARD) % 8, 0), lower)
         for i, value in enumerate((own, upper, lower, left, right)):
             coef[i, j, tile(4), :] = value
-        rims[0, j] = border(start_low, start_up, STEP1, 2, border(low, up, G1))
-        rims[1, j] = border(low, up, G2) + border(start_low, start_up, STEP2, 2) + border(low, up, PART, 2)
-        rims[2, j] = border(low, up, G3)
+        rims[0, j] = border(sub, low, up, G1)
+        rims[1, j] = border(sub, low, up, PART, 2, border(sub, low, up, G2))
+        rims[2, j] = border(sub, low, up, G3)
+    which, at = lax.div(turn, 4), pl.ds(pl.multiple_of(8 * lax.rem(turn, 4), 8), 8)
+    chosen = Tiles(lambda j: jnp.where(which == 0, a[at, cols(j)], jnp.where(which == 1, b[at, cols(j)], d[at, cols(j)])))
+    for j in range(tiles):
+        x, y, z = (chosen[i % tiles] for i in (j - 1, j, j + 1))
+        packed[2 * j] = pltpu.roll(jnp.where(lane >= LANES - HALO, x, y), HALO, 1)
+        packed[2 * j + 1] = pltpu.roll(jnp.where(lane < HALO, z, y), LANES - HALO, 1)
+
+
+def residual_kernel(flag, before, initial, start_one, start_two, guess, forcing, coef, rims, packed,
+                    messages, ends, two, three, four, one, res, edge, begin):
+    tiles = guess.shape[1] // LANES
+    lane, sub = iota(1), iota(0)
+    first, even = flag[0] == 1, flag[4] == 0
+    for j in range(tiles):
+        edge[0, j, 0:4, :] = jnp.where(even, start_one[j], start_two[j])
+        edge[1, j, 0:4, :] = jnp.where(even, start_two[j], start_one[j])
+        for i in (2 * j, 2 * j + 1):
+            messages[i, tile(4), :] = packed[i]
+    for j in range(tiles):
+        low, up = edge[0, j], edge[1, j]
+        for r in range(4):
+            put(one, j, r, jnp.where(first, initial[tile(r), cols(j)], before[tile(r), cols(j)]))
+        put(one, j, 4, border(sub, low, up, START2, 2, border(sub, low, up, START1)))
+        begin[0, j] = border(sub, low, up, STEP1, 2, rims[0, j])
+        begin[1, j] = rims[1, j] + border(sub, low, up, STEP2, 2)
+        begin[2, j] = rims[2, j]
 
     for inner, (source, target) in enumerate([(one, two), (two, three), (three, four)]):
 
         def fine(j, r, value, _, inner=inner, target=target):
-            put(target, j, r, value + (forcing[inner, tile(r), cols(j)] if r < 4 else rims[inner, j]))
+            put(target, j, r, value + (forcing[inner, tile(r), cols(j)] if r < 4 else begin[inner, j]))
 
         sweep(source, coef, range(5), fine)
 
@@ -216,15 +232,6 @@
             x, y, z = (res[i % tiles, tile(r), :] for i in (j - 1, j, j + 1))
             messages[2 * j, tile(r), :] = pltpu.roll(jnp.where(lane >= LANES - HALO, x, y), HALO, 1)
             messages[2 * j + 1, tile(r), :] = pltpu.roll(jnp.where(lane < HALO, z, y), LANES - HALO, 1)
-
-    which, at = lax.div(turn, 4), pl.ds(pl.multiple_of(8 * lax.rem(turn, 4), 8), 8)
-    for j in range(tiles):
-        x, y, z = (
-            jnp.where(which == 0, a[at, cols(i % tiles)], jnp.where(which == 1, b[at, cols(i % tiles)], d[at, cols(i % tiles)]))
-            for i in (j - 1, j, j + 1)
-        )
-        messages[2 * j, tile(4), :] = pltpu.roll(jnp.where(lane >= LANES - HALO, x, y), HALO, 1)
-        messages[2 * j + 1, tile(4), :] = pltpu.roll(jnp.where(lane < HALO, z, y), LANES - HALO, 1)
 
 
 def chain_kernel(flag, mine, other, messages, coef, one, two):
@@ -410,20 +417,28 @@
 
     field = pltpu.VMEM((tiles, 48, LANES), F32)
     tall = shaped(tiles, 48, LANES)
-    messages, ends, coef, *fields = pl.pallas_call(
+    coef, rims, packed = pl.pallas_call(
+        prepare_kernel,
+        in_specs=[SMEM] + [VMEM] * 5,
+        out_specs=[VMEM] * 3,
+        out_shape=[shaped(5, tiles, 40, LANES), shaped(3, tiles, 8, LANES), shaped(2 * tiles, 8, LANES)],
+        compiler_params=params(20),
+        name="prepare",
+    )(flag, rim_one, rim_two, courant_rows, courant_cols, diffusion)
+    messages, ends, *fields = pl.pallas_call(
         residual_kernel,
-        in_specs=[SMEM] + [VMEM] * 11,
-        out_specs=[VMEM] * 6,
-        out_shape=[shaped(2 * tiles, 40, LANES), shaped(tiles, ROWS, LANES), shaped(5, tiles, 40, LANES), tall, tall, tall],
+        in_specs=[SMEM] + [VMEM] * 9,
+        out_specs=[VMEM] * 5,
+        out_shape=[shaped(2 * tiles, 40, LANES), shaped(tiles, ROWS, LANES), tall, tall, tall],
         scratch_shapes=[
-            pltpu.VMEM((3, tiles, 8, LANES), F32),
             field,
             pltpu.VMEM((tiles, ROWS, LANES), F32),
             pltpu.VMEM((2, tiles, 8, LANES), F32),
+            pltpu.VMEM((3, tiles, 8, LANES), F32),
         ],
         compiler_params=params(20),
         name="residual",
-    )(flag, before, initial, start_one, start_two, rim_one, rim_two, last, forcing, courant_rows, courant_cols, diffusion)
+    )(flag, before, initial, start_one, start_two, last, forcing, coef, rims, packed)
 
     mine = lax.all_to_all(messages, ("chip", "space"), 0, 0, tiled=True)
     other = lax.ppermute(mine, "core", [(0, 1), (1, 0)])

time: 86.6 us -> 86.4 us (level)
  waiting for transfers between devices: 5.03 us -> 3.96 us
    ppermute x4, waiting for transfers between devices: 1.99 us -> 0.92 us  [exchanged(): return lax.ppermute(value, everything, pairs)]
    pallas_call x1 -> x2, Pallas kernels: 2.99 us -> 3.51 us  [the longest x1 2.47 us: on_device(): pl.pallas_call(residual_kernel, in_specs=[SMEM] + [VMEM] * 9, out_specs=[...]
  transfers between devices with their start and end apart: 6 -> 6, of which waited for: 2 -> 2; matrix products, arithmetic and copies ran while one was open for 0% -> 0% of each run, Pallas kernels for 4% -> 5%
where the time goes in v4:
time: 86.4 us; the launch traced here: 86.2 us
  blocking collectives  56.1 us (65%)
  Pallas kernels  14.1 us (16%)
  starting transfers between devices  11.7 us (14%)
  waiting for transfers between devices  3.96 us (5%)
    all_to_all x1, blocking collectives, on_device(): mine = lax.all_to_all(messages, ('chip', 'space'), 0, 0, tiled=True)  34.9 us
    all_to_all x1, blocking collectives, on_device(): returned = lax.all_to_all(answer, ('chip', 'space'), 0, 0, tiled=True)  21.2 us
    ppermute x4, starting transfers between devices, exchanged(): return lax.ppermute(value, everything, pairs)  10.4 us
    pallas_call x1, Pallas kernels, on_device(): pl.pallas_call(chain_kernel, in_specs=[SMEM, VMEM, VMEM], out_specs=VMEM,...  3.72 us
    pallas_call x1, Pallas kernels, on_device(): pl.pallas_call(rim_kernel, in_specs=[SMEM] + [ANY] * 6, out_specs=[VMEM]...  3.18 us
    ppermute x1, waiting for transfers between devices, on_device(): other = lax.ppermute(mine, 'core', [(0, 1), (1, 0)])  3.03 us
    pallas_call x1, Pallas kernels, on_device(): pl.pallas_call(final_kernel, in_specs=[VMEM] * 6, out_specs=ANY, out_shap...  2.54 us
    pallas_call x1, Pallas kernels, on_device(): pl.pallas_call(residual_kernel, in_specs=[SMEM] + [VMEM] * 9, out_specs=[...  2.47 us
  transfers between devices with their start and end apart: 6, of which 2 were waited for; matrix products, arithmetic and copies ran while one was open for 0% of the time, Pallas kernels for 5%

profile of v4, /device:TPU:0, one launch (start us, length us, event | category | flops | bytes accessed | tf_op | source)
XLA Modules:
  0.0 86.2 jit_solution(13457626231174653453)
XLA Ops:
  0.0 0.0 copy-start.2
  0.0 0.0 copy-start.1
  0.0 0.0 copy-start.4
  0.0 1.2 %last.1.guess = f32[32,4096]{1,0:T(8,128)S(1)} custom-call(f32[4,32,4096]{2,1,0:T(8,128)} %guess.3), custom_call_target="tpu_custom_call" | custom-call | tf_op jit(solution)/shard_map/last/pallas_call | solution.py:374
  1.2 1.3 %collective-permute-start.2 = (f32[32,4096]{1,0:T(8,128)S(1)}, f32[32,4096]{1,0:T(8,128)S(1)}, u32[]{:S(2)}, u32[]{:S(2)}) collective-permute-start(f32[32,4096]{1,0:T(8,128)S(1)} %last.1.guess), channel_id=1, source_target_pairs={{0,8},{8,16},{16,24},{24,32},{32,40},{40,48},{48,56},{56,64},{64,7... | collective-permute-start | bytes 1572872 | tf_op jit(solution)/shard_map/ppermute | solution.py:383
  2.5 0.1 stack.31.flag
  2.6 0.0 copy-done.2
  2.6 0.0 copy-done.1
  2.6 0.0 copy-done.4
  2.6 0.0 copy-start.3
  2.6 0.0 copy-start
  2.6 3.2 %rim.1 = (f32[32,8,128]{2,1,0:T(8,128)S(1)}, f32[32,8,128]{2,1,0:T(8,128)S(1)}, f32[32,4,128]{2,1,0:T(4,128)S(1)}, f32[32,4,128]{2,1,0:T(4,128)S(1)}) custom-call(s32[5]{0:T(128)S(1)} %stack.31.flag, f32[4,32,4096]{2,1,0:T(8,128)} %guess.3, f32[32,4096]{1,0:T(8,128)S(1)} %copy-done.4, f32[32,4096]{1,0:T(8,128)S(1)} %copy-done.1, f32[32,4096]{1,0:T(8,128)S(1)} %copy-done.2, ...), custom_call_target="tpu_custom_call" | custom-call | tf_op jit(solution)/shard_map/rim/pallas_call | solution.py:386
  5.8 2.5 %collective-permute-start = (f32[32,8,128]{2,1,0:T(8,128)S(1)}, f32[32,8,128]{2,1,0:T(8,128)S(1)}, u32[]{:S(2)}, u32[]{:S(2)}) collective-permute-start(f32[32,8,128]{2,1,0:T(8,128)S(1)} %get-tuple-element.17), channel_id=1, source_target_pairs={{0,1},{1,0},{2,3},{3,2},{4,5},{5,4},{6,7},{7,6},{8,9},{9,8},{10,11... | collective-permute-start | bytes 393224 | tf_op jit(solution)/shard_map/ppermute | solution.py:413
  8.4 0.7 collective-permute-start.1
  9.0 6.5 %collective-permute-start.3 = (f32[32,4,128]{2,1,0:T(4,128)S(1)}, f32[32,4,128]{2,1,0:T(4,128)S(1)}, u32[]{:S(2)}, u32[]{:S(2)}) collective-permute-start(f32[32,4,128]{2,1,0:T(4,128)S(1)} %get-tuple-element.20), channel_id=1, source_target_pairs={{0,9},{1,8},{2,11},{3,10},{4,13},{5,12},{6,15},{7,14},{8,17},{9,16... | collective-permute-start | bytes 196616 | tf_op jit(solution)/shard_map/ppermute | solution.py:413
  15.6 0.7 collective-permute-start.4
  16.2 0.0 collective-permute-done.rim_one
  16.2 0.0 collective-permute-done.1.rim_two
  16.3 0.0 copy-done.3
  16.3 1.0 %prepare.1 = (f32[5,32,40,128]{3,2,1,0:T(8,128)S(1)}, f32[3,32,8,128]{3,2,1,0:T(8,128)S(1)}, f32[64,8,128]{2,1,0:T(8,128)S(1)}) custom-call(s32[5]{0:T(128)S(1)} %stack.31.flag, f32[32,8,128]{2,1,0:T(8,128)S(1)} %collective-permute-done.rim_one, f32[32,8,128]{2,1,0:T(8,128)S(1)} %collective-permute-done.1.rim_two, f32[32,4096]{1,0:T(8,128)S(1)} %copy-done.1, ...), custom_call_target="tpu_custom_call" | custom-call | tf_op jit(solution)/shard_map/prepare/pallas_call | solution.py:420
  17.3 0.9 %collective-permute-done.3.start_one = f32[32,4,128]{2,1,0:T(4,128)S(1)} collective-permute-done((f32[32,4,128]{2,1,0:T(4,128)S(1)}, f32[32,4,128]{2,1,0:T(4,128)S(1)}, u32[]{:S(2)}, u32[]{:S(2)}) %collective-permute-start.3) | collective-permute-done | bytes 65568 | tf_op jit(solution)/shard_map/ppermute | solution.py:413
  18.2 0.0 collective-permute-done.4.start_two
  18.2 0.0 collective-permute-done.2.before
  18.2 0.0 copy-done
  18.2 2.5 %residual.1 = (f32[64,40,128]{2,1,0:T(8,128)S(1)}, f32[32,32,128]{2,1,0:T(8,128)S(1)}, f32[32,48,128]{2,1,0:T(8,128)S(1)}, f32[32,48,128]{2,1,0:T(8,128)S(1)}, f32[32,48,128]{2,1,0:T(8,128)S(1)}) custom-call(s32[5]{0:T(128)S(1)} %stack.31.flag, f32[32,4096]{1,0:T(8,128)S(1)} %collective-permute-done.2.before, f32[32,4096]{1,0:T(8,128)S(1)} %copy-done.4, ...), custom_call_target="tpu_custom_call" | custom-call | tf_op jit(solution)/shard_map/residual/pallas_call | solution.py:428
  20.7 34.9 %all_to_all.10.mine = f32[64,40,128]{2,1,0:T(8,128)S(1)} all-to-all(f32[64,40,128]{2,1,0:T(8,128)S(1)} %get-tuple-element.28), channel_id=1, replica_groups=mesh['chip'=8,'core'=2,'space'=8] {'chip','space'}, dimensions={0} | all-to-all | bytes 2621440 | tf_op jit(solution)/shard_map/all_to_all | solution.py:443
  55.6 0.0 collective-permute-start.5
  55.6 3.0 %collective-permute-done.5.other = f32[64,40,128]{2,1,0:T(8,128)S(1)} collective-permute-done((f32[64,40,128]{2,1,0:T(8,128)S(1)}, f32[64,40,128]{2,1,0:T(8,128)S(1)}, u32[]{:S(2)}, u32[]{:S(2)}) %collective-permute-start.5) | collective-permute-done | bytes 1310752 | tf_op jit(solution)/shard_map/ppermute | solution.py:444
  58.7 3.7 %chain.1 = f32[64,24,128]{2,1,0:T(8,128)S(1)} custom-call(s32[5]{0:T(128)S(1)} %stack.31.flag, f32[64,40,128]{2,1,0:T(8,128)S(1)} %all_to_all.10.mine, f32[64,40,128]{2,1,0:T(8,128)S(1)} %collective-permute-done.5.other), custom_call_target="tpu_custom_call" | custom-call | tf_op jit(solution)/shard_map/chain/pallas_call | solution.py:446
  62.4 21.2 %all_to_all.11.returned = f32[64,24,128]{2,1,0:T(8,128)S(1)} all-to-all(f32[64,24,128]{2,1,0:T(8,128)S(1)} %chain.1), channel_id=1, replica_groups=mesh['chip'=8,'core'=2,'space'=8] {'chip','space'}, dimensions={0} | all-to-all | bytes 1572864 | tf_op jit(solution)/shard_map/all_to_all | solution.py:459
  83.6 2.5 %final.1 = f32[4,32,4096]{2,1,0:T(8,128)} custom-call(f32[5,32,40,128]{3,2,1,0:T(8,128)S(1)} %get-tuple-element.19.coef, f32[32,48,128]{2,1,0:T(8,128)S(1)} %get-tuple-element.24.first, f32[32,48,128]{2,1,0:T(8,128)S(1)} %get-tuple-element.25.second, f32[32,48,128]{2,1,0:T(8,128)S(1)} %get-tuple-element.26.third, f32[32,32,128]{2,1,0:T(8,128)S(1)} %get-tuple-element.27.ends, ...), custom_call_target="tpu_custom_call" | custom-call | tf_op jit(solution)/shard_map/final/pallas_call | solution.py:460
Async XLA Ops:
  0.0 2.6 %copy-start.2 = (f32[32,4096]{1,0:T(8,128)S(1)}, f32[32,4096]{1,0:T(8,128)}, u32[]{:S(2)}) copy-start(f32[32,4096]{1,0:T(8,128)} %b.3) | copy-start | bytes 1572868
  0.0 2.6 %copy-start.1 = (f32[32,4096]{1,0:T(8,128)S(1)}, f32[32,4096]{1,0:T(8,128)}, u32[]{:S(2)}) copy-start(f32[32,4096]{1,0:T(8,128)} %a.3) | copy-start | bytes 1572868
  0.0 2.6 %copy-start.4 = (f32[32,4096]{1,0:T(8,128)S(1)}, f32[32,4096]{1,0:T(8,128)}, u32[]{:S(2)}) copy-start(f32[32,4096]{1,0:T(8,128)} %initial.3) | copy-start | bytes 1572868
  1.2 17.0 %collective-permute-start.2 = (f32[32,4096]{1,0:T(8,128)S(1)}, f32[32,4096]{1,0:T(8,128)S(1)}, u32[]{:S(2)}, u32[]{:S(2)}) collective-permute-start(f32[32,4096]{1,0:T(8,128)S(1)} %last.1.guess), channel_id=1, source_target_pairs={{0,8},{8,16},{16,24},{24,32},{32,40},{40,48},{48,56},{56,64},{64,7... | collective-permute-start | bytes 1572872 | tf_op jit(solution)/shard_map/ppermute | solution.py:383
  2.6 13.6 %copy-start.3 = (f32[32,4096]{1,0:T(8,128)S(1)}, f32[32,4096]{1,0:T(8,128)}, u32[]{:S(2)}) copy-start(f32[32,4096]{1,0:T(8,128)} %d.3) | copy-start | bytes 1572868
  2.6 15.6 %copy-start = (f32[4,32,4096]{2,1,0:T(8,128)S(1)}, f32[4,32,4096]{2,1,0:T(8,128)}, u32[]{:S(2)}) copy-start(f32[4,32,4096]{2,1,0:T(8,128)} %forcing.3) | copy-start | bytes 6291460
  5.8 10.4 %collective-permute-start = (f32[32,8,128]{2,1,0:T(8,128)S(1)}, f32[32,8,128]{2,1,0:T(8,128)S(1)}, u32[]{:S(2)}, u32[]{:S(2)}) collective-permute-start(f32[32,8,128]{2,1,0:T(8,128)S(1)} %get-tuple-element.17), channel_id=1, source_target_pairs={{0,1},{1,0},{2,3},{3,2},{4,5},{5,4},{6,7},{7,6},{8,9},{9,8},{10,11... | collective-permute-start | bytes 393224 | tf_op jit(solution)/shard_map/ppermute | solution.py:413
  8.4 7.9 %collective-permute-start.1 = (f32[32,8,128]{2,1,0:T(8,128)S(1)}, f32[32,8,128]{2,1,0:T(8,128)S(1)}, u32[]{:S(2)}, u32[]{:S(2)}) collective-permute-start(f32[32,8,128]{2,1,0:T(8,128)S(1)} %get-tuple-element.18), channel_id=1, source_target_pairs={{1,2},{2,1},{3,4},{4,3},{5,6},{6,5},{9,10},{10,9},{11,12},{12,11},... | collective-permute-start | bytes 393224 | tf_op jit(solution)/shard_map/ppermute | solution.py:413
  9.0 9.2 %collective-permute-start.3 = (f32[32,4,128]{2,1,0:T(4,128)S(1)}, f32[32,4,128]{2,1,0:T(4,128)S(1)}, u32[]{:S(2)}, u32[]{:S(2)}) collective-permute-start(f32[32,4,128]{2,1,0:T(4,128)S(1)} %get-tuple-element.20), channel_id=1, source_target_pairs={{0,9},{1,8},{2,11},{3,10},{4,13},{5,12},{6,15},{7,14},{8,17},{9,16... | collective-permute-start | bytes 196616 | tf_op jit(solution)/shard_map/ppermute | solution.py:413
  15.6 2.6 %collective-permute-start.4 = (f32[32,4,128]{2,1,0:T(4,128)S(1)}, f32[32,4,128]{2,1,0:T(4,128)S(1)}, u32[]{:S(2)}, u32[]{:S(2)}) collective-permute-start(f32[32,4,128]{2,1,0:T(4,128)S(1)} %get-tuple-element.21), channel_id=1, source_target_pairs={{1,10},{2,9},{3,12},{4,11},{5,14},{6,13},{9,18},{10,17},{11,20},{1... | collective-permute-start | bytes 196616 | tf_op jit(solution)/shard_map/ppermute | solution.py:413
  55.6 3.0 %collective-permute-start.5 = (f32[64,40,128]{2,1,0:T(8,128)S(1)}, f32[64,40,128]{2,1,0:T(8,128)S(1)}, u32[]{:S(2)}, u32[]{:S(2)}) collective-permute-start(f32[64,40,128]{2,1,0:T(8,128)S(1)} %all_to_all.10.mine), channel_id=1, source_target_pairs={{0,8},{8,0},{1,9},{9,1},{2,10},{10,2},{3,11},{11,3},{4,12},{12,4},... | collective-permute-start | bytes 3932168 | tf_op jit(solution)/shard_map/ppermute | solution.py:444

commit v5 on v4

--- a/solution.py
+++ b/solution.py
@@ -88,28 +88,24 @@
         return self.seen[j]
 
 
-def rim_kernel(flag, guess, initial, a, b, d, forcing, rim_one, rim_two, start_one, start_two,
-               va, vi, vg, vc, coef, field, part, after, sems):
+def rim_kernel(flag, last, initial, a, b, d, forcing, rim_one, rim_two, start_one, start_two,
+               vg, coef, field, part, after, sems):
     rows, columns = a.shape
     tiles = columns // LANES
     sub, lane = iota(0), iota(1)
     copies = []
-    for side in range(2):
-        at = pl.ds(0 if side == 0 else rows - 8, 8)
-        moves = [(x.at[at, :], vc.at[i, side]) for i, x in enumerate((a, b, d))]
-        moves += [(forcing.at[i, at, :], vg.at[i, side]) for i in range(3)]
-        moves += [(guess.at[3, at, :], va.at[side]), (initial.at[at, :], vi.at[side])]
-        for source, target in moves:
+    for side, at in enumerate((pl.ds(0, 8), pl.ds(rows - 8, 8))):
+        for i in range(3):
+            source, target = forcing.at[i, at, :], vg.at[i, pl.ds(8 * side, 8), :]
             copies.append(pltpu.make_async_copy(source, target, sems.at[len(copies)]))
     for copy in copies:
         copy.start()
-    for copy in copies:
-        copy.wait()
     at_end, even = flag[2] == 1, flag[4] == 0
     top = sub < 4
 
     def both(ref, j):
-        return jnp.where(top, ref[0, :, cols(j)], ref[1, :, cols(j)])
+        end = ref.shape[0]
+        return jnp.where(top, ref[0:8, cols(j)], ref[end - 8 : end, cols(j)])
 
     def outward(x):
         return jnp.where(top, pltpu.roll(x, 7, 0), pltpu.roll(x, 1, 0))
@@ -131,19 +127,21 @@
         return total + (coef[LEFT, j] * left + coef[RIGHT, j] * right)
 
     for j in range(tiles):
-        own, upper, lower, left, right = rates(*(both(vc.at[n], j) for n in range(3)))
+        own, upper, lower, left, right = rates(*(both(x, j) for x in (a, b, d)))
         coef[OWN, j], coef[LEFT, j], coef[RIGHT, j] = own, left, right
         coef[OUT, j], coef[IN, j] = jnp.where(top, lower, upper), jnp.where(top, upper, lower)
-        field[j] = jnp.where(at_end, both(vi, j), both(va, j))
+        field[j] = jnp.where(at_end, both(initial, j), both(last, j))
     values = Tiles(lambda j: field[j])
     for j in range(tiles):
         part[j] = open_step(values, j)
         after[j] = part[j] + coef[IN, j] * inward(values[j])
+    for copy in copies:
+        copy.wait()
     forced, stepped = Tiles(lambda j: both(vg.at[0], j)), Tiles(lambda j: after[j])
     for j in range(tiles):
         g1, g2, g3 = forced[j], both(vg.at[1], j), both(vg.at[2], j)
         items = [(G1, g1, 1), (G2, g2 + coef[OUT, j] * outward(g1), 1), (G3, g3, 1), (PART, open_step(forced, j) + g2, 2)]
-        items += [(A1 + i, both(vc.at[i], j), 1) for i in range(3)]
+        items += [(A1 + i, both(x, j), 1) for i, x in enumerate((a, b, d))]
         items += [(INWARD, coef[IN, j], 2)]
         values, second = field[j], open_step(stepped, j)
         begins = [(START1, values, 1), (START2, values, 2), (STEP1, part[j], 2), (STEP2, second, 2)]
@@ -382,26 +380,16 @@
     )(guess)
     before = lax.ppermute(last, ("chip", "core"), [(i, i + 1) for i in range(owners - 1)])
     small = pltpu.VMEM((tiles, 8, LANES), F32)
-    edge_rows = pltpu.VMEM((2, 8, columns), F32)
     rim_one, rim_two, start_one, start_two = pl.pallas_call(
         rim_kernel,
-        in_specs=[SMEM] + [ANY] * 6,
+        in_specs=[SMEM] + [VMEM] * 5 + [ANY],
         out_specs=[VMEM] * 4,
         out_shape=[shaped(tiles, 8, LANES), shaped(tiles, 8, LANES), shaped(tiles, 4, LANES), shaped(tiles, 4, LANES)],
-        scratch_shapes=[
-            edge_rows,
-            edge_rows,
-            pltpu.VMEM((3, 2, 8, columns), F32),
-            pltpu.VMEM((3, 2, 8, columns), F32),
-            pltpu.VMEM((5, tiles, 8, LANES), F32),
-            small,
-            small,
-            small,
-            pltpu.SemaphoreType.DMA((16,)),
-        ],
+        scratch_shapes=[pltpu.VMEM((3, 16, columns), F32), pltpu.VMEM((5, tiles, 8, LANES), F32), small, small, small,
+                        pltpu.SemaphoreType.DMA((6,))],
         compiler_params=params(52),
         name="rim",
-    )(flag, guess, initial, courant_rows, courant_cols, diffusion, forcing)
+    )(flag, last, initial, courant_rows, courant_cols, diffusion, forcing)
 
     def exchanged(value, by_turn, first):
         pairs = []

time: 86.4 us -> 86.4 us (level)
  no operation moved by 1% of the time
where the time goes in v5:
time: 86.4 us; the launch traced here: 86.1 us
  blocking collectives  56.4 us (65%)
  Pallas kernels  13.9 us (16%)
  starting transfers between devices  11.7 us (14%)
  waiting for transfers between devices  3.95 us (5%)
    all_to_all x1, blocking collectives, on_device(): mine = lax.all_to_all(messages, ('chip', 'space'), 0, 0, tiled=True)  35.1 us
    all_to_all x1, blocking collectives, on_device(): returned = lax.all_to_all(answer, ('chip', 'space'), 0, 0, tiled=True)  21.2 us
    ppermute x4, starting transfers between devices, exchanged(): return lax.ppermute(value, everything, pairs)  10.4 us
    pallas_call x1, Pallas kernels, on_device(): pl.pallas_call(chain_kernel, in_specs=[SMEM, VMEM, VMEM], out_specs=VMEM,...  3.72 us
    ppermute x1, waiting for transfers between devices, on_device(): other = lax.ppermute(mine, 'core', [(0, 1), (1, 0)])  3.03 us
    pallas_call x1, Pallas kernels, on_device(): pl.pallas_call(rim_kernel, in_specs=[SMEM] + [VMEM] * 5 + [ANY], out_spec...  2.97 us
    pallas_call x1, Pallas kernels, on_device(): pl.pallas_call(final_kernel, in_specs=[VMEM] * 6, out_specs=ANY, out_shap...  2.54 us
    pallas_call x1, Pallas kernels, on_device(): pl.pallas_call(residual_kernel, in_specs=[SMEM] + [VMEM] * 9, out_specs=[...  2.47 us
  transfers between devices with their start and end apart: 6, of which 2 were waited for; matrix products, arithmetic and copies ran while one was open for 0% of the time, Pallas kernels for 5%

profile of v5, /device:TPU:0, one launch (start us, length us, event | category | flops | bytes accessed | tf_op | source)
XLA Modules:
  0.0 86.1 jit_solution(16193804963655000391)
XLA Ops:
  0.0 0.0 copy-start.1
  0.0 0.0 copy-start.4
  0.0 1.1 %last.1.guess = f32[32,4096]{1,0:T(8,128)S(1)} custom-call(f32[4,32,4096]{2,1,0:T(8,128)} %guess.1), custom_call_target="tpu_custom_call" | custom-call | tf_op jit(solution)/shard_map/last/pallas_call | solution.py:372
  1.1 1.3 %collective-permute-start.2 = (f32[32,4096]{1,0:T(8,128)S(1)}, f32[32,4096]{1,0:T(8,128)S(1)}, u32[]{:S(2)}, u32[]{:S(2)}) collective-permute-start(f32[32,4096]{1,0:T(8,128)S(1)} %last.1.guess), channel_id=1, source_target_pairs={{0,8},{8,16},{16,24},{24,32},{32,40},{40,48},{48,56},{56,64},{64,7... | collective-permute-start | bytes 1572872 | tf_op jit(solution)/shard_map/ppermute | solution.py:381
  2.5 0.1 stack.31.flag
  2.6 0.0 copy-done.1
  2.6 0.0 copy-done.4
  2.6 0.0 copy-start.2
  2.6 0.0 copy-start.3
  2.6 0.0 copy-start
  2.6 3.0 %rim.1 = (f32[32,8,128]{2,1,0:T(8,128)S(1)}, f32[32,8,128]{2,1,0:T(8,128)S(1)}, f32[32,4,128]{2,1,0:T(4,128)S(1)}, f32[32,4,128]{2,1,0:T(4,128)S(1)}) custom-call(s32[5]{0:T(128)S(1)} %stack.31.flag, f32[32,4096]{1,0:T(8,128)S(1)} %last.1.guess, f32[32,4096]{1,0:T(8,128)S(1)} %copy-done.4, f32[32,4096]{1,0:T(8,128)S(1)} %copy-done.1, f32[32,4096]{1,0:T(8,128)} %b.3, ...), custom_call_target="tpu_custom_call" | custom-call | tf_op jit(solution)/shard_map/rim/pallas_call | solution.py:383
  5.6 2.5 %collective-permute-start = (f32[32,8,128]{2,1,0:T(8,128)S(1)}, f32[32,8,128]{2,1,0:T(8,128)S(1)}, u32[]{:S(2)}, u32[]{:S(2)}) collective-permute-start(f32[32,8,128]{2,1,0:T(8,128)S(1)} %get-tuple-element.17), channel_id=1, source_target_pairs={{0,1},{1,0},{2,3},{3,2},{4,5},{5,4},{6,7},{7,6},{8,9},{9,8},{10,11... | collective-permute-start | bytes 393224 | tf_op jit(solution)/shard_map/ppermute | solution.py:401
  8.1 0.7 collective-permute-start.1
  8.8 6.5 %collective-permute-start.3 = (f32[32,4,128]{2,1,0:T(4,128)S(1)}, f32[32,4,128]{2,1,0:T(4,128)S(1)}, u32[]{:S(2)}, u32[]{:S(2)}) collective-permute-start(f32[32,4,128]{2,1,0:T(4,128)S(1)} %get-tuple-element.20), channel_id=1, source_target_pairs={{0,9},{1,8},{2,11},{3,10},{4,13},{5,12},{6,15},{7,14},{8,17},{9,16... | collective-permute-start | bytes 196616 | tf_op jit(solution)/shard_map/ppermute | solution.py:401
  15.3 0.7 collective-permute-start.4
  16.0 0.0 collective-permute-done.rim_one
  16.0 0.0 collective-permute-done.1.rim_two
  16.0 0.0 copy-done.2
  16.0 0.0 copy-done.3
  16.0 1.0 %prepare.1 = (f32[5,32,40,128]{3,2,1,0:T(8,128)S(1)}, f32[3,32,8,128]{3,2,1,0:T(8,128)S(1)}, f32[64,8,128]{2,1,0:T(8,128)S(1)}) custom-call(s32[5]{0:T(128)S(1)} %stack.31.flag, f32[32,8,128]{2,1,0:T(8,128)S(1)} %collective-permute-done.rim_one, f32[32,8,128]{2,1,0:T(8,128)S(1)} %collective-permute-done.1.rim_two, f32[32,4096]{1,0:T(8,128)S(1)} %copy-done.1, ...), custom_call_target="tpu_custom_call" | custom-call | tf_op jit(solution)/shard_map/prepare/pallas_call | solution.py:408
  17.1 0.9 %collective-permute-done.3.start_one = f32[32,4,128]{2,1,0:T(4,128)S(1)} collective-permute-done((f32[32,4,128]{2,1,0:T(4,128)S(1)}, f32[32,4,128]{2,1,0:T(4,128)S(1)}, u32[]{:S(2)}, u32[]{:S(2)}) %collective-permute-start.3) | collective-permute-done | bytes 65568 | tf_op jit(solution)/shard_map/ppermute | solution.py:401
  18.0 0.0 collective-permute-done.4.start_two
  18.0 0.0 collective-permute-done.2.before
  18.0 0.0 copy-done
  18.0 2.5 %residual.1 = (f32[64,40,128]{2,1,0:T(8,128)S(1)}, f32[32,32,128]{2,1,0:T(8,128)S(1)}, f32[32,48,128]{2,1,0:T(8,128)S(1)}, f32[32,48,128]{2,1,0:T(8,128)S(1)}, f32[32,48,128]{2,1,0:T(8,128)S(1)}) custom-call(s32[5]{0:T(128)S(1)} %stack.31.flag, f32[32,4096]{1,0:T(8,128)S(1)} %collective-permute-done.2.before, f32[32,4096]{1,0:T(8,128)S(1)} %copy-done.4, ...), custom_call_target="tpu_custom_call" | custom-call | tf_op jit(solution)/shard_map/residual/pallas_call | solution.py:416
  20.5 35.1 %all_to_all.10.mine = f32[64,40,128]{2,1,0:T(8,128)S(1)} all-to-all(f32[64,40,128]{2,1,0:T(8,128)S(1)} %get-tuple-element.28), channel_id=1, replica_groups=mesh['chip'=8,'core'=2,'space'=8] {'chip','space'}, dimensions={0} | all-to-all | bytes 2621440 | tf_op jit(solution)/shard_map/all_to_all | solution.py:431
  55.6 0.0 collective-permute-start.5
  55.6 3.0 %collective-permute-done.5.other = f32[64,40,128]{2,1,0:T(8,128)S(1)} collective-permute-done((f32[64,40,128]{2,1,0:T(8,128)S(1)}, f32[64,40,128]{2,1,0:T(8,128)S(1)}, u32[]{:S(2)}, u32[]{:S(2)}) %collective-permute-start.5) | collective-permute-done | bytes 1310752 | tf_op jit(solution)/shard_map/ppermute | solution.py:432
  58.6 3.7 %chain.1 = f32[64,24,128]{2,1,0:T(8,128)S(1)} custom-call(s32[5]{0:T(128)S(1)} %stack.31.flag, f32[64,40,128]{2,1,0:T(8,128)S(1)} %all_to_all.10.mine, f32[64,40,128]{2,1,0:T(8,128)S(1)} %collective-permute-done.5.other), custom_call_target="tpu_custom_call" | custom-call | tf_op jit(solution)/shard_map/chain/pallas_call | solution.py:434
  62.4 21.2 %all_to_all.11.returned = f32[64,24,128]{2,1,0:T(8,128)S(1)} all-to-all(f32[64,24,128]{2,1,0:T(8,128)S(1)} %chain.1), channel_id=1, replica_groups=mesh['chip'=8,'core'=2,'space'=8] {'chip','space'}, dimensions={0} | all-to-all | bytes 1572864 | tf_op jit(solution)/shard_map/all_to_all | solution.py:447
  83.6 2.5 %final.1 = f32[4,32,4096]{2,1,0:T(8,128)} custom-call(f32[5,32,40,128]{3,2,1,0:T(8,128)S(1)} %get-tuple-element.19.coef, f32[32,48,128]{2,1,0:T(8,128)S(1)} %get-tuple-element.24.first, f32[32,48,128]{2,1,0:T(8,128)S(1)} %get-tuple-element.25.second, f32[32,48,128]{2,1,0:T(8,128)S(1)} %get-tuple-element.26.third, f32[32,32,128]{2,1,0:T(8,128)S(1)} %get-tuple-element.27.ends, ...), custom_call_target="tpu_custom_call" | custom-call | tf_op jit(solution)/shard_map/final/pallas_call | solution.py:448
Async XLA Ops:
  0.0 2.6 %copy-start.1 = (f32[32,4096]{1,0:T(8,128)S(1)}, f32[32,4096]{1,0:T(8,128)}, u32[]{:S(2)}) copy-start(f32[32,4096]{1,0:T(8,128)} %a.3) | copy-start | bytes 1572868
  0.0 2.6 %copy-start.4 = (f32[32,4096]{1,0:T(8,128)S(1)}, f32[32,4096]{1,0:T(8,128)}, u32[]{:S(2)}) copy-start(f32[32,4096]{1,0:T(8,128)} %initial.3) | copy-start | bytes 1572868
  1.1 16.8 %collective-permute-start.2 = (f32[32,4096]{1,0:T(8,128)S(1)}, f32[32,4096]{1,0:T(8,128)S(1)}, u32[]{:S(2)}, u32[]{:S(2)}) collective-permute-start(f32[32,4096]{1,0:T(8,128)S(1)} %last.1.guess), channel_id=1, source_target_pairs={{0,8},{8,16},{16,24},{24,32},{32,40},{40,48},{48,56},{56,64},{64,7... | collective-permute-start | bytes 1572872 | tf_op jit(solution)/shard_map/ppermute | solution.py:381
  2.6 13.4 %copy-start.2 = (f32[32,4096]{1,0:T(8,128)S(1)}, f32[32,4096]{1,0:T(8,128)}, u32[]{:S(2)}) copy-start(f32[32,4096]{1,0:T(8,128)} %b.3) | copy-start | bytes 1572868
  2.6 13.4 %copy-start.3 = (f32[32,4096]{1,0:T(8,128)S(1)}, f32[32,4096]{1,0:T(8,128)}, u32[]{:S(2)}) copy-start(f32[32,4096]{1,0:T(8,128)} %d.3) | copy-start | bytes 1572868
  2.6 15.4 %copy-start = (f32[4,32,4096]{2,1,0:T(8,128)S(1)}, f32[4,32,4096]{2,1,0:T(8,128)}, u32[]{:S(2)}) copy-start(f32[4,32,4096]{2,1,0:T(8,128)} %forcing.3) | copy-start | bytes 6291460
  5.6 10.4 %collective-permute-start = (f32[32,8,128]{2,1,0:T(8,128)S(1)}, f32[32,8,128]{2,1,0:T(8,128)S(1)}, u32[]{:S(2)}, u32[]{:S(2)}) collective-permute-start(f32[32,8,128]{2,1,0:T(8,128)S(1)} %get-tuple-element.17), channel_id=1, source_target_pairs={{0,1},{1,0},{2,3},{3,2},{4,5},{5,4},{6,7},{7,6},{8,9},{9,8},{10,11... | collective-permute-start | bytes 393224 | tf_op jit(solution)/shard_map/ppermute | solution.py:401
  8.1 7.9 %collective-permute-start.1 = (f32[32,8,128]{2,1,0:T(8,128)S(1)}, f32[32,8,128]{2,1,0:T(8,128)S(1)}, u32[]{:S(2)}, u32[]{:S(2)}) collective-permute-start(f32[32,8,128]{2,1,0:T(8,128)S(1)} %get-tuple-element.18), channel_id=1, source_target_pairs={{1,2},{2,1},{3,4},{4,3},{5,6},{6,5},{9,10},{10,9},{11,12},{12,11},... | collective-permute-start | bytes 393224 | tf_op jit(solution)/shard_map/ppermute | solution.py:401
  8.8 9.2 %collective-permute-start.3 = (f32[32,4,128]{2,1,0:T(4,128)S(1)}, f32[32,4,128]{2,1,0:T(4,128)S(1)}, u32[]{:S(2)}, u32[]{:S(2)}) collective-permute-start(f32[32,4,128]{2,1,0:T(4,128)S(1)} %get-tuple-element.20), channel_id=1, source_target_pairs={{0,9},{1,8},{2,11},{3,10},{4,13},{5,12},{6,15},{7,14},{8,17},{9,16... | collective-permute-start | bytes 196616 | tf_op jit(solution)/shard_map/ppermute | solution.py:401
  15.3 2.6 %collective-permute-start.4 = (f32[32,4,128]{2,1,0:T(4,128)S(1)}, f32[32,4,128]{2,1,0:T(4,128)S(1)}, u32[]{:S(2)}, u32[]{:S(2)}) collective-permute-start(f32[32,4,128]{2,1,0:T(4,128)S(1)} %get-tuple-element.21), channel_id=1, source_target_pairs={{1,10},{2,9},{3,12},{4,11},{5,14},{6,13},{9,18},{10,17},{11,20},{1... | collective-permute-start | bytes 196616 | tf_op jit(solution)/shard_map/ppermute | solution.py:401
  55.6 3.0 %collective-permute-start.5 = (f32[64,40,128]{2,1,0:T(8,128)S(1)}, f32[64,40,128]{2,1,0:T(8,128)S(1)}, u32[]{:S(2)}, u32[]{:S(2)}) collective-permute-start(f32[64,40,128]{2,1,0:T(8,128)S(1)} %all_to_all.10.mine), channel_id=1, source_target_pairs={{0,8},{8,0},{1,9},{9,1},{2,10},{10,2},{3,11},{11,3},{4,12},{12,4},... | collective-permute-start | bytes 3932168 | tf_op jit(solution)/shard_map/ppermute | solution.py:432

commit v6 on v5

--- a/solution.py
+++ b/solution.py
@@ -30,6 +30,15 @@
 
 def tile(r, first=0):
     return slice(first + 8 * r, first + 8 * r + 8)
+
+
+def put_pair(ref, i, block, value):
+    ref[i, :, cols(block)] = value[0:4]
+    ref[i, :, cols(block + 1)] = pltpu.roll(value, 4, 0)[0:4]
+
+
+def get_pair(ref, i, block):
+    return jnp.concatenate([ref[i, :, cols(block)], ref[i, :, cols(block + 1)]], axis=0)
 
 
 def rates(a, b, d):
@@ -184,24 +193,30 @@
         rims[0, j] = border(sub, low, up, G1)
         rims[1, j] = border(sub, low, up, PART, 2, border(sub, low, up, G2))
         rims[2, j] = border(sub, low, up, G3)
-    which, at = lax.div(turn, 4), pl.ds(pl.multiple_of(8 * lax.rem(turn, 4), 8), 8)
-    chosen = Tiles(lambda j: jnp.where(which == 0, a[at, cols(j)], jnp.where(which == 1, b[at, cols(j)], d[at, cols(j)])))
+    at = pl.ds(pl.multiple_of(8 * lax.div(lax.rem(turn, 8), 2), 8), 8)
+    later, odd = turn >= 8, lax.rem(turn, 2) == 1
+
+    def choose(j):
+        value = jnp.where(later, b[at, cols(j)], a[at, cols(j)])
+        return jnp.where(odd, pltpu.roll(value, 4, 0), value)
+
+    chosen = Tiles(choose)
     for j in range(tiles):
         x, y, z = (chosen[i % tiles] for i in (j - 1, j, j + 1))
         packed[2 * j] = pltpu.roll(jnp.where(lane >= LANES - HALO, x, y), HALO, 1)
         packed[2 * j + 1] = pltpu.roll(jnp.where(lane < HALO, z, y), LANES - HALO, 1)
 
 
-def residual_kernel(flag, before, initial, start_one, start_two, guess, forcing, coef, rims, packed,
+def residual_kernel(flag, before, initial, start_one, start_two, guess, forcing, d, coef, rims, packed,
                     messages, ends, two, three, four, one, res, edge, begin):
     tiles = guess.shape[1] // LANES
     lane, sub = iota(1), iota(0)
-    first, even = flag[0] == 1, flag[4] == 0
+    first, even, at_end = flag[0] == 1, flag[4] == 0, flag[2] == 1
     for j in range(tiles):
         edge[0, j, 0:4, :] = jnp.where(even, start_one[j], start_two[j])
         edge[1, j, 0:4, :] = jnp.where(even, start_two[j], start_one[j])
         for i in (2 * j, 2 * j + 1):
-            messages[i, tile(4), :] = packed[i]
+            messages[i, :, cols(8)] = packed[i][0:4]
     for j in range(tiles):
         low, up = edge[0, j], edge[1, j]
         for r in range(4):
@@ -221,15 +236,15 @@
     def last(j, r, value, _):
         value = value + forcing[3, tile(r), cols(j)]
         ends[j, tile(r), :] = value
-        res[j, tile(r), :] = value - guess[tile(r), cols(j)]
+        res[j, tile(r), :] = jnp.where(at_end, d[tile(r), cols(j)], value - guess[tile(r), cols(j)])
 
     sweep(four, coef, range(4), last)
 
     for r in range(4):
         for j in range(tiles):
             x, y, z = (res[i % tiles, tile(r), :] for i in (j - 1, j, j + 1))
-            messages[2 * j, tile(r), :] = pltpu.roll(jnp.where(lane >= LANES - HALO, x, y), HALO, 1)
-            messages[2 * j + 1, tile(r), :] = pltpu.roll(jnp.where(lane < HALO, z, y), LANES - HALO, 1)
+            put_pair(messages, 2 * j, 2 * r, pltpu.roll(jnp.where(lane >= LANES - HALO, x, y), HALO, 1))
+            put_pair(messages, 2 * j + 1, 2 * r, pltpu.roll(jnp.where(lane < HALO, z, y), LANES - HALO, 1))
 
 
 def chain_kernel(flag, mine, other, messages, coef, one, two):
@@ -262,9 +277,10 @@
             low = [pltpu.roll(x, LANES - HALO, 1) for x in tiles[:3]]
             high = [pltpu.roll(x, HALO, 1) for x in (tiles[3], rim)]
             where = pair * spaces + s
-            messages[where, 0:8, :] = jnp.where(lane < 64, low[0], high[0])
-            messages[where, 8:16, :] = jnp.where(lane < 64, low[1], high[1])
-            messages[where, 16:24, :] = low[2]
+            put_pair(messages, where, 0, jnp.where(lane < 64, low[0], high[0]))
+            put_pair(messages, where, 2, jnp.where(lane < 64, low[1], high[1]))
+            shifted = pltpu.roll(pltpu.roll(tiles[2], 4, 0), HALO, 1)
+            messages[where, :, cols(4)] = jnp.where(lane < 64, low[2], shifted)[0:4]
 
     def half():
         for t in range(blocks):
@@ -274,7 +290,7 @@
         sources = (mine, other) if even else (other, mine)
 
         def arrived(pair, odd, t):
-            return sources[int(odd)][pair * spaces + t // 4, tile(t % 4), :]
+            return get_pair(sources[int(odd)], pair * spaces + t // 4, 2 * (t % 4))
 
         def rest(pair, odd):
             for t in range(blocks):
@@ -282,7 +298,10 @@
 
         for s in range(spaces):
             for r in range(4):
-                a, b, d = (sources[r % 2][(4 * i + r) // 2 * spaces + s, tile(4), :] for i in range(3))
+                a, b = (
+                    jnp.concatenate([x[(4 * i + r) * spaces + s, :, cols(8)] for x in sources], axis=0) for i in range(2)
+                )
+                d = arrived(pairs - 1, True, 4 * s + r)
                 own, up, low, left, right = rates(a, b, d)
                 at = tile(r, s * ROWS)
                 coef[0, at, :] = 2.0 * own - 1.0
@@ -292,7 +311,7 @@
             one[tile(t, 8), :] = arrived(0, False, t)
         if even:
             for s in range(spaces):
-                messages[s] = jnp.zeros((24, LANES), F32)
+                messages[s] = jnp.zeros((4, 5 * LANES), F32)
 
         def turn(pair, _):
             half()
@@ -320,11 +339,16 @@
     copies = [pltpu.make_async_copy(out.at[i], states.at[i], sems.at[i]) for i in range(4)]
     for j in range(tiles):
         for r in range(5):
-            x, y = returned[2 * j, tile(r % 3), :], returned[2 * j + 1, tile(r % 3), :]
-            if r < 3:
-                error = jnp.where(lane < 64, x, pltpu.roll(y, 64, 1))
+            if r == 2:
+                x, y = (jnp.concatenate([returned[i, :, cols(4)]] * 2, axis=0) for i in (2 * j, 2 * j + 1))
+                upper = jnp.where(lane < 64, x, pltpu.roll(y, 64, 1))
+                error = jnp.where(sub < 4, upper, jnp.where(lane < 64, pltpu.roll(x, 64, 1), y))
             else:
-                error = jnp.where(lane < 64, pltpu.roll(x, 64, 1), y)
+                x, y = (get_pair(returned, i, 2 * (r % 3)) for i in (2 * j, 2 * j + 1))
+                if r < 3:
+                    error = jnp.where(lane < 64, x, pltpu.roll(y, 64, 1))
+                else:
+                    error = jnp.where(lane < 64, pltpu.roll(x, 64, 1), y)
             put(err, j, r, error)
         after, behind = pltpu.roll(error, 7, 0), pltpu.roll(error, 1, 0)
         under = after - coef[1, j, tile(4), :] * behind
@@ -415,9 +439,9 @@
     )(flag, rim_one, rim_two, courant_rows, courant_cols, diffusion)
     messages, ends, *fields = pl.pallas_call(
         residual_kernel,
-        in_specs=[SMEM] + [VMEM] * 9,
+        in_specs=[SMEM] + [VMEM] * 10,
         out_specs=[VMEM] * 5,
-        out_shape=[shaped(2 * tiles, 40, LANES), shaped(tiles, ROWS, LANES), tall, tall, tall],
+        out_shape=[shaped(2 * tiles, 4, 9 * LANES), shaped(tiles, ROWS, LANES), tall, tall, tall],
         scratch_shapes=[
             field,
             pltpu.VMEM((tiles, ROWS, LANES), F32),
@@ -426,7 +450,7 @@
         ],
         compiler_params=params(20),
         name="residual",
-    )(flag, before, initial, start_one, start_two, last, forcing, coef, rims, packed)
+    )(flag, before, initial, start_one, start_two, last, forcing, diffusion, coef, rims, packed)
 
     mine = lax.all_to_all(messages, ("chip", "space"), 0, 0, tiled=True)
     other = lax.ppermute(mine, "core", [(0, 1), (1, 0)])
@@ -435,7 +459,7 @@
         chain_kernel,
         in_specs=[SMEM, VMEM, VMEM],
         out_specs=VMEM,
-        out_shape=shaped(chips * spaces, 24, LANES),
+        out_shape=shaped(chips * spaces, 4, 5 * LANES),
         scratch_shapes=[
             pltpu.VMEM((5, rows, LANES), F32),
             pltpu.VMEM((rows + 16, LANES), F32),

time: 86.4 us -> 83.6 us (0.968)
  blocking collectives: 56.4 us -> 53.6 us
    all_to_all x1, blocking collectives: 35.1 us -> 33.8 us  [on_device(): mine = lax.all_to_all(messages, ('chip', 'space'), 0, 0, tiled=True)]
    all_to_all x1, blocking collectives: 21.2 us -> 19.9 us  [on_device(): returned = lax.all_to_all(answer, ('chip', 'space'), 0, 0, tiled=True)]
where the time goes in v6:
time: 83.6 us; the launch traced here: 83.3 us
  blocking collectives  53.6 us (64%)
  Pallas kernels  14 us (17%)
  starting transfers between devices  11.7 us (14%)
  waiting for transfers between devices  3.76 us (4%)
    all_to_all x1, blocking collectives, on_device(): mine = lax.all_to_all(messages, ('chip', 'space'), 0, 0, tiled=True)  33.8 us
    all_to_all x1, blocking collectives, on_device(): returned = lax.all_to_all(answer, ('chip', 'space'), 0, 0, tiled=True)  19.9 us
    ppermute x4, starting transfers between devices, exchanged(): return lax.ppermute(value, everything, pairs)  10.4 us
    pallas_call x1, Pallas kernels, on_device(): pl.pallas_call(chain_kernel, in_specs=[SMEM, VMEM, VMEM], out_specs=VMEM,...  3.78 us
    pallas_call x1, Pallas kernels, on_device(): pl.pallas_call(rim_kernel, in_specs=[SMEM] + [VMEM] * 5 + [ANY], out_spec...  2.97 us
    ppermute x1, waiting for transfers between devices, on_device(): other = lax.ppermute(mine, 'core', [(0, 1), (1, 0)])  2.84 us
    pallas_call x1, Pallas kernels, on_device(): pl.pallas_call(final_kernel, in_specs=[VMEM] * 6, out_specs=ANY, out_shap...  2.57 us
    pallas_call x1, Pallas kernels, on_device(): pl.pallas_call(residual_kernel, in_specs=[SMEM] + [VMEM] * 10, out_specs=...  2.49 us
  transfers between devices with their start and end apart: 6, of which 2 were waited for; matrix products, arithmetic and copies ran while one was open for 0% of the time, Pallas kernels for 5%

profile of v6, /device:TPU:0, one launch (start us, length us, event | category | flops | bytes accessed | tf_op | source)
XLA Modules:
  0.0 83.3 jit_solution(8522858897236387156)
XLA Ops:
  0.0 0.0 copy-start.3
  0.0 0.0 copy-start.2
  0.0 1.1 %last.1.guess = f32[32,4096]{1,0:T(8,128)S(1)} custom-call(f32[4,32,4096]{2,1,0:T(8,128)} %guess.1), custom_call_target="tpu_custom_call" | custom-call | tf_op jit(solution)/shard_map/last/pallas_call | solution.py:396
  1.1 1.3 %collective-permute-start.2 = (f32[32,4096]{1,0:T(8,128)S(1)}, f32[32,4096]{1,0:T(8,128)S(1)}, u32[]{:S(2)}, u32[]{:S(2)}) collective-permute-start(f32[32,4096]{1,0:T(8,128)S(1)} %last.1.guess), channel_id=1, source_target_pairs={{0,8},{8,16},{16,24},{24,32},{32,40},{40,48},{48,56},{56,64},{64,7... | collective-permute-start | bytes 1572872 | tf_op jit(solution)/shard_map/ppermute | solution.py:405
  2.5 0.1 stack.31.flag
  2.6 0.0 copy-done.3
  2.6 0.0 copy-done.2
  2.6 0.0 copy-start.1
  2.6 0.0 copy-start.4
  2.6 0.0 copy-start
  2.6 3.0 %rim.1 = (f32[32,8,128]{2,1,0:T(8,128)S(1)}, f32[32,8,128]{2,1,0:T(8,128)S(1)}, f32[32,4,128]{2,1,0:T(4,128)S(1)}, f32[32,4,128]{2,1,0:T(4,128)S(1)}) custom-call(s32[5]{0:T(128)S(1)} %stack.31.flag, f32[32,4096]{1,0:T(8,128)S(1)} %last.1.guess, f32[32,4096]{1,0:T(8,128)S(1)} %copy-done.2, f32[32,4096]{1,0:T(8,128)S(1)} %copy-done.3, f32[32,4096]{1,0:T(8,128)} %b.3, ...), custom_call_target="tpu_custom_call" | custom-call | tf_op jit(solution)/shard_map/rim/pallas_call | solution.py:407
  5.6 2.5 %collective-permute-start = (f32[32,8,128]{2,1,0:T(8,128)S(1)}, f32[32,8,128]{2,1,0:T(8,128)S(1)}, u32[]{:S(2)}, u32[]{:S(2)}) collective-permute-start(f32[32,8,128]{2,1,0:T(8,128)S(1)} %get-tuple-element.17), channel_id=1, source_target_pairs={{0,1},{1,0},{2,3},{3,2},{4,5},{5,4},{6,7},{7,6},{8,9},{9,8},{10,11... | collective-permute-start | bytes 393224 | tf_op jit(solution)/shard_map/ppermute | solution.py:425
  8.1 0.7 collective-permute-start.1
  8.8 6.5 %collective-permute-start.3 = (f32[32,4,128]{2,1,0:T(4,128)S(1)}, f32[32,4,128]{2,1,0:T(4,128)S(1)}, u32[]{:S(2)}, u32[]{:S(2)}) collective-permute-start(f32[32,4,128]{2,1,0:T(4,128)S(1)} %get-tuple-element.20), channel_id=1, source_target_pairs={{0,9},{1,8},{2,11},{3,10},{4,13},{5,12},{6,15},{7,14},{8,17},{9,16... | collective-permute-start | bytes 196616 | tf_op jit(solution)/shard_map/ppermute | solution.py:425
  15.3 0.7 collective-permute-start.4
  16.0 0.0 collective-permute-done.rim_one
  16.0 0.0 collective-permute-done.1.rim_two
  16.0 0.0 copy-done.1
  16.0 0.0 copy-done.4
  16.0 1.0 %prepare.1 = (f32[5,32,40,128]{3,2,1,0:T(8,128)S(1)}, f32[3,32,8,128]{3,2,1,0:T(8,128)S(1)}, f32[64,8,128]{2,1,0:T(8,128)S(1)}) custom-call(s32[5]{0:T(128)S(1)} %stack.31.flag, f32[32,8,128]{2,1,0:T(8,128)S(1)} %collective-permute-done.rim_one, f32[32,8,128]{2,1,0:T(8,128)S(1)} %collective-permute-done.1.rim_two, f32[32,4096]{1,0:T(8,128)S(1)} %copy-done.3, ...), custom_call_target="tpu_custom_call" | custom-call | tf_op jit(solution)/shard_map/prepare/pallas_call | solution.py:432
  17.1 0.9 %collective-permute-done.3.start_one = f32[32,4,128]{2,1,0:T(4,128)S(1)} collective-permute-done((f32[32,4,128]{2,1,0:T(4,128)S(1)}, f32[32,4,128]{2,1,0:T(4,128)S(1)}, u32[]{:S(2)}, u32[]{:S(2)}) %collective-permute-start.3) | collective-permute-done | bytes 65568 | tf_op jit(solution)/shard_map/ppermute | solution.py:425
  18.0 0.0 collective-permute-done.4.start_two
  18.0 0.0 collective-permute-done.2.before
  18.0 0.0 copy-done
  18.0 2.5 %residual.1 = (f32[64,4,1152]{2,1,0:T(4,128)S(1)}, f32[32,32,128]{2,1,0:T(8,128)S(1)}, f32[32,48,128]{2,1,0:T(8,128)S(1)}, f32[32,48,128]{2,1,0:T(8,128)S(1)}, f32[32,48,128]{2,1,0:T(8,128)S(1)}) custom-call(s32[5]{0:T(128)S(1)} %stack.31.flag, f32[32,4096]{1,0:T(8,128)S(1)} %collective-permute-done.2.before, f32[32,4096]{1,0:T(8,128)S(1)} %copy-done.2, ...), custom_call_target="tpu_custom_call" | custom-call | tf_op jit(solution)/shard_map/residual/pallas_call | solution.py:440
  20.5 33.8 %all_to_all.10.mine = f32[64,4,1152]{2,1,0:T(4,128)S(1)} all-to-all(f32[64,4,1152]{2,1,0:T(4,128)S(1)} %get-tuple-element.28), channel_id=1, replica_groups=mesh['chip'=8,'core'=2,'space'=8] {'chip','space'}, dimensions={0} | all-to-all | bytes 2359296 | tf_op jit(solution)/shard_map/all_to_all | solution.py:455
  54.2 0.0 collective-permute-start.5
  54.2 2.8 %collective-permute-done.5.other = f32[64,4,1152]{2,1,0:T(4,128)S(1)} collective-permute-done((f32[64,4,1152]{2,1,0:T(4,128)S(1)}, f32[64,4,1152]{2,1,0:T(4,128)S(1)}, u32[]{:S(2)}, u32[]{:S(2)}) %collective-permute-start.5) | collective-permute-done | bytes 1179680 | tf_op jit(solution)/shard_map/ppermute | solution.py:456
  57.1 3.8 %chain.1 = f32[64,4,640]{2,1,0:T(4,128)S(1)} custom-call(s32[5]{0:T(128)S(1)} %stack.31.flag, f32[64,4,1152]{2,1,0:T(4,128)S(1)} %all_to_all.10.mine, f32[64,4,1152]{2,1,0:T(4,128)S(1)} %collective-permute-done.5.other), custom_call_target="tpu_custom_call" | custom-call | tf_op jit(solution)/shard_map/chain/pallas_call | solution.py:458
  60.9 19.9 %all_to_all.11.returned = f32[64,4,640]{2,1,0:T(4,128)S(1)} all-to-all(f32[64,4,640]{2,1,0:T(4,128)S(1)} %chain.1), channel_id=1, replica_groups=mesh['chip'=8,'core'=2,'space'=8] {'chip','space'}, dimensions={0} | all-to-all | bytes 1310720 | tf_op jit(solution)/shard_map/all_to_all | solution.py:471
  80.7 2.6 %final.1 = f32[4,32,4096]{2,1,0:T(8,128)} custom-call(f32[5,32,40,128]{3,2,1,0:T(8,128)S(1)} %get-tuple-element.19.coef, f32[32,48,128]{2,1,0:T(8,128)S(1)} %get-tuple-element.24.first, f32[32,48,128]{2,1,0:T(8,128)S(1)} %get-tuple-element.25.second, f32[32,48,128]{2,1,0:T(8,128)S(1)} %get-tuple-element.26.third, f32[32,32,128]{2,1,0:T(8,128)S(1)} %get-tuple-element.27.ends, ...), custom_call_target="tpu_custom_call" | custom-call | tf_op jit(solution)/shard_map/final/pallas_call | solution.py:472
Async XLA Ops:
  0.0 2.6 %copy-start.3 = (f32[32,4096]{1,0:T(8,128)S(1)}, f32[32,4096]{1,0:T(8,128)}, u32[]{:S(2)}) copy-start(f32[32,4096]{1,0:T(8,128)} %a.3) | copy-start | bytes 1572868
  0.0 2.6 %copy-start.2 = (f32[32,4096]{1,0:T(8,128)S(1)}, f32[32,4096]{1,0:T(8,128)}, u32[]{:S(2)}) copy-start(f32[32,4096]{1,0:T(8,128)} %initial.3) | copy-start | bytes 1572868
  1.1 16.8 %collective-permute-start.2 = (f32[32,4096]{1,0:T(8,128)S(1)}, f32[32,4096]{1,0:T(8,128)S(1)}, u32[]{:S(2)}, u32[]{:S(2)}) collective-permute-start(f32[32,4096]{1,0:T(8,128)S(1)} %last.1.guess), channel_id=1, source_target_pairs={{0,8},{8,16},{16,24},{24,32},{32,40},{40,48},{48,56},{56,64},{64,7... | collective-permute-start | bytes 1572872 | tf_op jit(solution)/shard_map/ppermute | solution.py:405
  2.6 13.4 %copy-start.1 = (f32[32,4096]{1,0:T(8,128)S(1)}, f32[32,4096]{1,0:T(8,128)}, u32[]{:S(2)}) copy-start(f32[32,4096]{1,0:T(8,128)} %d.5) | copy-start | bytes 1572868
  2.6 13.4 %copy-start.4 = (f32[32,4096]{1,0:T(8,128)S(1)}, f32[32,4096]{1,0:T(8,128)}, u32[]{:S(2)}) copy-start(f32[32,4096]{1,0:T(8,128)} %b.3) | copy-start | bytes 1572868
  2.6 15.4 %copy-start = (f32[4,32,4096]{2,1,0:T(8,128)S(1)}, f32[4,32,4096]{2,1,0:T(8,128)}, u32[]{:S(2)}) copy-start(f32[4,32,4096]{2,1,0:T(8,128)} %forcing.3) | copy-start | bytes 6291460
  5.6 10.4 %collective-permute-start = (f32[32,8,128]{2,1,0:T(8,128)S(1)}, f32[32,8,128]{2,1,0:T(8,128)S(1)}, u32[]{:S(2)}, u32[]{:S(2)}) collective-permute-start(f32[32,8,128]{2,1,0:T(8,128)S(1)} %get-tuple-element.17), channel_id=1, source_target_pairs={{0,1},{1,0},{2,3},{3,2},{4,5},{5,4},{6,7},{7,6},{8,9},{9,8},{10,11... | collective-permute-start | bytes 393224 | tf_op jit(solution)/shard_map/ppermute | solution.py:425
  8.1 7.9 %collective-permute-start.1 = (f32[32,8,128]{2,1,0:T(8,128)S(1)}, f32[32,8,128]{2,1,0:T(8,128)S(1)}, u32[]{:S(2)}, u32[]{:S(2)}) collective-permute-start(f32[32,8,128]{2,1,0:T(8,128)S(1)} %get-tuple-element.18), channel_id=1, source_target_pairs={{1,2},{2,1},{3,4},{4,3},{5,6},{6,5},{9,10},{10,9},{11,12},{12,11},... | collective-permute-start | bytes 393224 | tf_op jit(solution)/shard_map/ppermute | solution.py:425
  8.8 9.2 %collective-permute-start.3 = (f32[32,4,128]{2,1,0:T(4,128)S(1)}, f32[32,4,128]{2,1,0:T(4,128)S(1)}, u32[]{:S(2)}, u32[]{:S(2)}) collective-permute-start(f32[32,4,128]{2,1,0:T(4,128)S(1)} %get-tuple-element.20), channel_id=1, source_target_pairs={{0,9},{1,8},{2,11},{3,10},{4,13},{5,12},{6,15},{7,14},{8,17},{9,16... | collective-permute-start | bytes 196616 | tf_op jit(solution)/shard_map/ppermute | solution.py:425
  15.3 2.6 %collective-permute-start.4 = (f32[32,4,128]{2,1,0:T(4,128)S(1)}, f32[32,4,128]{2,1,0:T(4,128)S(1)}, u32[]{:S(2)}, u32[]{:S(2)}) collective-permute-start(f32[32,4,128]{2,1,0:T(4,128)S(1)} %get-tuple-element.21), channel_id=1, source_target_pairs={{1,10},{2,9},{3,12},{4,11},{5,14},{6,13},{9,18},{10,17},{11,20},{1... | collective-permute-start | bytes 196616 | tf_op jit(solution)/shard_map/ppermute | solution.py:425
  54.2 2.8 %collective-permute-start.5 = (f32[64,4,1152]{2,1,0:T(4,128)S(1)}, f32[64,4,1152]{2,1,0:T(4,128)S(1)}, u32[]{:S(2)}, u32[]{:S(2)}) collective-permute-start(f32[64,4,1152]{2,1,0:T(4,128)S(1)} %all_to_all.10.mine), channel_id=1, source_target_pairs={{0,8},{8,0},{1,9},{9,1},{2,10},{10,2},{3,11},{11,3},{4,12},{12,4},... | collective-permute-start | bytes 3538952 | tf_op jit(solution)/shard_map/ppermute | solution.py:456

commit v7 on v6

--- a/solution.py
+++ b/solution.py
@@ -12,7 +12,7 @@
 SMEM = pl.BlockSpec(memory_space=pltpu.SMEM)
 F32 = jnp.float32
 ANY = pl.BlockSpec(memory_space=pl.ANY)
-G1, G2, G3, PART, A1, B1, D1, INWARD = range(8)
+G1, PART, G2, INWARD, G3, A1, B1, D1 = range(8)
 START1, START2, STEP1, STEP2 = range(4)
 
 
@@ -122,9 +122,24 @@
     def inward(x):
         return jnp.where(top, pltpu.roll(x, 1, 0), pltpu.roll(x, 7, 0))
 
-    def row(x, side, place, to):
-        at = place - 1 if side == 0 else 8 - place
-        return pltpu.roll(x, (to - at) % 8, 0)
+    second_row = (sub == 1) | (sub == 6)
+
+    def collect(pieces, side):
+        total = None
+        for value, by in pieces:
+            if by:
+                value = pltpu.roll(value, by if side == 0 else 8 - by, 0)
+            here = sub >= by if side == 0 else sub <= 7 - by
+            total = value if total is None else jnp.where(here, value, total)
+        return total
+
+    def start_rows(pieces, side):
+        (values, _), (first, by), (second, far) = pieces
+        ways = [by, far] if side == 0 else [8 - by, 8 - far]
+        first, second = (pltpu.roll(x, way, 0) for x, way in zip((first, second), ways, strict=True))
+        places = (STEP1, STEP2) if side == 0 else (7 - STEP1, 7 - STEP2)
+        total = jnp.where(sub == places[0], first, jnp.where(sub == places[1], second, values))
+        return total if side == 0 else pltpu.roll(total, 4, 0)
 
     OWN, OUT, IN, LEFT, RIGHT = range(5)
 
@@ -149,19 +164,14 @@
     forced, stepped = Tiles(lambda j: both(vg.at[0], j)), Tiles(lambda j: after[j])
     for j in range(tiles):
         g1, g2, g3 = forced[j], both(vg.at[1], j), both(vg.at[2], j)
-        items = [(G1, g1, 1), (G2, g2 + coef[OUT, j] * outward(g1), 1), (G3, g3, 1), (PART, open_step(forced, j) + g2, 2)]
-        items += [(A1 + i, both(x, j), 1) for i, x in enumerate((a, b, d))]
-        items += [(INWARD, coef[IN, j], 2)]
-        values, second = field[j], open_step(stepped, j)
-        begins = [(START1, values, 1), (START2, values, 2), (STEP1, part[j], 2), (STEP2, second, 2)]
-        rims, starts = [], []
-        for side in range(2):
-            for found, made in ((items, rims), (begins, starts)):
-                total = None
-                for to, value, place in found:
-                    value = row(value, side, place, to)
-                    total = value if total is None else jnp.where(sub == to, value, total)
-                made.append(total)
+        second = open_step(stepped, j)
+        forced_rows = jnp.where(second_row, open_step(forced, j) + g2, g1)
+        mixed_rows = jnp.where(second_row, coef[IN, j], g2 + coef[OUT, j] * outward(g1))
+        pieces = [(forced_rows, G1), (mixed_rows, G2), (g3, G3)]
+        pieces += [(both(x, j), to) for x, to in ((a, A1), (b, B1), (d, D1))]
+        begins = [(field[j], START1), (part[j], STEP1 - 1), (second, STEP2 - 1)]
+        rims = [collect(pieces, side) for side in range(2)]
+        starts = [start_rows(begins, side) for side in range(2)]
         rim_one[j] = jnp.where(even, rims[1], rims[0])
         rim_two[j] = jnp.where(even, rims[0], rims[1])
         start_one[j] = jnp.where(even, starts[1], starts[0])[0:4]
@@ -170,7 +180,7 @@
 
 def border(sub, under, over, item, place=1, rest=0.0):
     under = pltpu.roll(under, (place - 1 - item) % 8, 0)
-    over = pltpu.roll(over, (8 - place - item) % 8, 0)
+    over = pltpu.roll(over, (1 - place + item) % 8, 0)
     return jnp.where(sub == place - 1, under, jnp.where(sub == 8 - place, over, rest))
 
 
@@ -187,7 +197,7 @@
         own, upper, lower, left, right = rates(*(border(sub, low, up, item) for item in (A1, B1, D1)))
         own = jnp.where((sub == 0) | (sub == 7), own, 0.0)
         upper = jnp.where(sub == 1, pltpu.roll(low, (1 - INWARD) % 8, 0), upper)
-        lower = jnp.where(sub == 6, pltpu.roll(up, (6 - INWARD) % 8, 0), lower)
+        lower = jnp.where(sub == 6, pltpu.roll(up, (INWARD - 1) % 8, 0), lower)
         for i, value in enumerate((own, upper, lower, left, right)):
             coef[i, j, tile(4), :] = value
         rims[0, j] = border(sub, low, up, G1)
@@ -214,7 +224,7 @@
     first, even, at_end = flag[0] == 1, flag[4] == 0, flag[2] == 1
     for j in range(tiles):
         edge[0, j, 0:4, :] = jnp.where(even, start_one[j], start_two[j])
-        edge[1, j, 0:4, :] = jnp.where(even, start_two[j], start_one[j])
+        edge[1, j, 4:8, :] = jnp.where(even, start_two[j], start_one[j])
         for i in (2 * j, 2 * j + 1):
             messages[i, :, cols(8)] = packed[i][0:4]
     for j in range(tiles):
@@ -313,7 +323,7 @@
             for s in range(spaces):
                 messages[s] = jnp.zeros((4, 5 * LANES), F32)
 
-        def turn(pair, _):
+        def turn(pair):
             half()
             if not even:
                 emit(pair)
@@ -322,9 +332,9 @@
             if even:
                 emit(pair + 1)
             rest(pair + 1, False)
-            return 0
-
-        lax.fori_loop(0, pairs - 1, turn, 0)
+
+        for pair in range(pairs - 1):
+            turn(pair)
         if not even:
             half()
             emit(pairs - 1)

time: 83.6 us -> 83 us (level)
  no operation moved by 1% of the time
where the time goes in v7:
time: 83 us; the launch traced here: 82.7 us
  blocking collectives  53.5 us (64%)
  Pallas kernels  13.5 us (16%)
  starting transfers between devices  11.7 us (14%)
  waiting for transfers between devices  3.76 us (5%)
    all_to_all x1, blocking collectives, on_device(): mine = lax.all_to_all(messages, ('chip', 'space'), 0, 0, tiled=True)  33.8 us
    all_to_all x1, blocking collectives, on_device(): returned = lax.all_to_all(answer, ('chip', 'space'), 0, 0, tiled=True)  19.7 us
    ppermute x4, starting transfers between devices, exchanged(): return lax.ppermute(value, everything, pairs)  10.4 us
    pallas_call x1, Pallas kernels, on_device(): pl.pallas_call(chain_kernel, in_specs=[SMEM, VMEM, VMEM], out_specs=VMEM,...  3.38 us
    pallas_call x1, Pallas kernels, on_device(): pl.pallas_call(rim_kernel, in_specs=[SMEM] + [VMEM] * 5 + [ANY], out_spec...  2.95 us
    ppermute x1, waiting for transfers between devices, on_device(): other = lax.ppermute(mine, 'core', [(0, 1), (1, 0)])  2.84 us
    pallas_call x1, Pallas kernels, on_device(): pl.pallas_call(final_kernel, in_specs=[VMEM] * 6, out_specs=ANY, out_shap...  2.57 us
    pallas_call x1, Pallas kernels, on_device(): pl.pallas_call(residual_kernel, in_specs=[SMEM] + [VMEM] * 10, out_specs=...  2.46 us
  transfers between devices with their start and end apart: 6, of which 2 were waited for; matrix products, arithmetic and copies ran while one was open for 0% of the time, Pallas kernels for 5%

profile of v7, /device:TPU:0, one launch (start us, length us, event | category | flops | bytes accessed | tf_op | source)
XLA Modules:
  0.0 82.7 jit_solution(11403033881103709832)
XLA Ops:
  0.0 0.0 copy-start.3
  0.0 0.0 copy-start.2
  0.0 1.1 %last.1.guess = f32[32,4096]{1,0:T(8,128)S(1)} custom-call(f32[4,32,4096]{2,1,0:T(8,128)} %guess.1), custom_call_target="tpu_custom_call" | custom-call | tf_op jit(solution)/shard_map/last/pallas_call | solution.py:406
  1.1 1.3 %collective-permute-start.2 = (f32[32,4096]{1,0:T(8,128)S(1)}, f32[32,4096]{1,0:T(8,128)S(1)}, u32[]{:S(2)}, u32[]{:S(2)}) collective-permute-start(f32[32,4096]{1,0:T(8,128)S(1)} %last.1.guess), channel_id=1, source_target_pairs={{0,8},{8,16},{16,24},{24,32},{32,40},{40,48},{48,56},{56,64},{64,7... | collective-permute-start | bytes 1572872 | tf_op jit(solution)/shard_map/ppermute | solution.py:415
  2.5 0.1 stack.31.flag
  2.6 0.0 copy-done.3
  2.6 0.0 copy-done.2
  2.6 0.0 copy-start.1
  2.6 0.0 copy-start.4
  2.6 0.0 copy-start
  2.6 3.0 %rim.1 = (f32[32,8,128]{2,1,0:T(8,128)S(1)}, f32[32,8,128]{2,1,0:T(8,128)S(1)}, f32[32,4,128]{2,1,0:T(4,128)S(1)}, f32[32,4,128]{2,1,0:T(4,128)S(1)}) custom-call(s32[5]{0:T(128)S(1)} %stack.31.flag, f32[32,4096]{1,0:T(8,128)S(1)} %last.1.guess, f32[32,4096]{1,0:T(8,128)S(1)} %copy-done.2, f32[32,4096]{1,0:T(8,128)S(1)} %copy-done.3, f32[32,4096]{1,0:T(8,128)} %b.3, ...), custom_call_target="tpu_custom_call" | custom-call | tf_op jit(solution)/shard_map/rim/pallas_call | solution.py:417
  5.6 2.5 %collective-permute-start = (f32[32,8,128]{2,1,0:T(8,128)S(1)}, f32[32,8,128]{2,1,0:T(8,128)S(1)}, u32[]{:S(2)}, u32[]{:S(2)}) collective-permute-start(f32[32,8,128]{2,1,0:T(8,128)S(1)} %get-tuple-element.17), channel_id=1, source_target_pairs={{0,1},{1,0},{2,3},{3,2},{4,5},{5,4},{6,7},{7,6},{8,9},{9,8},{10,11... | collective-permute-start | bytes 393224 | tf_op jit(solution)/shard_map/ppermute | solution.py:435
  8.1 0.7 collective-permute-start.1
  8.8 6.5 %collective-permute-start.3 = (f32[32,4,128]{2,1,0:T(4,128)S(1)}, f32[32,4,128]{2,1,0:T(4,128)S(1)}, u32[]{:S(2)}, u32[]{:S(2)}) collective-permute-start(f32[32,4,128]{2,1,0:T(4,128)S(1)} %get-tuple-element.20), channel_id=1, source_target_pairs={{0,9},{1,8},{2,11},{3,10},{4,13},{5,12},{6,15},{7,14},{8,17},{9,16... | collective-permute-start | bytes 196616 | tf_op jit(solution)/shard_map/ppermute | solution.py:435
  15.3 0.7 collective-permute-start.4
  16.0 0.0 collective-permute-done.rim_one
  16.0 0.0 collective-permute-done.1.rim_two
  16.0 0.0 copy-done.1
  16.0 0.0 copy-done.4
  16.0 1.0 %prepare.1 = (f32[5,32,40,128]{3,2,1,0:T(8,128)S(1)}, f32[3,32,8,128]{3,2,1,0:T(8,128)S(1)}, f32[64,8,128]{2,1,0:T(8,128)S(1)}) custom-call(s32[5]{0:T(128)S(1)} %stack.31.flag, f32[32,8,128]{2,1,0:T(8,128)S(1)} %collective-permute-done.rim_one, f32[32,8,128]{2,1,0:T(8,128)S(1)} %collective-permute-done.1.rim_two, f32[32,4096]{1,0:T(8,128)S(1)} %copy-done.3, ...), custom_call_target="tpu_custom_call" | custom-call | tf_op jit(solution)/shard_map/prepare/pallas_call | solution.py:442
  17.1 0.9 %collective-permute-done.3.start_one = f32[32,4,128]{2,1,0:T(4,128)S(1)} collective-permute-done((f32[32,4,128]{2,1,0:T(4,128)S(1)}, f32[32,4,128]{2,1,0:T(4,128)S(1)}, u32[]{:S(2)}, u32[]{:S(2)}) %collective-permute-start.3) | collective-permute-done | bytes 65568 | tf_op jit(solution)/shard_map/ppermute | solution.py:435
  18.0 0.0 collective-permute-done.4.start_two
  18.0 0.0 collective-permute-done.2.before
  18.0 0.0 copy-done
  18.0 2.5 %residual.1 = (f32[64,4,1152]{2,1,0:T(4,128)S(1)}, f32[32,32,128]{2,1,0:T(8,128)S(1)}, f32[32,48,128]{2,1,0:T(8,128)S(1)}, f32[32,48,128]{2,1,0:T(8,128)S(1)}, f32[32,48,128]{2,1,0:T(8,128)S(1)}) custom-call(s32[5]{0:T(128)S(1)} %stack.31.flag, f32[32,4096]{1,0:T(8,128)S(1)} %collective-permute-done.2.before, f32[32,4096]{1,0:T(8,128)S(1)} %copy-done.2, ...), custom_call_target="tpu_custom_call" | custom-call | tf_op jit(solution)/shard_map/residual/pallas_call | solution.py:450
  20.4 33.8 %all_to_all.10.mine = f32[64,4,1152]{2,1,0:T(4,128)S(1)} all-to-all(f32[64,4,1152]{2,1,0:T(4,128)S(1)} %get-tuple-element.28), channel_id=1, replica_groups=mesh['chip'=8,'core'=2,'space'=8] {'chip','space'}, dimensions={0} | all-to-all | bytes 2359296 | tf_op jit(solution)/shard_map/all_to_all | solution.py:465
  54.2 0.0 collective-permute-start.5
  54.2 2.8 %collective-permute-done.5.other = f32[64,4,1152]{2,1,0:T(4,128)S(1)} collective-permute-done((f32[64,4,1152]{2,1,0:T(4,128)S(1)}, f32[64,4,1152]{2,1,0:T(4,128)S(1)}, u32[]{:S(2)}, u32[]{:S(2)}) %collective-permute-start.5) | collective-permute-done | bytes 1179680 | tf_op jit(solution)/shard_map/ppermute | solution.py:466
  57.1 3.4 %chain.1 = f32[64,4,640]{2,1,0:T(4,128)S(1)} custom-call(s32[5]{0:T(128)S(1)} %stack.31.flag, f32[64,4,1152]{2,1,0:T(4,128)S(1)} %all_to_all.10.mine, f32[64,4,1152]{2,1,0:T(4,128)S(1)} %collective-permute-done.5.other), custom_call_target="tpu_custom_call" | custom-call | tf_op jit(solution)/shard_map/chain/pallas_call | solution.py:468
  60.5 19.7 %all_to_all.11.returned = f32[64,4,640]{2,1,0:T(4,128)S(1)} all-to-all(f32[64,4,640]{2,1,0:T(4,128)S(1)} %chain.1), channel_id=1, replica_groups=mesh['chip'=8,'core'=2,'space'=8] {'chip','space'}, dimensions={0} | all-to-all | bytes 1310720 | tf_op jit(solution)/shard_map/all_to_all | solution.py:481
  80.2 2.6 %final.1 = f32[4,32,4096]{2,1,0:T(8,128)} custom-call(f32[5,32,40,128]{3,2,1,0:T(8,128)S(1)} %get-tuple-element.19.coef, f32[32,48,128]{2,1,0:T(8,128)S(1)} %get-tuple-element.24.first, f32[32,48,128]{2,1,0:T(8,128)S(1)} %get-tuple-element.25.second, f32[32,48,128]{2,1,0:T(8,128)S(1)} %get-tuple-element.26.third, f32[32,32,128]{2,1,0:T(8,128)S(1)} %get-tuple-element.27.ends, ...), custom_call_target="tpu_custom_call" | custom-call | tf_op jit(solution)/shard_map/final/pallas_call | solution.py:482
Async XLA Ops:
  0.0 2.6 %copy-start.3 = (f32[32,4096]{1,0:T(8,128)S(1)}, f32[32,4096]{1,0:T(8,128)}, u32[]{:S(2)}) copy-start(f32[32,4096]{1,0:T(8,128)} %a.3) | copy-start | bytes 1572868
  0.0 2.6 %copy-start.2 = (f32[32,4096]{1,0:T(8,128)S(1)}, f32[32,4096]{1,0:T(8,128)}, u32[]{:S(2)}) copy-start(f32[32,4096]{1,0:T(8,128)} %initial.3) | copy-start | bytes 1572868
  1.1 16.8 %collective-permute-start.2 = (f32[32,4096]{1,0:T(8,128)S(1)}, f32[32,4096]{1,0:T(8,128)S(1)}, u32[]{:S(2)}, u32[]{:S(2)}) collective-permute-start(f32[32,4096]{1,0:T(8,128)S(1)} %last.1.guess), channel_id=1, source_target_pairs={{0,8},{8,16},{16,24},{24,32},{32,40},{40,48},{48,56},{56,64},{64,7... | collective-permute-start | bytes 1572872 | tf_op jit(solution)/shard_map/ppermute | solution.py:415
  2.6 13.4 %copy-start.1 = (f32[32,4096]{1,0:T(8,128)S(1)}, f32[32,4096]{1,0:T(8,128)}, u32[]{:S(2)}) copy-start(f32[32,4096]{1,0:T(8,128)} %d.5) | copy-start | bytes 1572868
  2.6 13.4 %copy-start.4 = (f32[32,4096]{1,0:T(8,128)S(1)}, f32[32,4096]{1,0:T(8,128)}, u32[]{:S(2)}) copy-start(f32[32,4096]{1,0:T(8,128)} %b.3) | copy-start | bytes 1572868
  2.6 15.4 %copy-start = (f32[4,32,4096]{2,1,0:T(8,128)S(1)}, f32[4,32,4096]{2,1,0:T(8,128)}, u32[]{:S(2)}) copy-start(f32[4,32,4096]{2,1,0:T(8,128)} %forcing.3) | copy-start | bytes 6291460
  5.6 10.4 %collective-permute-start = (f32[32,8,128]{2,1,0:T(8,128)S(1)}, f32[32,8,128]{2,1,0:T(8,128)S(1)}, u32[]{:S(2)}, u32[]{:S(2)}) collective-permute-start(f32[32,8,128]{2,1,0:T(8,128)S(1)} %get-tuple-element.17), channel_id=1, source_target_pairs={{0,1},{1,0},{2,3},{3,2},{4,5},{5,4},{6,7},{7,6},{8,9},{9,8},{10,11... | collective-permute-start | bytes 393224 | tf_op jit(solution)/shard_map/ppermute | solution.py:435
  8.1 7.9 %collective-permute-start.1 = (f32[32,8,128]{2,1,0:T(8,128)S(1)}, f32[32,8,128]{2,1,0:T(8,128)S(1)}, u32[]{:S(2)}, u32[]{:S(2)}) collective-permute-start(f32[32,8,128]{2,1,0:T(8,128)S(1)} %get-tuple-element.18), channel_id=1, source_target_pairs={{1,2},{2,1},{3,4},{4,3},{5,6},{6,5},{9,10},{10,9},{11,12},{12,11},... | collective-permute-start | bytes 393224 | tf_op jit(solution)/shard_map/ppermute | solution.py:435
  8.8 9.2 %collective-permute-start.3 = (f32[32,4,128]{2,1,0:T(4,128)S(1)}, f32[32,4,128]{2,1,0:T(4,128)S(1)}, u32[]{:S(2)}, u32[]{:S(2)}) collective-permute-start(f32[32,4,128]{2,1,0:T(4,128)S(1)} %get-tuple-element.20), channel_id=1, source_target_pairs={{0,9},{1,8},{2,11},{3,10},{4,13},{5,12},{6,15},{7,14},{8,17},{9,16... | collective-permute-start | bytes 196616 | tf_op jit(solution)/shard_map/ppermute | solution.py:435
  15.3 2.6 %collective-permute-start.4 = (f32[32,4,128]{2,1,0:T(4,128)S(1)}, f32[32,4,128]{2,1,0:T(4,128)S(1)}, u32[]{:S(2)}, u32[]{:S(2)}) collective-permute-start(f32[32,4,128]{2,1,0:T(4,128)S(1)} %get-tuple-element.21), channel_id=1, source_target_pairs={{1,10},{2,9},{3,12},{4,11},{5,14},{6,13},{9,18},{10,17},{11,20},{1... | collective-permute-start | bytes 196616 | tf_op jit(solution)/shard_map/ppermute | solution.py:435
  54.2 2.8 %collective-permute-start.5 = (f32[64,4,1152]{2,1,0:T(4,128)S(1)}, f32[64,4,1152]{2,1,0:T(4,128)S(1)}, u32[]{:S(2)}, u32[]{:S(2)}) collective-permute-start(f32[64,4,1152]{2,1,0:T(4,128)S(1)} %all_to_all.10.mine), channel_id=1, source_target_pairs={{0,8},{8,0},{1,9},{9,1},{2,10},{10,2},{3,11},{11,3},{4,12},{12,4},... | collective-permute-start | bytes 3538952 | tf_op jit(solution)/shard_map/ppermute | solution.py:466
